TPU v7x, 32 devices: a whole 2x2x4 slice. The times are simulated.
32 devices in a mesh: dp: 8 (over z, core), seq: 4 (over y, x).
Axes of the slice: x: 2, y: 2, z: 4, core: 2. Of those that a mesh axis runs over, the one named last changes fastest.
Arguments:
- segment: bfloat16 [24, 768, 1024], P('dp', 'seq'), may hold values from -6 to 6
- memory: bfloat16 [24, 768, 1024], P('dp', 'seq'), may hold values from -6 to 6
- compressed: bfloat16 [24, 256, 1024], P('dp', 'seq'), may hold values from -6 to 6
- eob: int32 [24, 768], P('dp'), may hold values from 0 to 1, as said below
- reset: int32 [24], P('dp'), may hold values 0 or 1
- ln1_gain: bfloat16 [1024], P('seq'), may hold values from 0.5 to 1.5
- ln1_bias: bfloat16 [1024], P('seq'), may hold values from -1 to 1
- w_query: bfloat16 [1024, 1024], P('seq'), may hold values from -0.1875 to 0.1875
- w_key: bfloat16 [1024, 1024], P('seq'), may hold values from -0.1875 to 0.1875
- w_value: bfloat16 [1024, 1024], P('seq'), may hold values from -0.1875 to 0.1875
- w_out: bfloat16 [1024, 1024], P('seq'), may hold values from -1 to 1
- out_bias: bfloat16 [1024], P('seq'), may hold values from -1.5 to 1.5
- w_rel: bfloat16 [1024, 1024], P('seq'), may hold values from -0.1875 to 0.1875
- bias_content: bfloat16 [1024], P('seq'), may hold values from -2.5 to 2.5
- bias_position: bfloat16 [1024], P('seq'), may hold values from -2.5 to 2.5
- ln2_gain: bfloat16 [1024], P('seq'), may hold values from 0.5 to 1.5
- ln2_bias: bfloat16 [1024], P('seq'), may hold values from -1 to 1
- w_up: bfloat16 [1024, 4096], P('seq'), may hold values from -0.1875 to 0.1875
- up_bias: bfloat16 [4096], P('seq'), may hold values from -2.5 to 2.5
- w_down: bfloat16 [4096, 1024], P('seq'), may hold values from -0.1875 to 0.1875
- down_bias: bfloat16 [1024], P('seq'), may hold values from -1.5 to 1.5
- conv_weight: bfloat16 [3, 1024, 1024], P(None, 'seq'), may hold values from -0.109375 to 0.109375
- conv_bias: bfloat16 [1024], P('seq'), may hold values from -1.5 to 1.5
- cotangent: bfloat16 [24, 768, 1024], P('dp', 'seq'), may hold values from -6 to 6
Outputs:
- mixed: bfloat16 [24, 768, 1024], P('dp', 'seq')
- segment_grad: float32 [24, 768, 1024], P('dp', 'seq')
- ln1_gain_grad: float32 [1024], P('seq')
- ln1_bias_grad: float32 [1024], P('seq')
- w_query_grad: float32 [1024, 1024], P('seq')
- w_key_grad: float32 [1024, 1024], P('seq')
- w_value_grad: float32 [1024, 1024], P('seq')
- w_out_grad: float32 [1024, 1024], P('seq')
- out_bias_grad: float32 [1024], P('seq')
- w_rel_grad: float32 [1024, 1024], P('seq')
- bias_content_grad: float32 [1024], P('seq')
- bias_position_grad: float32 [1024], P('seq')
- ln2_gain_grad: float32 [1024], P('seq')
- ln2_bias_grad: float32 [1024], P('seq')
- w_up_grad: float32 [1024, 4096], P('seq')
- up_bias_grad: float32 [4096], P('seq')
- w_down_grad: float32 [4096, 1024], P('seq')
- down_bias_grad: float32 [1024], P('seq')
- new_compressed: bfloat16 [24, 256, 1024], P('dp', 'seq')
Inputs may be any that keep to these rules, and one draw needn't show every extreme that they name: `eob`: in each aligned block of 3 streams at least one stream has no 1.
All inputs are finite; a program needn't handle non-finite values. No bound on the sum of `reset` on one device may be relied on, other than what follows from the above.
Results may differ from a plain program's by a relative error of at most 0.02.
Values may be sent and summed in bfloat16 or wider, within the bound.
No kernel may reach another device: no remote copies, remote signals or barrier semaphores. Data moves between devices by JAX's collectives and lax.ppermute only.
A program may use at most 384 MiB of HBM per device.

v0:
```python
import functools
import math

import jax
import jax.numpy as jnp
from jax import lax
from jax.experimental import pallas as pl
from jax.experimental.pallas import tpu as pltpu
from jax.sharding import PartitionSpec as P

HEADS = 8
DH = 128
EPSILON = 1e-05
MASKED = -1e30
LANES = 128
BLOCK = 256
CHUNK = 16
VMEM_LIMIT = 60 * 2**20
SCALE = 1.0 / math.sqrt(DH)
LOG2E = 1.4426950408889634
BF16 = jnp.bfloat16
F32 = jnp.float32


def cost(microseconds):
    return pl.CostEstimate(flops=int(microseconds * 1.15e7), bytes_accessed=0, transcendentals=0)


def mm(left, right, dims):
    return lax.dot_general(left, right, (dims, ((), ())), preferred_element_type=F32)


NN = ((1,), (0,))
NT = ((1,), (1,))
TN = ((0,), (0,))


def lean_left(block, first_row, fill_columns):
    columns = block.shape[1] // LANES
    far = BLOCK - 1 - first_row
    whole, part = far // LANES, far % LANES
    turned = [
        pltpu.roll(
            block[:, LANES * t : LANES * (t + 1)], LANES - part, 1, stride=1, stride_axis=0
        )
        for t in range(columns)
    ]
    rows = lax.broadcasted_iota(jnp.int32, (block.shape[0], LANES), 0)
    lanes = lax.broadcasted_iota(jnp.int32, (block.shape[0], LANES), 1)
    near = lanes - rows < LANES - part
    out = []
    for t in range(fill_columns):
        a = turned[(t + whole) % columns]
        b = turned[(t + whole + 1) % columns]
        out.append(jnp.where(near, a, b))
    return jnp.concatenate(out, axis=1)


def lean_right(block, first_row):
    columns = block.shape[1] // LANES
    whole, part = first_row // LANES, first_row % LANES
    turned = [
        pltpu.roll(block[:, LANES * t : LANES * (t + 1)], part, 1, stride=1, stride_axis=0)
        for t in range(columns)
    ]
    rows = lax.broadcasted_iota(jnp.int32, (block.shape[0], LANES), 0)
    lanes = lax.broadcasted_iota(jnp.int32, (block.shape[0], LANES), 1)
    wrapped = lanes - rows < part
    out = []
    for t in range(columns):
        a = turned[(t - whole) % columns]
        b = turned[(t - whole - 1) % columns]
        out.append(jnp.where(wrapped, b, a))
    return jnp.concatenate(out, axis=1)


def flip_matrix(kind):
    rows = lax.broadcasted_iota(jnp.int32, (BLOCK, BLOCK), 0)
    lanes = lax.broadcasted_iota(jnp.int32, (BLOCK, BLOCK), 1)
    return (rows + lanes == BLOCK - 1).astype(F32).astype(kind)


def in_place_order(parts_ref, out_ref, cuts):
    parts = parts_ref.shape[0]
    low, base = 0, 0
    for size in cuts:
        for part in range(parts):
            out_ref[base + part * size : base + (part + 1) * size, :] = parts_ref[
                part, low : low + size, :
            ]
        low += size
        base += parts * size


def attend_kernel(
    cuts, q_ref, cb_ref, pb_ref, k_ref, v_ref, t_ref, info_ref,
    e_ref, inv_ref, o_ref, cq_ref, pq_ref,
    keys, values, raw, lean, mix, tops, sums,
):
    parts, seg, _ = q_ref.shape
    queries = parts * seg
    old = parts * (cuts[0] + cuts[1])
    in_place_order(k_ref, keys, cuts)
    in_place_order(v_ref, values, cuts)
    q = q_ref[...].reshape(queries, DH)
    content_q = (q + cb_ref[...]).astype(BF16)
    position_q = (q + pb_ref[...]).astype(BF16)
    cq_ref[...] = content_q.reshape(parts, seg, DH)
    pq_ref[...] = position_q.reshape(parts, seg, DH)
    for block in range(queries // BLOCK):
        row0 = block * BLOCK
        width = old + row0 + BLOCK
        skip = queries - BLOCK - row0
        raw[:, :width] = mm(content_q[row0 : row0 + BLOCK], keys[:width, :], NT)
        lean[:, :width] = mm(position_q[row0 : row0 + BLOCK], t_ref[skip : skip + width, :], NT)
        for chunk in range(BLOCK // CHUNK):
            r0 = chunk * CHUNK
            rows = slice(r0, r0 + CHUNK)
            turned = lean_left(lean[rows, :width], r0, width // LANES)
            score = raw[rows, :width] + turned
            start = info_ref[row0 + r0 : row0 + r0 + CHUNK, 0:1].astype(jnp.int32)
            shade = info_ref[row0 + r0 : row0 + r0 + CHUNK, 1:2]
            past = score[:, :old] + shade
            place = lax.broadcasted_iota(jnp.int32, (CHUNK, row0 + BLOCK), 1)
            own = lax.broadcasted_iota(jnp.int32, (CHUNK, row0 + BLOCK), 0) + (row0 + r0)
            now = jnp.where((place <= own) & (place >= start), score[:, old:], MASKED)
            raw[rows, :old] = past
            raw[rows, old:width] = now
            top = past[:, :LANES]
            for low in range(LANES, old, LANES):
                top = jnp.maximum(top, past[:, low : low + LANES])
            for low in range(0, row0 + BLOCK, LANES):
                top = jnp.maximum(top, now[:, low : low + LANES])
            tops[rows, :] = top
        top = jnp.max(tops[...], axis=1, keepdims=True)
        tops[...] = jnp.broadcast_to(top, (BLOCK, LANES))
        for chunk in range(BLOCK // CHUNK):
            r0 = chunk * CHUNK
            rows = slice(r0, r0 + CHUNK)
            top = tops[rows, :]
            total = jnp.zeros((CHUNK, LANES), F32)
            for low in range(0, width, LANES):
                weight = jnp.exp2((raw[rows, low : low + LANES] - top) * (SCALE * LOG2E))
                total = total + weight
                e_ref[row0 + r0 : row0 + r0 + CHUNK, low : low + LANES] = weight.astype(BF16)
            sums[rows, :] = total
        total = jnp.sum(sums[...], axis=1, keepdims=True)
        inv_ref[row0 : row0 + BLOCK, :] = jnp.broadcast_to(1.0 / total, (BLOCK, DH))
        mix[row0 : row0 + BLOCK, :] = mm(
            e_ref[row0 : row0 + BLOCK, :width], values[:width, :], NN
        )
    o_ref[...] = (mix[...] * inv_ref[...]).astype(BF16).reshape(parts, seg, DH)


def attend(query, content_shift, position_shift, keys, values, table_rev, info, cuts):
    parts, group, seg, cols = query.shape
    rows = keys.shape[2]
    queries, key_count, heads = parts * seg, parts * rows, cols // DH
    by_head = lambda size: pl.BlockSpec((parts, None, size, DH), lambda s, h: (0, s, 0, h))
    grid_spec = pl.GridSpec(
        grid=(group, heads),
        in_specs=[
            by_head(seg),
            pl.BlockSpec((1, DH), lambda s, h: (0, h)),
            pl.BlockSpec((1, DH), lambda s, h: (0, h)),
            by_head(rows),
            by_head(rows),
            pl.BlockSpec((key_count, DH), lambda s, h: (0, h)),
            pl.BlockSpec((None, queries, LANES), lambda s, h: (s, 0, 0)),
        ],
        out_specs=[
            pl.BlockSpec((None, None, queries, key_count), lambda s, h: (s, h, 0, 0)),
            pl.BlockSpec((None, None, queries, DH), lambda s, h: (s, h, 0, 0)),
            by_head(seg),
            by_head(seg),
            by_head(seg),
        ],
        scratch_shapes=[
            pltpu.VMEM((key_count, DH), BF16),
            pltpu.VMEM((key_count, DH), BF16),
            pltpu.VMEM((BLOCK, key_count), F32),
            pltpu.VMEM((BLOCK, key_count), F32),
            pltpu.VMEM((queries, DH), F32),
            pltpu.VMEM((BLOCK, LANES), F32),
            pltpu.VMEM((BLOCK, LANES), F32),
        ],
    )
    small = jax.ShapeDtypeStruct((parts, group, seg, cols), BF16)
    return pl.pallas_call(
        functools.partial(attend_kernel, cuts),
        grid_spec=grid_spec,
        out_shape=[
            jax.ShapeDtypeStruct((group, heads, queries, key_count), BF16),
            jax.ShapeDtypeStruct((group, heads, queries, DH), F32),
            small,
            small,
            small,
        ],
        compiler_params=pltpu.CompilerParams(
            dimension_semantics=("arbitrary", "arbitrary"), vmem_limit_bytes=VMEM_LIMIT
        ),
        cost_estimate=cost(40),
        name="attend",
    )(query, content_shift, position_shift, keys, values, table_rev, info)


def pull_kernel(
    cuts, e_ref, inv_ref, o_ref, g_ref, cq_ref, pq_ref, k_ref, v_ref, t_ref,
    dq_ref, dk_ref, dv_ref, ks_ref, vs_ref, dt_ref, sums_ref,
    keys, values, grad, prob, part, score, lean, key_sum, value_sum,
):
    stream = pl.program_id(1)
    parts, seg, _ = g_ref.shape
    queries = parts * seg
    old = parts * (cuts[0] + cuts[1])
    in_place_order(k_ref, keys, cuts)
    in_place_order(v_ref, values, cuts)
    grad[...] = (g_ref[...].reshape(queries, DH).astype(F32) * inv_ref[...]).astype(BF16)
    attended = o_ref[...].reshape(queries, DH)
    content_q = cq_ref[...].reshape(queries, DH)
    position_q = pq_ref[...].reshape(queries, DH)

    @pl.when(stream == 0)
    def _():
        dt_ref[...] = jnp.zeros_like(dt_ref)
        sums_ref[...] = jnp.zeros_like(sums_ref)

    key_sum[...] = jnp.zeros_like(key_sum)
    value_sum[...] = jnp.zeros_like(value_sum)
    content_total = jnp.zeros((1, DH), F32)
    position_total = jnp.zeros((1, DH), F32)
    query_total = jnp.zeros((1, DH), F32)
    flip = flip_matrix(BF16)
    turn = lambda rows: mm(flip, rows, NN).astype(BF16)
    for block in range(queries // BLOCK):
        row0 = block * BLOCK
        width = old + row0 + BLOCK
        skip = queries - BLOCK - row0
        rows = slice(row0, row0 + BLOCK)
        grad_back = turn(grad[rows, :])
        dots_back = jnp.sum(
            grad_back.astype(F32) * turn(attended[rows]).astype(F32), axis=1, keepdims=True
        )
        content_back = turn(content_q[rows])
        position_back = turn(position_q[rows])
        prob[:, :width] = mm(grad_back, values[:width, :], NT)
        both = mm(jnp.concatenate([flip, grad[rows, :].T], axis=0), e_ref[rows, :width], NN)
        part[:, :width] = both[:BLOCK]
        value_sum[:, :width] += both[BLOCK:]
        for chunk in range(BLOCK // CHUNK):
            r0 = chunk * CHUNK
            mean = dots_back[r0 : r0 + CHUNK, 0:1]
            change = part[r0 : r0 + CHUNK, :width] * (prob[r0 : r0 + CHUNK, :width] - mean)
            score[r0 : r0 + CHUNK, :width] = change.astype(BF16)
            lean[r0 : r0 + CHUNK, :width] = lean_right(change, r0).astype(BF16)
        content_grad = (mm(score[:, :width], keys[:width, :], NN) * SCALE).astype(BF16).astype(F32)
        position_grad = (
            (mm(lean[:, :width], t_ref[skip : skip + width, :], NN) * SCALE)
            .astype(BF16)
            .astype(F32)
        )
        query_grad = turn((content_grad + position_grad).astype(BF16))
        content_total += jnp.sum(content_grad, axis=0, keepdims=True)
        position_total += jnp.sum(position_grad, axis=0, keepdims=True)
        query_total += jnp.sum(query_grad.astype(F32), axis=0, keepdims=True)
        dq_ref[rows, :] = query_grad
        key_sum[:, :width] += mm(content_back, score[:, :width], TN)
        dt_ref[:, skip : skip + width] += mm(position_back, lean[:, :width], TN) * SCALE
    key_cols = (key_sum[...] * SCALE).astype(BF16)
    value_cols = value_sum[...].astype(BF16)
    dk_ref[...] = key_cols
    dv_ref[...] = value_cols
    ks_ref[...] = (key_sum[:, old:] * SCALE).T.astype(BF16)
    vs_ref[...] = value_sum[:, old:].T.astype(BF16)
    ones = jnp.ones((8, key_cols.shape[1]), BF16)
    key_total = mm(ones, key_cols, NT)[0:1]
    value_total = mm(ones, value_cols, NT)[0:1]
    sums_ref[...] += jnp.concatenate(
        [
            content_total,
            position_total,
            query_total,
            key_total,
            value_total,
            jnp.zeros((3, DH), F32),
        ],
        axis=0,
    )


def pull(weights, inverse, attended, out_grad, content_q, position_q, keys, values, table_rev, cuts):
    parts, group, seg, cols = out_grad.shape
    rows = keys.shape[2]
    queries, key_count, heads = parts * seg, parts * rows, cols // DH
    by_head = lambda size: pl.BlockSpec((parts, None, size, DH), lambda h, s: (0, s, 0, h))
    by_row = lambda: pl.BlockSpec((None, queries, DH), lambda h, s: (s, 0, h))
    by_place = lambda: pl.BlockSpec((None, DH, key_count), lambda h, s: (s, h, 0))
    grid_spec = pl.GridSpec(
        grid=(heads, group),
        in_specs=[
            pl.BlockSpec((None, None, queries, key_count), lambda h, s: (s, h, 0, 0)),
            pl.BlockSpec((None, None, queries, DH), lambda h, s: (s, h, 0, 0)),
            by_head(seg),
            by_head(seg),
            by_head(seg),
            by_head(seg),
            by_head(rows),
            by_head(rows),
            pl.BlockSpec((key_count, DH), lambda h, s: (0, h)),
        ],
        out_specs=[
            by_row(),
            by_place(),
            by_place(),
            by_row(),
            by_row(),
            pl.BlockSpec((None, DH, key_count), lambda h, s: (h, 0, 0)),
            pl.BlockSpec((None, 8, DH), lambda h, s: (h, 0, 0)),
        ],
        scratch_shapes=[
            pltpu.VMEM((key_count, DH), BF16),
            pltpu.VMEM((key_count, DH), BF16),
            pltpu.VMEM((queries, DH), BF16),
            pltpu.VMEM((BLOCK, key_count), F32),
            pltpu.VMEM((BLOCK, key_count), F32),
            pltpu.VMEM((BLOCK, key_count), BF16),
            pltpu.VMEM((BLOCK, key_count), BF16),
            pltpu.VMEM((DH, key_count), F32),
            pltpu.VMEM((DH, key_count), F32),
        ],
    )
    return pl.pallas_call(
        functools.partial(pull_kernel, cuts),
        grid_spec=grid_spec,
        out_shape=[
            jax.ShapeDtypeStruct((group, queries, cols), BF16),
            jax.ShapeDtypeStruct((group, cols, key_count), BF16),
            jax.ShapeDtypeStruct((group, cols, key_count), BF16),
            jax.ShapeDtypeStruct((group, queries, cols), BF16),
            jax.ShapeDtypeStruct((group, queries, cols), BF16),
            jax.ShapeDtypeStruct((heads, DH, key_count), F32),
            jax.ShapeDtypeStruct((heads, 8, DH), F32),
        ],
        compiler_params=pltpu.CompilerParams(
            dimension_semantics=("arbitrary", "arbitrary"), vmem_limit_bytes=VMEM_LIMIT
        ),
        cost_estimate=cost(39),
        name="pull",
    )(weights, inverse, attended, out_grad, content_q, position_q, keys, values, table_rev)


def project_kernel(
    cuts, rows_ref, gain_ref, shift_ref, w_ref, old_ref, mem_ref, seg_ref, q_ref, k_ref, v_ref, normed
):
    rows, width = rows_ref.shape
    cols = k_ref.shape[1]
    step = 64 if rows % 64 == 0 else 32
    for low in range(0, rows, step):
        wide = rows_ref[low : low + step, :].astype(F32)
        centred = wide - jnp.mean(wide, axis=1, keepdims=True)
        rate = lax.rsqrt(jnp.mean(centred * centred, axis=1, keepdims=True) + EPSILON)
        normed[low : low + step, :] = (centred * rate * gain_ref[...] + shift_ref[...]).astype(BF16)
    cut = cuts[0] + cuts[1]
    old_ref[...] = normed[: cuts[0], :]
    mem_ref[...] = normed[cuts[0] : cut, :]
    seg_ref[...] = normed[cut:, :]
    q_ref[...] = mm(normed[cut:, :], w_ref[:, :cols], NN)
    k_ref[...] = mm(normed[...], w_ref[:, cols : 2 * cols], NN).astype(BF16)
    v_ref[...] = mm(normed[...], w_ref[:, 2 * cols : 3 * cols], NN).astype(BF16)


def project(rows_all, gain, shift, columns, cuts):
    parts, group, each, width = rows_all.shape
    cols = columns.shape[1] // 4
    block = lambda size, wide: pl.BlockSpec((None, None, size, wide), lambda p, s: (p, s, 0, 0))
    placed = lambda size: pl.BlockSpec((None, size, width), lambda p, s: (s, p, 0))
    whole = lambda *shape: pl.BlockSpec(shape, lambda p, s: (0,) * len(shape))
    shape = lambda size, kind: jax.ShapeDtypeStruct((parts, group, size, cols), kind)
    return pl.pallas_call(
        functools.partial(project_kernel, cuts),
        grid_spec=pl.GridSpec(
            grid=(parts, group),
            in_specs=[
                block(each, width),
                whole(1, width),
                whole(1, width),
                whole(width, 4 * cols),
            ],
            out_specs=[placed(size) for size in cuts]
            + [block(cuts[2], cols), block(each, cols), block(each, cols)],
            scratch_shapes=[pltpu.VMEM((each, width), BF16)],
        ),
        out_shape=[jax.ShapeDtypeStruct((group, parts * size, width), BF16) for size in cuts]
        + [shape(cuts[2], F32), shape(each, BF16), shape(each, BF16)],
        compiler_params=pltpu.CompilerParams(
            dimension_semantics=("arbitrary", "arbitrary"), vmem_limit_bytes=VMEM_LIMIT
        ),
        cost_estimate=cost(17),
        name="project",
    )(rows_all, gain, shift, columns)


def gelu_both(x):
    near = jnp.abs(x)
    t = 1.0 / (1.0 + (0.3275911 * math.sqrt(0.5)) * near)
    bell = jnp.exp2((x * x) * (-0.5 * LOG2E))
    tail = 0.5 * 1.061405429
    for factor in (-1.453152027, 1.421413741, -0.284496736, 0.254829592):
        tail = tail * t + 0.5 * factor
    tail = tail * t * bell
    below = jnp.where(x < 0.0, tail, 1.0 - tail)
    return x * below, below + x * bell * (1.0 / math.sqrt(2.0 * math.pi))


def forward_back_kernel(
    last, parts, pair, n_ref, c_ref, *rest,
):
    up_refs, down_refs, shift_ref = rest[:parts], rest[parts : parts + pair], rest[parts + pair]
    rest = rest[parts + pair + 1 :]
    if last:
        part_in, grad_in, part_out, part_far, grad_out, grad_far, late_ref, sums_ref = rest[:8]
        pre, slope, hidden, act, up_out, down_out, sems, part_ref, grad_ref = rest[8:]
    else:
        part_ref, grad_ref, late_ref, sums_ref = rest[:4]
        pre, slope, hidden, act, up_out, down_out, sems = rest[4:]
    tile = pl.program_id(0)
    tiles = pl.num_programs(0)
    cols, units = up_refs[0].shape
    unit_cols, width = down_refs[0].shape
    rows = n_ref.shape[0]
    slot = lax.rem(tile, 2)
    up_weight = jnp.concatenate([ref[...] for ref in up_refs], axis=0)
    down_weight = jnp.concatenate([ref[...] for ref in down_refs], axis=0)

    def copies(at, index):
        return (
            pltpu.make_async_copy(
                up_out.at[at],
                late_ref.at[:, pl.ds(0, cols), pl.ds(pl.multiple_of(index * units, units), units)],
                sems.at[at, 0],
            ),
            pltpu.make_async_copy(
                down_out.at[at],
                late_ref.at[pl.ds(index * pair, pair), pl.ds(cols, unit_cols), :],
                sems.at[at, 1],
            ),
        )

    @pl.when(tile == 0)
    def _():
        if last:
            part_ref[...] = part_in[...]
            grad_ref[...] = grad_in[...]
        else:
            part_ref[...] = jnp.zeros_like(part_ref)
            grad_ref[...] = jnp.zeros_like(grad_ref)

    pre[...] = mm(n_ref[...], up_weight, NN)
    slope[...] = mm(c_ref[...], down_weight, NT)
    step = 64
    for low in range(0, rows, step):
        value, change = gelu_both(pre[low : low + step, :] + shift_ref[...])
        hidden[low : low + step, :] = value.astype(BF16)
        act[low : low + step, :] = (change * slope[low : low + step, :]).astype(BF16)
    part_ref[...] += mm(hidden[...], down_weight, NN)
    grad_ref[...] += mm(act[...], up_weight, NT)
    sums_ref[...] = jnp.sum(act[...].astype(F32), axis=0, keepdims=True)

    @pl.when(tile >= 2)
    def _():
        for copy in copies(slot, tile - 2):
            copy.wait()

    up_out[slot] = mm(n_ref[...], act[...], TN).astype(BF16).reshape(parts, cols, units)
    down_out[slot] = mm(hidden[...], c_ref[...], TN).astype(BF16).reshape(pair, unit_cols, width)
    for copy in copies(slot, tile):
        copy.start()

    @pl.when(tile == tiles - 1)
    def _():
        if last:
            part_out[...] = part_ref[: rows // 2, :]
            part_far[...] = part_ref[rows // 2 :, :].astype(BF16)
            grad_out[...] = grad_ref[: rows // 2, :]
            grad_far[...] = grad_ref[rows // 2 :, :].astype(BF16)
        for copy in (copies(1 - slot, tile - 1) if parts > pair else ()) + copies(slot, tile):
            copy.wait()


def forward_back(normed, cot, gathered, shift, carry):
    parts, _, width = gathered.shape
    rows = normed.shape[0]
    cols = width // parts
    unit_cols = shift.shape[1] // parts
    pair = 2
    units = pair * unit_cols
    last = len(carry) > 0
    one = pl.Buffered(1)
    whole = lambda *shape: pl.BlockSpec(shape, lambda t: (0,) * len(shape), pipeline_mode=one)
    up = lambda p: pl.BlockSpec((None, cols, units), lambda t: (p, 0, t))
    down = lambda i: pl.BlockSpec(
        (None, unit_cols, width), lambda t: (t * pair + i, cols // unit_cols, 0)
    )
    if last:
        sums = [((rows // 2, width), F32), ((rows // 2, width), BF16)] * 2
    else:
        sums = [((rows, width), F32)] * 2
    return pl.pallas_call(
        functools.partial(forward_back_kernel, last, parts, pair),
        grid_spec=pl.GridSpec(
            grid=(parts // pair,),
            in_specs=[
                whole(rows, width),
                whole(rows, width),
            ]
            + [up(p) for p in range(parts)]
            + [down(i) for i in range(pair)]
            + [pl.BlockSpec((1, units), lambda t: (0, t))]
            + [whole(rows, width) for _ in carry],
            out_specs=[whole(*shape) for shape, _ in sums]
            + [
                pl.BlockSpec(memory_space=pl.ANY),
                pl.BlockSpec((1, units), lambda t: (0, t)),
            ],
            scratch_shapes=[
                pltpu.VMEM((rows, units), F32),
                pltpu.VMEM((rows, units), F32),
                pltpu.VMEM((rows, units), BF16),
                pltpu.VMEM((rows, units), BF16),
                pltpu.VMEM((2, parts, cols, units), BF16),
                pltpu.VMEM((2, pair, unit_cols, width), BF16),
                pltpu.SemaphoreType.DMA((2, 2)),
            ]
            + [pltpu.VMEM((rows, width), F32) for _ in carry],
        ),
        out_shape=[jax.ShapeDtypeStruct(shape, kind) for shape, kind in sums]
        + [
            jax.ShapeDtypeStruct((parts, cols + unit_cols, width), BF16),
            jax.ShapeDtypeStruct((1, parts * unit_cols), F32),
        ],
        compiler_params=pltpu.CompilerParams(
            dimension_semantics=("arbitrary",), vmem_limit_bytes=VMEM_LIMIT
        ),
        cost_estimate=cost(29),
        name="forward_back",
    )(normed, cot, *[gathered] * (parts + pair), shift, *carry)


def leave_kernel(a_ref, s_ref, w_ref, shift_ref, gain_ref, bias_ref, flat_ref, m_ref, n_ref):
    parts = a_ref.shape[0]
    flat_ref[...] = jnp.concatenate([a_ref[part] for part in range(parts)], axis=1)
    m_ref[...] = s_ref[...].astype(F32) + (mm(flat_ref[...], w_ref[...], NN) + shift_ref[...])
    step = 32
    for low in range(0, m_ref.shape[0], step):
        unit, _ = standardise(m_ref[low : low + step, :])
        n_ref[low : low + step, :] = (unit * gain_ref[...] + bias_ref[...]).astype(BF16)


def leave(mixed_heads, segment, base, weight, shift, gain, bias):
    parts, group, seg, cols = mixed_heads.shape
    width = parts * cols
    rows = lambda: pl.BlockSpec((None, seg, width), lambda s: (s, 0, 0))
    vector = lambda: pl.BlockSpec((1, width), lambda s: (0, 0))
    shape = lambda kind: jax.ShapeDtypeStruct((group, seg, width), kind)
    return pl.pallas_call(
        leave_kernel,
        grid_spec=pl.GridSpec(
            grid=(group,),
            in_specs=[
                pl.BlockSpec((parts, None, seg, cols), lambda s: (0, s, 0, 0)),
                pl.BlockSpec((None, seg, width), lambda s: (s + base, 0, 0)),
                pl.BlockSpec((width, width), lambda s: (0, 0)),
                vector(),
                vector(),
                vector(),
            ],
            out_specs=[rows(), rows(), rows()],
        ),
        out_shape=[shape(BF16), shape(F32), shape(BF16)],
        compiler_params=pltpu.CompilerParams(vmem_limit_bytes=VMEM_LIMIT),
        cost_estimate=cost(6),
        name="leave",
    )(mixed_heads, segment, weight, shift, gain, bias)


def enter_kernel(
    m_ref, g_ref, far_ref, c_ref, w_ref, gain_ref, mg_ref, b_ref, a_ref, sums_ref
):
    @pl.when(pl.program_id(0) == 0)
    def _():
        sums_ref[...] = jnp.zeros_like(sums_ref)

    parts = a_ref.shape[0]
    rows, width = m_ref.shape
    step = 32
    total = [jnp.zeros((1, width), F32) for _ in range(4)]
    for low in range(0, rows, step):
        at = slice(low, low + step)
        unit, rate = standardise(m_ref[at, :])
        grad = g_ref[at, :] + far_ref[at, :].astype(F32)
        cot = c_ref[at, :].astype(F32)
        middle_grad = cot + standardise_back(unit, rate, grad, gain_ref[...])
        branch = middle_grad.astype(BF16)
        mg_ref[at, :] = middle_grad
        b_ref[at, :] = branch
        for i, value in enumerate((branch.astype(F32), grad * unit, grad, cot)):
            total[i] = total[i] + jnp.sum(value, axis=0, keepdims=True)
    sums_ref[...] += jnp.concatenate(total + [jnp.zeros((4, width), F32)], axis=0)
    for part in range(parts):
        low = part * a_ref.shape[2]
        weight = w_ref[low : low + a_ref.shape[2], :]
        a_ref[part] = mm(b_ref[...], weight, NT).astype(BF16)


def enter(middle, grad, far, cot, base, weight, gain, parts):
    group, seg, width = middle.shape
    cols = width // parts
    rows = lambda: pl.BlockSpec((None, seg, width), lambda s: (s, 0, 0))
    later = lambda: pl.BlockSpec((None, seg, width), lambda s: (s + base, 0, 0))
    shape = lambda kind: jax.ShapeDtypeStruct((group, seg, width), kind)
    return pl.pallas_call(
        enter_kernel,
        grid_spec=pl.GridSpec(
            grid=(group,),
            in_specs=[
                rows(),
                later(),
                later(),
                later(),
                pl.BlockSpec((width, width), lambda s: (0, 0)),
                pl.BlockSpec((1, width), lambda s: (0, 0)),
            ],
            out_specs=[
                rows(),
                rows(),
                pl.BlockSpec((parts, None, seg, cols), lambda s: (0, s, 0, 0)),
                pl.BlockSpec((8, width), lambda s: (0, 0)),
            ],
        ),
        out_shape=[
            shape(F32),
            shape(BF16),
            jax.ShapeDtypeStruct((parts, group, seg, cols), BF16),
            jax.ShapeDtypeStruct((8, width), F32),
        ],
        compiler_params=pltpu.CompilerParams(
            dimension_semantics=("arbitrary",), vmem_limit_bytes=VMEM_LIMIT
        ),
        cost_estimate=cost(7),
        name="enter",
    )(middle, grad, far, cot, weight, gain)


def compress_kernel(low, rows_ref, w_ref, shift_ref, out_ref, wide):
    count = out_ref.shape[0]
    cols = out_ref.shape[1]
    blocks = wide.shape[0]
    for at in range(blocks):
        wide[at] = rows_ref[low : low + 3 * count, at * LANES : (at + 1) * LANES].astype(F32)
    total = jnp.broadcast_to(shift_ref[...], (count, cols))
    for k in range(3):
        every = jnp.concatenate(
            [wide[at, pl.ds(k, count, stride=3), :] for at in range(blocks)], axis=1
        ).astype(BF16)
        total = total + mm(every, w_ref[:, k * cols : (k + 1) * cols], NN)
    out_ref[...] = total.astype(BF16)


def compress(rows_all, columns, shift, low, count):
    parts, group, each, width = rows_all.shape
    cols = columns.shape[1] // 3
    return pl.pallas_call(
        functools.partial(compress_kernel, low),
        grid_spec=pl.GridSpec(
            grid=(parts, group),
            in_specs=[
                pl.BlockSpec((None, None, each, width), lambda p, s: (p, s, 0, 0)),
                pl.BlockSpec((width, 3 * cols), lambda p, s: (0, 0)),
                pl.BlockSpec((1, cols), lambda p, s: (0, 0)),
            ],
            out_specs=pl.BlockSpec((None, None, count, cols), lambda p, s: (p, s, 0, 0)),
            scratch_shapes=[pltpu.VMEM((width // LANES, 3 * count, LANES), F32)],
        ),
        out_shape=jax.ShapeDtypeStruct((parts, group, count, cols), BF16),
        compiler_params=pltpu.CompilerParams(
            dimension_semantics=("arbitrary", "arbitrary"), vmem_limit_bytes=VMEM_LIMIT
        ),
        cost_estimate=cost(6.5),
        name="compress",
    )(rows_all, columns, shift)


def lay_out_kernel(
    parts, unit_cols, core_ref, a_ref, b_ref, c_ref, d_ref, up_ref, down_ref
):
    flipped = core_ref[0] == 1
    for half, (mine_ref, far_ref) in enumerate(((a_ref, c_ref), (b_ref, d_ref))):
        mine, far = mine_ref[...].astype(F32), far_ref[...].astype(F32)
        for core, value in enumerate(
            (jnp.where(flipped, far, mine), jnp.where(flipped, mine, far))
        ):
            for part in range(parts):
                at = ((part * 2 + core) * 2 + half) * unit_cols
                up_ref[:, at : at + unit_cols] = value[
                    0, :, part * unit_cols : (part + 1) * unit_cols
                ]
            down_ref[2 * core + half] = value[1]


def lay_out(core, mine, far, parts):
    _, rows, width = mine.shape
    step = rows // 4 if rows % 64 == 0 else rows
    half = lambda i: pl.BlockSpec((2, step, width), lambda r, *_: (i, r, 0))
    return pl.pallas_call(
        functools.partial(lay_out_kernel, parts, rows),
        grid_spec=pltpu.PrefetchScalarGridSpec(
            num_scalar_prefetch=1,
            grid=(rows // step,),
            in_specs=[half(0), half(1), half(0), half(1)],
            out_specs=[
                pl.BlockSpec((step, 4 * width), lambda r, *_: (r, 0)),
                pl.BlockSpec((4, step, width), lambda r, *_: (0, r, 0)),
            ],
        ),
        out_shape=[
            jax.ShapeDtypeStruct((rows, 4 * width), F32),
            jax.ShapeDtypeStruct((4, rows, width), F32),
        ],
        compiler_params=pltpu.CompilerParams(vmem_limit_bytes=VMEM_LIMIT),
        cost_estimate=cost(4),
        name="lay_out",
    )(core.reshape(1), mine, mine, far, far)


def lay_squares_kernel(in_ref, *out_refs):
    parts = in_ref.shape[0]
    cols = in_ref.shape[2] // len(out_refs)
    for at, out_ref in enumerate(out_refs):
        for part in range(parts):
            out_ref[:, part * cols : (part + 1) * cols] = in_ref[
                part, :, at * cols : (at + 1) * cols
            ].astype(F32)


def lay_squares(summed, rows):
    parts, _, wide = summed.shape
    width = parts * wide // 4
    step = rows // 2
    return pl.pallas_call(
        lay_squares_kernel,
        grid_spec=pl.GridSpec(
            grid=(2,),
            in_specs=[pl.BlockSpec((parts, step, wide), lambda i: (0, i, 0))],
            out_specs=[pl.BlockSpec((step, width), lambda i: (i, 0)) for _ in range(4)],
        ),
        out_shape=[jax.ShapeDtypeStruct((rows, width), F32) for _ in range(4)],
        compiler_params=pltpu.CompilerParams(vmem_limit_bytes=VMEM_LIMIT),
        cost_estimate=cost(2.5),
        name="lay_squares",
    )(summed)


def settle_kernel(
    me_ref, old_ref, mem_ref, seg_ref, q_ref, k_ref, v_ref, ks_ref, vs_ref, w_ref, table_ref, dt_ref,
    sums_ref, gain_ref, shift_ref, small_ref, part_ref, out_ref, total,
):
    stream = pl.program_id(0)
    parts, rows, wide = out_ref.shape
    cols = wide // 4
    width = parts * cols

    @pl.when(stream == 0)
    def _():
        total[...] = jnp.zeros_like(total)

    total[:cols, :] += mm(q_ref[...], seg_ref[...], TN)
    for at, grad in ((cols, k_ref), (2 * cols, v_ref)):
        low = 0
        for normed in (old_ref, mem_ref, seg_ref):
            high = low + normed.shape[0]
            total[at : at + cols, :] += mm(grad[:, low:high], normed[...], NN)
            low = high
    three = jnp.concatenate([q_ref[...], ks_ref[...], vs_ref[...]], axis=1)
    part = mm(three, w_ref[:, : 3 * cols], NT).astype(BF16)
    part_ref[...] = part.reshape(part_ref.shape)

    @pl.when(stream == pl.num_programs(0) - 1)
    def _():
        heads = dt_ref.shape[0]
        rel = jnp.concatenate(
            [mm(dt_ref[head].astype(BF16), table_ref[...], NN) for head in range(heads)], axis=0
        )
        line = lambda row: jnp.concatenate(
            [sums_ref[head, row : row + 1, :] for head in range(heads)], axis=1
        )
        row_sums = jnp.concatenate([line(2), line(3), line(4)], axis=1)
        weight = w_ref[:, : 3 * cols].astype(F32)
        shift_grad = lax.dot_general(
            jnp.broadcast_to(row_sums, (8, 3 * cols)),
            weight,
            (NT, ((), ())),
            precision=lax.Precision.HIGHEST,
            preferred_element_type=F32,
        )[0:1]
        along = jnp.sum(weight.T * total[...], axis=0, keepdims=True)
        gain_grad = (along - shift_ref[...] * shift_grad) / gain_ref[...]
        for at in range(parts):
            low, high = at * cols, (at + 1) * cols
            out_ref[at, :cols, : 3 * cols] = total[:, low:high].T.astype(BF16)
            out_ref[at, :cols, 3 * cols :] = rel[:, low:high].T.astype(BF16)
            mine = (me_ref[0] == at).astype(F32)
            none = jnp.zeros((1, 2 * cols), F32)
            first = jnp.concatenate([gain_grad[:, low:high], shift_grad[:, low:high], none], axis=1)
            second = jnp.concatenate([none, mine * line(0), mine * line(1)], axis=1)
            added = jnp.concatenate([first, second, jnp.zeros((14, wide), F32)], axis=0)
            out_ref[at, cols:, :] = (small_ref[at] + added).astype(BF16)


def settle(me, normed, grads, columns, table, table_grad, sums, gain, shift, small, parts):
    group, queries, width = normed[2].shape
    cols = width // parts
    wide = 4 * cols
    block = lambda array: pl.BlockSpec((None, *array.shape[1:]), lambda s, *_: (s, 0, 0))
    whole = lambda *shape: pl.BlockSpec(
        shape, lambda s, *_: (0,) * len(shape), pipeline_mode=pl.Buffered(1)
    )
    return pl.pallas_call(
        settle_kernel,
        grid_spec=pltpu.PrefetchScalarGridSpec(
            num_scalar_prefetch=1,
            grid=(group,),
            in_specs=[block(rows) for rows in normed]
            + [block(grad) for grad in grads]
            + [
                whole(*columns.shape),
                whole(*table.shape),
                whole(*table_grad.shape),
                whole(*sums.shape),
                whole(1, width),
                whole(1, width),
                whole(*small.shape),
            ],
            out_specs=[
                pl.BlockSpec((parts, None, queries // parts, width), lambda s, *_: (0, s, 0, 0)),
                whole(parts, cols + 16, wide),
            ],
            scratch_shapes=[pltpu.VMEM((3 * cols, width), F32)],
        ),
        out_shape=[
            jax.ShapeDtypeStruct((parts, group, queries // parts, width), BF16),
            jax.ShapeDtypeStruct((parts, cols + 16, wide), BF16),
        ],
        compiler_params=pltpu.CompilerParams(
            dimension_semantics=("arbitrary",), vmem_limit_bytes=VMEM_LIMIT
        ),
        cost_estimate=cost(14),
        name="settle",
    )(me.reshape(1), *normed, *grads, columns, table, table_grad, sums, gain, shift, small)


def standardise(rows):
    mean = jnp.mean(rows, axis=-1, keepdims=True)
    centred = rows - mean
    rate = lax.rsqrt(jnp.mean(centred * centred, axis=-1, keepdims=True) + EPSILON)
    return centred * rate, rate


def standardise_back(unit, rate, grad, gain):
    scaled = grad * gain
    mean = jnp.mean(scaled, axis=-1, keepdims=True)
    along = jnp.mean(scaled * unit, axis=-1, keepdims=True)
    return rate * (scaled - mean - unit * along)


def sinusoid_reversed(rows, width):
    positions = (rows - 1 - jnp.arange(rows, dtype=jnp.int32)).astype(F32)[:, None]
    frequency = jnp.exp(
        jnp.arange(width // 2, dtype=F32) * (-2.0 * math.log(10000.0) / width)
    )
    angles = positions * frequency[None, :]
    return jnp.concatenate([jnp.sin(angles), jnp.cos(angles)], axis=1).astype(BF16)


def dot(left, right):
    return mm(left, right, NN)


def swap(value):
    return lax.ppermute(value, "core", [(0, 1), (1, 0)])


def exchange(blocks, name, axis=0):
    count = lax.axis_size(name)
    me = lax.axis_index(name)
    block = lambda at: lax.dynamic_index_in_dim(blocks, at, axis, keepdims=False)
    return [block(me)] + [
        lax.ppermute(block(me ^ apart), name, [(i, i ^ apart) for i in range(count)])
        for apart in range(1, count)
    ]


def collect(block, name):
    count = lax.axis_size(name)
    me = lax.axis_index(name)
    found = jnp.stack(
        [block]
        + [
            lax.ppermute(block, name, [(i, i ^ apart) for i in range(count)])
            for apart in range(1, count)
        ]
    )
    return jnp.stack(
        [lax.dynamic_index_in_dim(found, me ^ i, 0, keepdims=False) for i in range(count)]
    )


def add_up(arrays, kind=BF16):
    total = arrays[0].astype(F32)
    for array in arrays[1:]:
        total = total + array.astype(F32)
    return total.astype(kind)


def body(
    segment, memory, compressed, eob, reset, ln1_gain, ln1_bias, w_query, w_key, w_value,
    w_out, out_bias, w_rel, bias_content, bias_position, ln2_gain, ln2_bias, w_up, up_bias,
    w_down, down_bias, conv_weight, conv_bias, cotangent,
):
    parts = lax.axis_size("seq")
    layers = lax.axis_size("z")
    core = lax.axis_index("core")
    me = lax.axis_index("seq")
    group, seg, width = segment.shape
    mem, old = memory.shape[1], compressed.shape[1]
    cuts = (old, mem, seg)
    each = old + mem + seg
    keys_in_all = parts * each
    cols = width // parts
    wide = 4 * cols
    own = group * seg
    unit_cols = w_up.shape[1] // (4 * parts)
    barrier = lax.optimization_barrier

    def by_columns(matrices):
        count = matrices.shape[0]
        sent = matrices.reshape(count, cols, parts, cols).transpose(2, 1, 0, 3)
        return sent.reshape(parts, cols, count * cols)

    up_bias_own = lax.dynamic_slice_in_dim(up_bias, core * 2 * unit_cols, 2 * unit_cols, 0)
    vectors = jnp.concatenate(
        [ln1_gain, ln1_bias, out_bias, ln2_gain, ln2_bias, down_bias, up_bias_own]
    )
    vectors = jnp.pad(vectors.reshape(2, wide), ((0, 14), (0, 0)))
    half = cols // 2
    sent = by_columns(jnp.concatenate([jnp.stack([w_query, w_key, w_value, w_rel]), conv_weight]))
    sent = lax.dynamic_slice_in_dim(sent, core * half, half, 1)
    out_half = lax.dynamic_slice_in_dim(w_out, core * half, half, 0)
    sent = jnp.concatenate([sent, jnp.broadcast_to(out_half, (parts, half, width))], axis=2)
    vectors = jnp.pad(vectors, ((0, 0), (0, 3 * cols + width)))
    sent = jnp.concatenate([sent, jnp.broadcast_to(vectors, (parts, *vectors.shape))], axis=1)
    got = lax.all_to_all(sent, "seq", 0, 0, tiled=True)
    spans = [(0, group)]
    local = [
        jnp.concatenate([compressed[low:high], memory[low:high], segment[low:high]], axis=1)
        for low, high in spans
    ]
    rows_all = [lax.all_gather(local[0], "seq")]
    mine = got[:, :half]
    far = swap(mine)
    columns = jnp.stack(
        [jnp.where(core == 0, mine, far), jnp.where(core == 0, far, mine)], axis=1
    ).reshape(width, 7 * cols + width)
    columns, conv_columns, out_full = (
        columns[:, :wide],
        columns[:, wide : 7 * cols],
        columns[:, 7 * cols :],
    )
    vectors = got[:, half : half + 2, :wide].reshape(parts, 2 * wide).astype(F32)
    gain_one, shift_one, out_shift, gain_two, shift_two, down_shift = (
        vectors[:, cols * i : cols * (i + 1)].reshape(1, width) for i in range(6)
    )
    up_shift = vectors[:, 6 * cols :].reshape(parts, 2, unit_cols).transpose(1, 0, 2)
    up_shift = up_shift.reshape(2, 1, parts * unit_cols)
    up_quarters = lax.dynamic_slice_in_dim(
        w_up.reshape(cols, parts, 2, 2, unit_cols), core, 1, 2
    ).reshape(cols, parts, 2, unit_cols)
    up_quarters = [up_quarters[:, :, i].reshape(cols, width) for i in range(2)]
    down_half = lax.dynamic_slice_in_dim(w_down, core * 2 * unit_cols, 2 * unit_cols, 0)
    down_quarters = [down_half[unit_cols * i : unit_cols * (i + 1)] for i in range(2)]
    first = jnp.concatenate([up_quarters[0], down_quarters[0]], axis=0)
    second = jnp.concatenate([up_quarters[1], down_quarters[1]], axis=0)
    cot_own = cotangent.reshape(own, width)
    cot_both = jnp.concatenate([cot_own, swap(cot_own)], axis=0)

    table_rev = sinusoid_reversed(keys_in_all, width)
    proj_rev = dot(table_rev, columns[:, 3 * cols :]).astype(BF16)
    index = jnp.arange(eob.shape[1], dtype=jnp.int32)[None, :]
    opens = jnp.pad(eob, ((0, 0), (1, 0)))[:, :-1] == 1
    start = lax.cummax(jnp.where(opens, index, 0), axis=1)
    shade = jnp.where((start == 0) & (reset[:, None] == 0), 0.0, MASKED)
    info = jnp.stack([start.astype(F32), shade], axis=2)
    info = jnp.pad(info, ((0, 0), (0, 0), (0, LANES - 2)))
    rows_all[0], proj_rev, info, cot_both, table_rev, columns, conv_columns, out_full, *local = barrier(
        (rows_all[0], proj_rev, info, cot_both, table_rev, columns, conv_columns, out_full, *local)
    )
    rows_all = [rows_all[0]] + [lax.all_gather(rows, "seq") for rows in local[1:]]

    kept, heads = [], []
    for batch, (low, high) in enumerate(spans):
        if batch == len(spans) - 1:
            rows_all[batch], first, *heads = barrier((rows_all[batch], first, *heads))
            first = lax.all_gather(first, "seq")
        *normed, query, keys, values = project(rows_all[batch], gain_one, shift_one, columns, cuts)
        second, query = barrier((second, query))
        second = lax.all_gather(second, "seq")
        weights, inverse, mixed_heads, content_q, position_q = attend(
            query,
            bias_content.astype(F32).reshape(1, cols),
            bias_position.astype(F32).reshape(1, cols),
            keys,
            values,
            proj_rev,
            info[low:high],
            cuts,
        )
        kept.append((weights, inverse, mixed_heads, content_q, position_q, keys, values))
        heads.append(lax.all_to_all(mixed_heads, "seq", 0, 0, tiled=True))

    mixed_heads, conv_columns = barrier((mixed_heads, conv_columns))
    packed = compress(
        rows_all[0], conv_columns, conv_bias.astype(F32).reshape(1, cols), old, mem // 3
    )
    packed, *heads = barrier((packed, *heads))

    attended, middle, normed_two = [], [], []
    for (low, high), batch in zip(spans, heads):
        one, two, three = leave(batch, segment, low, out_full, out_shift, gain_two, shift_two)
        attended.append(one.reshape(-1, width))
        middle.append(two)
        normed_two.append(three.reshape(-1, width))
    both = jnp.concatenate(normed_two + [swap(rows) for rows in normed_two], axis=0)
    part, part_grad, late_one, unit_one = forward_back(both, cot_both, first, up_shift[0], ())
    late_one = lax.psum_scatter(
        late_one.reshape(-1, width), "seq", scatter_dimension=0, tiled=True
    )
    part, part_far, part_grad, grad_far, late_two, unit_two = forward_back(
        both, cot_both, second, up_shift[1], (part, part_grad)
    )
    grad_far = swap(grad_far)
    by_stream = lambda rows: rows.reshape(group, seg, width)
    middle_grad, branch_grad, head_grad, sums_two = [], [], [], 0.0
    for (low, high), batch in zip(spans, middle):
        one, two, three, four = enter(
            batch, by_stream(part_grad), by_stream(grad_far), cotangent, low, out_full, gain_two, parts
        )
        middle_grad.append(one)
        branch_grad.append(two.reshape(-1, width))
        three, part_grad = barrier((three, part_grad))
        head_grad.append(lax.all_to_all(three, "seq", 0, 0, tiled=True))
        sums_two = sums_two + four
    result = part + swap(part_far).astype(F32) + down_shift
    output = (jnp.concatenate(middle).reshape(own, width) + result).astype(BF16)
    output = output.reshape(group, seg, width)

    out_shift_grad, gain_two_grad, shift_two_grad, down_shift_grad = (
        sums_two[i].reshape(parts, cols) for i in range(4)
    )
    none = jnp.zeros((parts, 2 * cols), F32)
    unit_sums = jnp.stack(
        [unit_one.reshape(parts, unit_cols), unit_two.reshape(parts, unit_cols)], axis=1
    ).reshape(parts, 2 * unit_cols)
    small = jnp.stack(
        [
            jnp.concatenate([none, out_shift_grad, gain_two_grad], axis=1),
            jnp.concatenate([shift_two_grad, down_shift_grad, none], axis=1),
            jnp.concatenate(
                [jnp.where(core == 0, unit_sums, 0.0), jnp.where(core == 1, unit_sums, 0.0)], axis=1
            ),
        ],
        axis=1,
    )
    small = jnp.pad(small, ((0, 0), (0, 13), (0, 0)))
    weights, inverse, mixed_heads, content_q, position_q, keys, values = kept[0]
    out_grad = mm(jnp.concatenate(attended), jnp.concatenate(branch_grad), TN)
    out_grad = out_grad.astype(BF16).reshape(parts, cols, width)
    late_one, small, out_grad, late_two, head_grad = barrier(
        (late_one, small, out_grad, late_two, head_grad[0])
    )
    late_two = lax.psum_scatter(
        late_two.reshape(-1, width), "seq", scatter_dimension=0, tiled=True
    )
    late_one = exchange(late_one.reshape(layers, -1, width), "z")
    query_grad, *key_grads, table_grad, sums = pull(
        weights, inverse, mixed_heads, head_grad, content_q, position_q, keys, values, proj_rev, cuts
    )
    late_one, late_two, out_grad, query_grad = barrier((late_one, late_two, out_grad, query_grad))
    late_two = exchange(late_two.reshape(layers, -1, width), "z")
    out_sent = exchange(out_grad, "seq")
    late_one = add_up(late_one)
    seg_part, square_grads = settle(
        me, normed, (query_grad, *key_grads), columns, table_rev, table_grad, sums, gain_one,
        shift_one, small, parts,
    )
    late_two, out_sent, square_grads = barrier((late_two, out_sent, square_grads))
    summed = lax.all_to_all(square_grads, "seq", 0, 0, tiled=True)
    late = collect(jnp.stack([late_one, add_up(late_two)]), "z")
    out_sent = add_up(out_sent)
    late, out_sent, summed, seg_part = barrier((late, out_sent, summed, seg_part))
    squares = parts * (cols + 16)
    summed = jnp.concatenate([summed.reshape(squares, wide), out_sent.reshape(-1, wide)], axis=0)
    summed, packed = barrier((summed, packed))
    summed = lax.psum(summed, ("z", "core"))
    packed = jnp.stack(exchange(packed, "seq"))
    new_compressed = jnp.concatenate(
        [lax.dynamic_index_in_dim(packed, p ^ me, 0, keepdims=False) for p in range(parts)], axis=2
    )
    seg_grad = lax.all_to_all(seg_part, "seq", 0, 0, tiled=True).astype(F32)
    seg_grad = jnp.sum(seg_grad, axis=0).reshape(own, width)
    unit_seg, rate_seg = standardise(segment.reshape(own, width).astype(F32))
    rows_grad = standardise_back(unit_seg, rate_seg, seg_grad, gain_one)
    segment_grad = jnp.concatenate(middle_grad, axis=0) + by_stream(rows_grad)

    late = late.reshape(layers, 2, -1, width).transpose(1, 0, 2, 3).reshape(4, unit_cols, width)
    up_w, down_w = lay_out(core, late, swap(late), parts)
    down_w = down_w.reshape(4 * unit_cols, width)
    summed, output, segment_grad, new_compressed, up_w, down_w = barrier(
        (summed, output, segment_grad, new_compressed, up_w, down_w)
    )
    out_w = summed[squares:].reshape(cols, width).astype(F32)
    summed = summed[:squares].reshape(parts, cols + 16, wide)
    query_w, key_w, value_w, rel_w = lay_squares(summed, cols)
    small = jnp.sum(summed[:, cols : cols + 3].astype(F32), axis=0)
    piece = lambda row, i: small[row, cols * i : cols * (i + 1)]
    return (
        output,
        segment_grad,
        piece(0, 0),
        piece(0, 1),
        query_w,
        key_w,
        value_w,
        out_w,
        piece(0, 2),
        rel_w,
        piece(1, 2),
        piece(1, 3),
        piece(0, 3),
        piece(1, 0),
        up_w,
        small[2],
        down_w,
        piece(1, 1),
        new_compressed,
    )


def solution(mesh):
    dp = mesh.shape["dp"]
    cores = jax.sharding.Mesh(
        mesh.devices.reshape(dp // 2, 2, mesh.shape["seq"]), ("z", "core", "seq")
    )
    rows = P(("z", "core"), "seq", None)
    shard, matrix = P("seq"), P("seq", None)
    return jax.shard_map(
        body,
        mesh=cores,
        in_specs=(
            rows, rows, rows, P(("z", "core"), None), P(("z", "core")), shard, shard, matrix,
            matrix, matrix, matrix, shard, matrix, shard, shard, shard, shard, matrix, shard,
            matrix, shard, P(None, "seq", None), shard, rows,
        ),
        out_specs=(
            rows, rows, shard, shard, matrix, matrix, matrix, matrix, shard, matrix, shard,
            shard, shard, shard, matrix, shard, matrix, shard, rows,
        ),
        check_vma=False,
    )
```

profile of v0, /device:TPU:0, one launch (start us, length us, event | category | flops | bytes accessed | tf_op | source)
XLA Modules:
  0.0 585.9 jit_solution(5266909359258005052)
XLA Ops:
  26.3 3.8 pad_maximum_fusion
  30.1 7.5 %copy.118 = bf16[4,144,2816]{2,1,0:T(8,128)(2,1)} copy(bf16[4,144,2816]{1,2,0:T(8,128)(2,1)} %pad_maximum_fusion) | data formatting | bytes 6488064 | tf_op jit(solution)/shard_map/concatenate | solution.py:960
  37.6 5.3 all-to-all-start
  44.6 48.2 %all-to-all-done = bf16[4,144,2816]{2,1,0:T(8,128)(2,1)S(1)} async-done(((bf16[4,144,2816]{2,1,0:T(8,128)(2,1)}), bf16[4,144,2816]{2,1,0:T(8,128)(2,1)S(1)}, u32[]{:S(2)}, u32[]{:S(2)}) %all-to-all-start) | async-done | bytes 3244064 | tf_op jit(solution)/shard_map/all_to_all | solution.py:961
  98.2 4.5 reshape.346
  109.3 13.8 %fusion = (bf16[1792,512]{1,0:T(8,128)(2,1)S(1)}, bf16[1792,512]{1,0:T(8,128)(2,1)S(1)}) fusion(f32[512]{0:T(512)S(1)} %multiply_exponential_fusion, f32[1792]{0:T(1024)S(1)} %subtract_convert_fusion), kind=kLoop, calls=%fused_computation.6 | loop fusion | flops 2752512 | bytes 3679232 | tf_op jit(solution)/shard_map/convert.4
  137.4 16.6 %all-gather.7.cloned.1.call-done = bf16[12,448,1024]{2,1,0:T(8,128)(2,1)} async-done(((bf16[3,448,1024]{2,1,0:T(8,128)(2,1)}), bf16[12,448,1024]{2,1,0:T(8,128)(2,1)}) %all-gather.7.cloned.1.call-update) | async-done | bytes 11010064 | tf_op jit(solution)/shard_map/all_gather | solution.py:967
  155.6 18.3 %project.1 = (bf16[3,256,1024]{2,1,0:T(8,128)(2,1)}, bf16[3,768,1024]{2,1,0:T(8,128)(2,1)}, bf16[3,768,1024]{2,1,0:T(8,128)(2,1)}, f32[4,3,192,256]{3,2,1,0:T(8,...) custom-call(bf16[4,3,448,1024]{3,2,1,0:T(8,128)(2,1)} %bitcast.181, f32[1,1024]{1,0:T(1,128)} %bitcast.224, ...), custom_call_target="tpu_custom_call" | custom-call | flops 195500000 | tf_op jit(solution)/shard_map/project/pallas_call | solution.py:379
  175.0 29.7 %attend.1 = (bf16[3,2,768,1792]{3,2,1,0:T(8,128)(2,1)}, f32[3,2,768,128]{3,2,1,0:T(8,128)}, bf16[4,3,192,256]{3,2,1,0:T(8,128)(2,1)}, bf16[4,3,192,256]{3,2,1,0:T(8,128)(2,1)}, bf16[4,3,192,256]{3,2,1,0:T(8,128)(2,1)}) custom-call(f32[4,3,192,256]{3,2,1,0:T(8,128)} %get-tuple-element.115.q_ref, f32[1,256]{1,0:T(1,128)} %bitcast.250, f32[1,256]{1,0:T(1,128)} %bitcast.251, ...), custom_call_target="tpu_custom_call" | custom-call | flops 460000000 | tf_op jit(solution)/shard_map/attend/pallas_call | solution.py:189
  204.7 3.5 all-to-all-start.1
  211.1 11.8 %compress.1 = bf16[4,3,64,256]{3,2,1,0:T(8,128)(2,1)} custom-call(bf16[4,3,448,1024]{3,2,1,0:T(8,128)(2,1)} %bitcast.182, bf16[1024,768]{1,0:T(8,128)(2,1)} %slice.159.w_ref, f32[1,256]{1,0:T(1,128)} %bitcast.241), custom_call_target="tpu_custom_call" | custom-call | flops 74750000 | tf_op jit(solution)/shard_map/compress/pallas_call | solution.py:672
  226.9 5.9 %leave.1 = (bf16[3,192,1024]{2,1,0:T(8,128)(2,1)}, f32[3,192,1024]{2,1,0:T(8,128)}, bf16[3,192,1024]{2,1,0:T(8,128)(2,1)}) custom-call(bf16[4,3,192,256]{3,2,1,0:T(8,128)(2,1)} %copy-done.8, bf16[3,192,1024]{2,1,0:T(8,128)(2,1)} %s_ref.1, bf16[1024,1024]{1,0:T(8,128)(2,1)} %get-tuple-element.124.w_ref, f32[1,1024]{1,0:T(1,128)} %bitcast.234, ...), custom_call_target="tpu_custom_call" | custom-call | flops 69000000 | tf_op jit(solution)/shard_map/leave/pallas_call | solution.py:565
  238.7 27.7 %forward_back.2 = (f32[1152,1024]{1,0:T(8,128)}, f32[1152,1024]{1,0:T(8,128)}, bf16[4,512,1024]{2,1,0:T(8,128)(2,1)}, f32[1,1024]{1,0:T(1,128)}) custom-call(bf16[1152,1024]{1,0:T(8,128)(2,1)} %pad_maximum_fusion.5.n_ref, bf16[1152,1024]{1,0:T(8,128)(2,1)} %pad_maximum_fusion.4.c_ref, bf16[4,512,1024]{2,1,0:T(8,128)(2,1)} %bitcast.175, ...), custom_call_target="tpu_custom_call" | custom-call | flops 333500000 | tf_op jit(solution)/shard_map/forward_back/pallas_call | solution.py:508
  267.0 29.2 %forward_back.3 = (f32[576,1024]{1,0:T(8,128)}, bf16[576,1024]{1,0:T(8,128)(2,1)}, f32[576,1024]{1,0:T(8,128)}, bf16[576,1024]{1,0:T(8,128)(2,1)}, bf16[4,512,1024]{2,1,0:T(8,128)(2,1)}, /*index=5*/f32[1,1024]{1,0:T(1,128)}) custom-call(bf16[1152,1024]{1,0:T(8,128)(2,1)} %pad_maximum_fusion.5.n_ref, bf16[1152,1024]{1,0:T(8,128)(2,1)} %pad_maximum_fusion.4.c_ref, ...), custom_call_target="tpu_custom_call" | custom-call | flops 333500000 | tf_op jit(solution)/shard_map/forward_back/pallas_call | solution.py:508
  300.3 8.5 %enter.1 = (f32[3,192,1024]{2,1,0:T(8,128)}, bf16[3,192,1024]{2,1,0:T(8,128)(2,1)}, bf16[4,3,192,256]{3,2,1,0:T(8,128)(2,1)}, f32[8,1024]{1,0:T(8,128)}) custom-call(f32[3,192,1024]{2,1,0:T(8,128)} %get-tuple-element.129.m_ref, f32[3,192,1024]{2,1,0:T(8,128)} %bitcast.199, bf16[3,192,1024]{2,1,0:T(8,128)(2,1)} %bitcast.212, bf16[3,192,1024]{2,1,0:T(8,128)(2,1)} %c_ref.1, ...), custom_call_target="tpu_custom_call" | custom-call | flops 80500000 | tf_op jit(solution)/shard_map/enter/pallas_call | solution.py:621
  308.9 3.5 all-to-all-start.2
  313.6 3.5 bitcast_convert_fusion
  317.0 15.6 %all-to-all-done.2.g_ref = bf16[4,3,192,256]{3,2,1,0:T(8,128)(2,1)S(1)} async-done(((bf16[4,3,192,256]{3,2,1,0:T(8,128)(2,1)}), bf16[4,3,192,256]{3,2,1,0:T(8,128)(2,1)S(1)}, u32[]{:S(2)}, u32[]{:S(2)}) %all-to-all-start.2) | async-done | bytes 1179680 | tf_op jit(solution)/shard_map/all_to_all | solution.py:1059
  339.5 34.8 %pull.1 = (bf16[3,768,256]{2,1,0:T(8,128)(2,1)}, bf16[3,256,1792]{2,1,0:T(8,128)(2,1)}, bf16[3,256,1792]{2,1,0:T(8,128)(2,1)}, bf16[3,768,256]{2,1,0:T(8,128)(2,...) custom-call(bf16[3,2,768,1792]{3,2,1,0:T(8,128)(2,1)} %get-tuple-element.146.e_ref, ...), custom_call_target="tpu_custom_call" | custom-call | flops 448500000 | tf_op jit(solution)/shard_map/pull/pallas_call | solution.py:332
  374.4 13.8 %reduce-scatter.5.cloned.1.call-done = bf16[512,1024]{1,0:T(8,128)(2,1)} async-done(((bf16[2048,1024]{1,0:T(8,128)(2,1)}), bf16[512,1024]{1,0:T(8,128)(2,1)}) %reduce-scatter.5.cloned.1.call-update) | async-done | bytes 1048592 | tf_op jit(solution)/shard_map/reduce_scatter | solution.py:1089
  398.8 3.7 collective-permute-start.9
  402.5 23.2 %settle.1 = (bf16[4,3,192,1024]{3,2,1,0:T(8,128)(2,1)}, bf16[4,272,1024]{2,1,0:T(8,128)(2,1)}) custom-call(s32[1]{0:T(128)} %bitcast.46.me_ref, bf16[3,256,1024]{2,1,0:T(8,128)(2,1)} %get-tuple-element.158.old_ref, bf16[3,768,1024]{2,1,0:T(8,128)(2,1)} %get-tuple-element.159.mem_ref, bf16[3,768,1024]{2,1,0:T(8,128)(2,1)} %get-tuple-element.160.seg_ref, ...), custom_call_target="tpu_custom_call" | custom-call | flops 161000000 | tf_op jit(solution)/shard_map/settle/pallas_call | solution.py:827
  425.9 4.9 all-to-all-start.3
  438.9 11.2 %collective-permute-done.15 = bf16[2,128,1024]{2,1,0:T(8,128)(2,1)S(1)} collective-permute-done((bf16[2,128,1024]{2,1,0:T(8,128)(2,1)S(1)}, bf16[2,128,1024]{2,1,0:T(8,128)(2,1)S(1)}, u32[]{:S(2)}, u32[]{:S(2)}) %collective-permute-start.15) | collective-permute-done | bytes 524320 | tf_op jit(solution)/shard_map/ppermute | solution.py:908
  450.1 27.7 %collective-permute-done.14 = bf16[2,128,1024]{2,1,0:T(8,128)(2,1)S(1)} collective-permute-done((bf16[2,128,1024]{2,1,0:T(8,128)(2,1)S(1)}, bf16[2,128,1024]{2,1,0:T(8,128)(2,1)S(1)}, u32[]{:S(2)}, u32[]{:S(2)}) %collective-permute-start.14) | collective-permute-done | bytes 524320 | tf_op jit(solution)/shard_map/ppermute | solution.py:908
  478.6 5.2 all-to-all-start.4
  485.2 3.5 pad_maximum_fusion.3
  493.9 4.4 fusion.11
  498.4 40.5 %collective-permute-done.19 = bf16[3,64,256]{2,1,0:T(8,128)(2,1)} collective-permute-done((bf16[3,64,256]{2,1,0:T(8,128)(2,1)}, bf16[3,64,256]{2,1,0:T(8,128)(2,1)}, u32[]{:S(2)}, u32[]{:S(2)}) %collective-permute-start.19) | collective-permute-done | bytes 98336 | tf_op jit(solution)/shard_map/ppermute | solution.py:897
  540.8 5.8 lay_out.1
  546.6 3.8 convert_reduce_fusion
  554.3 14.4 %all-reduce.7.cloned.1.call-done = bf16[1344,1024]{1,0:T(8,128)(2,1)} async-done(((bf16[1344,1024]{1,0:T(8,128)(2,1)}), bf16[1344,1024]{1,0:T(8,128)(2,1)}) %all-reduce.7.cloned.1.call-update) | async-done | bytes 2752528 | tf_op jit(solution)/shard_map/psum | solution.py:1112
  (256 shorter events, 116.5 us)
Async XLA Ops:
  7.2 146.8 %all-gather.7.cloned.1.call-start = ((), (), s32[]{:S(2)}) async-start(), calls=%async_computation.10 | async-start | bytes 13762560 | tf_op jit(solution)/shard_map/all_gather | solution.py:967
  37.6 55.2 %all-to-all-start = ((bf16[4,144,2816]{2,1,0:T(8,128)(2,1)}), bf16[4,144,2816]{2,1,0:T(8,128)(2,1)S(1)}, u32[]{:S(2)}, u32[]{:S(2)}) async-start(bf16[4,144,2816]{2,1,0:T(8,128)(2,1)} %copy.118), calls=%async_computation | async-start | bytes 6488064 | tf_op jit(solution)/shard_map/all_to_all | solution.py:961
  42.8 195.9 %all-gather.9.cloned.1.call-start = ((), (), s32[]{:S(2)}) async-start(), calls=%async_computation.11 | async-start | bytes 5242880 | tf_op jit(solution)/shard_map/all_gather | solution.py:1012
  43.1 82.3 %collective-permute-start.1 = (bf16[576,1024]{1,0:T(8,128)(2,1)}, bf16[576,1024]{1,0:T(8,128)(2,1)}, u32[]{:S(2)}, u32[]{:S(2)}) collective-permute-start(bf16[576,1024]{1,0:T(8,128)(2,1)} %bitcast.194), channel_id=1, source_target_pairs={{0,4},{4,0},{1,5},{5,1},{2,6},{6,2},{3,7},{7,3},{8,12},{12,8},{9,1... | collective-permute-start | bytes 3538952 | tf_op jit(solution)/shard_map/ppermute | solution.py:889
  94.9 33.5 %collective-permute-start = (bf16[4,128,2816]{2,1,0:T(8,128)(2,1)}, bf16[4,128,2816]{2,1,0:T(8,128)(2,1)}, u32[]{:S(2)}, u32[]{:S(2)}) collective-permute-start(bf16[4,128,2816]{2,1,0:T(8,128)(2,1)} %slice.155), channel_id=1, source_target_pairs={{0,4},{4,0},{1,5},{5,1},{2,6},{6,2},{3,7},{7,3},{8,12},{12,8},{9,1... | collective-permute-start | bytes 8650760 | tf_op jit(solution)/shard_map/ppermute | solution.py:889
  154.0 113.0 %all-gather.11.cloned.1.call-start = ((), (), s32[]{:S(2)}) async-start(), calls=%async_computation.12 | async-start | bytes 5242880 | tf_op jit(solution)/shard_map/all_gather | solution.py:1015
  204.7 21.2 %all-to-all-start.1 = ((bf16[4,3,192,256]{3,2,1,0:T(8,128)(2,1)}), bf16[4,3,192,256]{3,2,1,0:T(8,128)(2,1)S(1)}, u32[]{:S(2)}, u32[]{:S(2)}) async-start(bf16[4,3,192,256]{3,2,1,0:T(8,128)(2,1)} %get-tuple-element.120.o_ref), calls=%async_computation.1 | async-start | bytes 2359296 | tf_op jit(solution)/shard_map/all_to_all | solution.py:1027
  208.3 124.4 %reduce-scatter.3.cloned.1.call-start = ((), (), s32[]{:S(2)}) async-start(), calls=%async_computation.7 | async-start | bytes 5242880 | tf_op jit(solution)/shard_map/reduce_scatter | solution.py:1043
  232.8 3.1 collective-permute-start.2
  296.2 3.1 collective-permute-start.3
  308.9 23.7 %all-to-all-start.2 = ((bf16[4,3,192,256]{3,2,1,0:T(8,128)(2,1)}), bf16[4,3,192,256]{3,2,1,0:T(8,128)(2,1)S(1)}, u32[]{:S(2)}, u32[]{:S(2)}) async-start(bf16[4,3,192,256]{3,2,1,0:T(8,128)(2,1)} %get-tuple-element.142), calls=%async_computation.3 | async-start | bytes 2359296 | tf_op jit(solution)/shard_map/all_to_all | solution.py:1059
  312.5 75.7 %reduce-scatter.5.cloned.1.call-start = ((), (), s32[]{:S(2)}) async-start(), calls=%async_computation.8 | async-start | bytes 5242880 | tf_op jit(solution)/shard_map/reduce_scatter | solution.py:1089
  335.1 39.2 %collective-permute-start.4 = (bf16[128,1024]{1,0:T(8,128)(2,1)}, bf16[128,1024]{1,0:T(8,128)(2,1)S(1)}, u32[]{:S(2)}, u32[]{:S(2)}) collective-permute-start(bf16[128,1024]{1,0:T(8,128)(2,1)} %get-tuple-element.229), channel_id=1, source_target_pairs={{0,8},{8,0},{16,24},{24,16},{1,9},{9,1},{17,25},{25,17},{2,10},{10... | collective-permute-start | bytes 786440 | tf_op jit(solution)/shard_map/ppermute | solution.py:897
  336.6 37.7 %collective-permute-start.5 = (bf16[128,1024]{1,0:T(8,128)(2,1)}, bf16[128,1024]{1,0:T(8,128)(2,1)S(1)}, u32[]{:S(2)}, u32[]{:S(2)}) collective-permute-start(bf16[128,1024]{1,0:T(8,128)(2,1)} %get-tuple-element.228), channel_id=1, source_target_pairs={{0,16},{8,24},{16,0},{24,8},{1,17},{9,25},{17,1},{25,9},{2,18},{10... | collective-permute-start | bytes 786440 | tf_op jit(solution)/shard_map/ppermute | solution.py:897
  339.1 35.3 %collective-permute-start.6 = (bf16[128,1024]{1,0:T(8,128)(2,1)}, bf16[128,1024]{1,0:T(8,128)(2,1)S(1)}, u32[]{:S(2)}, u32[]{:S(2)}) collective-permute-start(bf16[128,1024]{1,0:T(8,128)(2,1)} %get-tuple-element.227), channel_id=1, source_target_pairs={{0,24},{8,16},{16,8},{24,0},{1,25},{9,17},{17,9},{25,1},{2,26},{10... | collective-permute-start | bytes 786440 | tf_op jit(solution)/shard_map/ppermute | solution.py:897
  390.3 8.6 %collective-permute-start.7 = (bf16[128,1024]{1,0:T(8,128)(2,1)S(1)}, bf16[128,1024]{1,0:T(8,128)(2,1)S(1)}, u32[]{:S(2)}, u32[]{:S(2)}) collective-permute-start(bf16[128,1024]{1,0:T(8,128)(2,1)S(1)} %get-tuple-element.225), channel_id=1, source_target_pairs={{0,8},{8,0},{16,24},{24,16},{1,9},{9,1},{17,25},{25,17},{2,10},{10... | collective-permute-start | bytes 786440 | tf_op jit(solution)/shard_map/ppermute | solution.py:897
  392.9 32.9 %collective-permute-start.10 = (bf16[256,1024]{1,0:T(8,128)(2,1)}, bf16[256,1024]{1,0:T(8,128)(2,1)S(1)}, u32[]{:S(2)}, u32[]{:S(2)}) collective-permute-start(bf16[256,1024]{1,0:T(8,128)(2,1)} %get-tuple-element.219), channel_id=1, source_target_pairs={{0,1},{1,0},{2,3},{3,2},{4,5},{5,4},{6,7},{7,6},{8,9},{9,8},{10,11... | collective-permute-start | bytes 1572872 | tf_op jit(solution)/shard_map/ppermute | solution.py:897
  394.3 31.6 %collective-permute-start.11 = (bf16[256,1024]{1,0:T(8,128)(2,1)}, bf16[256,1024]{1,0:T(8,128)(2,1)S(1)}, u32[]{:S(2)}, u32[]{:S(2)}) collective-permute-start(bf16[256,1024]{1,0:T(8,128)(2,1)} %get-tuple-element.218), channel_id=1, source_target_pairs={{0,2},{1,3},{2,0},{3,1},{4,6},{5,7},{6,4},{7,5},{8,10},{9,11},{10,... | collective-permute-start | bytes 1572872 | tf_op jit(solution)/shard_map/ppermute | solution.py:897
  394.9 30.9 %collective-permute-start.12 = (bf16[256,1024]{1,0:T(8,128)(2,1)S(1)}, bf16[256,1024]{1,0:T(8,128)(2,1)S(1)}, u32[]{:S(2)}, u32[]{:S(2)}) collective-permute-start(bf16[256,1024]{1,0:T(8,128)(2,1)S(1)} %get-tuple-element.217), channel_id=1, source_target_pairs={{0,3},{1,2},{2,1},{3,0},{4,7},{5,6},{6,5},{7,4},{8,11},{9,10},{10,... | collective-permute-start | bytes 1572872 | tf_op jit(solution)/shard_map/ppermute | solution.py:897
  396.4 29.4 %collective-permute-start.8 = (bf16[128,1024]{1,0:T(8,128)(2,1)}, bf16[128,1024]{1,0:T(8,128)(2,1)}, u32[]{:S(2)}, u32[]{:S(2)}) collective-permute-start(bf16[128,1024]{1,0:T(8,128)(2,1)} %get-tuple-element.224), channel_id=1, source_target_pairs={{0,16},{8,24},{16,0},{24,8},{1,17},{9,25},{17,1},{25,9},{2,18},{10... | collective-permute-start | bytes 786440 | tf_op jit(solution)/shard_map/ppermute | solution.py:897
  398.8 27.0 %collective-permute-start.9 = (bf16[128,1024]{1,0:T(8,128)(2,1)}, bf16[128,1024]{1,0:T(8,128)(2,1)}, u32[]{:S(2)}, u32[]{:S(2)}) collective-permute-start(bf16[128,1024]{1,0:T(8,128)(2,1)} %get-tuple-element.223), channel_id=1, source_target_pairs={{0,24},{8,16},{16,8},{24,0},{1,25},{9,17},{17,9},{25,1},{2,26},{10... | collective-permute-start | bytes 786440 | tf_op jit(solution)/shard_map/ppermute | solution.py:897
  425.9 52.7 %all-to-all-start.3 = ((bf16[4,272,1024]{2,1,0:T(8,128)(2,1)}), bf16[4,272,1024]{2,1,0:T(8,128)(2,1)}, u32[]{:S(2)}, u32[]{:S(2)}) async-start(bf16[4,272,1024]{2,1,0:T(8,128)(2,1)} %get-tuple-element.179), calls=%async_computation.5 | async-start | bytes 4456448 | tf_op jit(solution)/shard_map/all_to_all | solution.py:1105
  433.3 16.8 %collective-permute-start.15 = (bf16[2,128,1024]{2,1,0:T(8,128)(2,1)S(1)}, bf16[2,128,1024]{2,1,0:T(8,128)(2,1)S(1)}, u32[]{:S(2)}, u32[]{:S(2)}) collective-permute-start(bf16[2,128,1024]{2,1,0:T(8,128)(2,1)S(1)} %get-tuple-element.234), channel_id=1, source_target_pairs={{0,24},{8,16},{16,8},{24,0},{1,25},{9,17},{17,9},{25,1},{2,26},{10... | collective-permute-start | bytes 1572872 | tf_op jit(solution)/shard_map/ppermute | solution.py:908
  433.5 44.3 %collective-permute-start.14 = (bf16[2,128,1024]{2,1,0:T(8,128)(2,1)S(1)}, bf16[2,128,1024]{2,1,0:T(8,128)(2,1)S(1)}, u32[]{:S(2)}, u32[]{:S(2)}) collective-permute-start(bf16[2,128,1024]{2,1,0:T(8,128)(2,1)S(1)} %get-tuple-element.234), channel_id=1, source_target_pairs={{0,16},{8,24},{16,0},{24,8},{1,17},{9,25},{17,1},{25,9},{2,18},{10... | collective-permute-start | bytes 1572872 | tf_op jit(solution)/shard_map/ppermute | solution.py:908
  434.8 43.0 %collective-permute-start.13 = (bf16[2,128,1024]{2,1,0:T(8,128)(2,1)S(1)}, bf16[2,128,1024]{2,1,0:T(8,128)(2,1)S(1)}, u32[]{:S(2)}, u32[]{:S(2)}) collective-permute-start(bf16[2,128,1024]{2,1,0:T(8,128)(2,1)S(1)} %get-tuple-element.234), channel_id=1, source_target_pairs={{0,8},{8,0},{16,24},{24,16},{1,9},{9,1},{17,25},{25,17},{2,10},{10... | collective-permute-start | bytes 1572872 | tf_op jit(solution)/shard_map/ppermute | solution.py:908
  478.6 68.1 %all-to-all-start.4 = ((bf16[4,3,192,1024]{3,2,1,0:T(8,128)(2,1)}), bf16[4,3,192,1024]{3,2,1,0:T(8,128)(2,1)}, u32[]{:S(2)}, u32[]{:S(2)}) async-start(bf16[4,3,192,1024]{3,2,1,0:T(8,128)(2,1)} %get-tuple-element.188), calls=%async_computation.6 | async-start | bytes 9437184 | tf_op jit(solution)/shard_map/all_to_all | solution.py:1117
  483.8 84.9 %all-reduce.7.cloned.1.call-start = ((), (), s32[]{:S(2)}) async-start(), calls=%async_computation.9 | async-start | bytes 5505024 | tf_op jit(solution)/shard_map/psum | solution.py:1112
  483.9 56.9 %collective-permute-start.20 = (bf16[4,256,1024]{2,1,0:T(8,128)(2,1)S(1)}, bf16[4,256,1024]{2,1,0:T(8,128)(2,1)}, u32[]{:S(2)}, u32[]{:S(2)}) collective-permute-start(bf16[4,256,1024]{2,1,0:T(8,128)(2,1)S(1)} %bitcast.186), channel_id=1, source_target_pairs={{0,4},{4,0},{1,5},{5,1},{2,6},{6,2},{3,7},{7,3},{8,12},{12,8},{9,1... | collective-permute-start | bytes 6291464 | tf_op jit(solution)/shard_map/ppermute | solution.py:889
  484.0 10.0 %collective-permute-start.16 = (bf16[576,1024]{1,0:T(8,128)(2,1)}, bf16[576,1024]{1,0:T(8,128)(2,1)}, u32[]{:S(2)}, u32[]{:S(2)}) collective-permute-start(bf16[576,1024]{1,0:T(8,128)(2,1)} %get-tuple-element.186), channel_id=1, source_target_pairs={{0,4},{4,0},{1,5},{5,1},{2,6},{6,2},{3,7},{7,3},{8,12},{12,8},{9,1... | collective-permute-start | bytes 3538952 | tf_op jit(solution)/shard_map/ppermute | solution.py:889
  490.4 48.4 %collective-permute-start.19 = (bf16[3,64,256]{2,1,0:T(8,128)(2,1)}, bf16[3,64,256]{2,1,0:T(8,128)(2,1)}, u32[]{:S(2)}, u32[]{:S(2)}) collective-permute-start(bf16[3,64,256]{2,1,0:T(8,128)(2,1)} %get-tuple-element.240), channel_id=1, source_target_pairs={{0,3},{1,2},{2,1},{3,0},{4,7},{5,6},{6,5},{7,4},{8,11},{9,10},{10,... | collective-permute-start | bytes 294920 | tf_op jit(solution)/shard_map/ppermute | solution.py:897
  493.3 45.6 %collective-permute-start.18 = (bf16[3,64,256]{2,1,0:T(8,128)(2,1)}, bf16[3,64,256]{2,1,0:T(8,128)(2,1)}, u32[]{:S(2)}, u32[]{:S(2)}) collective-permute-start(bf16[3,64,256]{2,1,0:T(8,128)(2,1)} %get-tuple-element.241), channel_id=1, source_target_pairs={{0,2},{1,3},{2,0},{3,1},{4,6},{5,7},{6,4},{7,5},{8,10},{9,11},{10,... | collective-permute-start | bytes 294920 | tf_op jit(solution)/shard_map/ppermute | solution.py:897
  493.8 45.1 %collective-permute-start.17 = (bf16[3,64,256]{2,1,0:T(8,128)(2,1)S(1)}, bf16[3,64,256]{2,1,0:T(8,128)(2,1)}, u32[]{:S(2)}, u32[]{:S(2)}) collective-permute-start(bf16[3,64,256]{2,1,0:T(8,128)(2,1)S(1)} %get-tuple-element.242), channel_id=1, source_target_pairs={{0,1},{1,0},{2,3},{3,2},{4,5},{5,4},{6,7},{7,6},{8,9},{9,8},{10,11... | collective-permute-start | bytes 294920 | tf_op jit(solution)/shard_map/ppermute | solution.py:897
  (39 other events, 223.1 us)
Sparse Core Ops, SparseCore 0:
  12.8 141.1 all-gather.6
  156.4 52.6 all-gather.8
  211.6 53.7 all-gather.10
  268.8 63.5 reduce-scatter.2
  336.0 52.1 reduce-scatter.4
  498.5 70.1 all-reduce.6
where the time goes:
time: 593 us; the launch traced here: 586 us
  Pallas kernels  198 us (33%)
  waiting for transfers between devices  196 us (33%)
  local copies, waits for them, and re-layouts  63.3 us (11%)
  other arithmetic  58.9 us (10%)
  starting transfers between devices  47.9 us (8%)
  between operations  15.5 us (3%)
    pallas_call x2, Pallas kernels, forward_back(): pl.pallas_call(functools.partial(forward_back_kernel, last, parts, pair),...  56.8 us
    all_to_all x1, waiting for transfers between devices, body(): got = lax.all_to_all(sent, 'seq', 0, 0, tiled=True)  48.2 us
    ppermute x12, waiting for transfers between devices, exchange(): lax.ppermute(block(me ^ apart), name, [(i, i ^ apart) for i in range(coun...  40.6 us
    ppermute x3, waiting for transfers between devices, collect(): lax.ppermute(block, name, [(i, i ^ apart) for i in range(count)])  38.9 us
    pallas_call x1, Pallas kernels, pull(): pl.pallas_call(functools.partial(pull_kernel, cuts), grid_spec=grid_spec,...  34.8 us
    pallas_call x1, Pallas kernels, attend(): pl.pallas_call(functools.partial(attend_kernel, cuts), grid_spec=grid_spe...  29.7 us
    pallas_call x1, Pallas kernels, settle(): pl.pallas_call(settle_kernel, grid_spec=pltpu.PrefetchScalarGridSpec(num_...  23.2 us
    unnamed x112, local copies, waits for them, and re-layouts  21.3 us
  transfers between devices with their start and end apart: 32, of which 12 were waited for; matrix products, arithmetic and copies ran while one was open for 19% of the time, Pallas kernels for 33%

commit v1 on v0

--- a/solution.py
+++ b/solution.py
@@ -288,25 +288,25 @@
     )
 
 
-def pull(weights, inverse, attended, out_grad, content_q, position_q, keys, values, table_rev, cuts):
+def pull(head, weights, inverse, attended, out_grad, content_q, position_q, keys, values, table_rev, cuts):
     parts, group, seg, cols = out_grad.shape
     rows = keys.shape[2]
-    queries, key_count, heads = parts * seg, parts * rows, cols // DH
-    by_head = lambda size: pl.BlockSpec((parts, None, size, DH), lambda h, s: (0, s, 0, h))
+    queries, key_count = parts * seg, parts * rows
+    by_head = lambda size: pl.BlockSpec((parts, None, size, DH), lambda h, s: (0, s, 0, head))
     by_row = lambda: pl.BlockSpec((None, queries, DH), lambda h, s: (s, 0, h))
     by_place = lambda: pl.BlockSpec((None, DH, key_count), lambda h, s: (s, h, 0))
     grid_spec = pl.GridSpec(
-        grid=(heads, group),
+        grid=(1, group),
         in_specs=[
-            pl.BlockSpec((None, None, queries, key_count), lambda h, s: (s, h, 0, 0)),
-            pl.BlockSpec((None, None, queries, DH), lambda h, s: (s, h, 0, 0)),
+            pl.BlockSpec((None, None, queries, key_count), lambda h, s: (s, head, 0, 0)),
+            pl.BlockSpec((None, None, queries, DH), lambda h, s: (s, head, 0, 0)),
             by_head(seg),
             by_head(seg),
             by_head(seg),
             by_head(seg),
             by_head(rows),
             by_head(rows),
-            pl.BlockSpec((key_count, DH), lambda h, s: (0, h)),
+            pl.BlockSpec((key_count, DH), lambda h, s: (0, head)),
         ],
         out_specs=[
             by_row(),
@@ -333,13 +333,13 @@
         functools.partial(pull_kernel, cuts),
         grid_spec=grid_spec,
         out_shape=[
-            jax.ShapeDtypeStruct((group, queries, cols), BF16),
-            jax.ShapeDtypeStruct((group, cols, key_count), BF16),
-            jax.ShapeDtypeStruct((group, cols, key_count), BF16),
-            jax.ShapeDtypeStruct((group, queries, cols), BF16),
-            jax.ShapeDtypeStruct((group, queries, cols), BF16),
-            jax.ShapeDtypeStruct((heads, DH, key_count), F32),
-            jax.ShapeDtypeStruct((heads, 8, DH), F32),
+            jax.ShapeDtypeStruct((group, queries, DH), BF16),
+            jax.ShapeDtypeStruct((group, DH, key_count), BF16),
+            jax.ShapeDtypeStruct((group, DH, key_count), BF16),
+            jax.ShapeDtypeStruct((group, queries, DH), BF16),
+            jax.ShapeDtypeStruct((group, queries, DH), BF16),
+            jax.ShapeDtypeStruct((1, DH, key_count), F32),
+            jax.ShapeDtypeStruct((1, 8, DH), F32),
         ],
         compiler_params=pltpu.CompilerParams(
             dimension_semantics=("arbitrary", "arbitrary"), vmem_limit_bytes=VMEM_LIMIT
@@ -354,7 +354,7 @@
 ):
     rows, width = rows_ref.shape
     cols = k_ref.shape[1]
-    step = 64 if rows % 64 == 0 else 32
+    step = 32
     for low in range(0, rows, step):
         wide = rows_ref[low : low + step, :].astype(F32)
         centred = wide - jnp.mean(wide, axis=1, keepdims=True)
@@ -455,15 +455,18 @@
             part_ref[...] = jnp.zeros_like(part_ref)
             grad_ref[...] = jnp.zeros_like(grad_ref)
 
-    pre[...] = mm(n_ref[...], up_weight, NN)
-    slope[...] = mm(c_ref[...], down_weight, NT)
-    step = 64
-    for low in range(0, rows, step):
-        value, change = gelu_both(pre[low : low + step, :] + shift_ref[...])
-        hidden[low : low + step, :] = value.astype(BF16)
-        act[low : low + step, :] = (change * slope[low : low + step, :]).astype(BF16)
-    part_ref[...] += mm(hidden[...], down_weight, NN)
-    grad_ref[...] += mm(act[...], up_weight, NT)
+    chunk = 288 if rows % 288 == 0 else rows
+    for base in range(0, rows, chunk):
+        at = slice(base, base + chunk)
+        pre[at, :] = mm(n_ref[at, :], up_weight, NN)
+        slope[at, :] = mm(c_ref[at, :], down_weight, NT)
+        for low in range(base, base + chunk, 16):
+            some = slice(low, low + 16)
+            value, change = gelu_both(pre[some, :] + shift_ref[...])
+            hidden[some, :] = value.astype(BF16)
+            act[some, :] = (change * slope[some, :]).astype(BF16)
+        part_ref[at, :] += mm(hidden[at, :], down_weight, NN)
+        grad_ref[at, :] += mm(act[at, :], up_weight, NT)
     sums_ref[...] = jnp.sum(act[...].astype(F32), axis=0, keepdims=True)
 
     @pl.when(tile >= 2)
@@ -550,7 +553,7 @@
     parts = a_ref.shape[0]
     flat_ref[...] = jnp.concatenate([a_ref[part] for part in range(parts)], axis=1)
     m_ref[...] = s_ref[...].astype(F32) + (mm(flat_ref[...], w_ref[...], NN) + shift_ref[...])
-    step = 32
+    step = 16
     for low in range(0, m_ref.shape[0], step):
         unit, _ = standardise(m_ref[low : low + step, :])
         n_ref[low : low + step, :] = (unit * gain_ref[...] + bias_ref[...]).astype(BF16)
@@ -592,7 +595,7 @@
 
     parts = a_ref.shape[0]
     rows, width = m_ref.shape
-    step = 32
+    step = 16
     total = [jnp.zeros((1, width), F32) for _ in range(4)]
     for low in range(0, rows, step):
         at = slice(low, low + step)
@@ -708,15 +711,15 @@
 
 
 def lay_out(core, mine, far, parts):
-    _, rows, width = mine.shape
+    _, rows, width = mine[0].shape
     step = rows // 4 if rows % 64 == 0 else rows
-    half = lambda i: pl.BlockSpec((2, step, width), lambda r, *_: (i, r, 0))
+    half = lambda: pl.BlockSpec((2, step, width), lambda r, *_: (0, r, 0))
     return pl.pallas_call(
         functools.partial(lay_out_kernel, parts, rows),
         grid_spec=pltpu.PrefetchScalarGridSpec(
             num_scalar_prefetch=1,
             grid=(rows // step,),
-            in_specs=[half(0), half(1), half(0), half(1)],
+            in_specs=[half(), half(), half(), half()],
             out_specs=[
                 pl.BlockSpec((step, 4 * width), lambda r, *_: (r, 0)),
                 pl.BlockSpec((4, step, width), lambda r, *_: (0, r, 0)),
@@ -729,7 +732,7 @@
         compiler_params=pltpu.CompilerParams(vmem_limit_bytes=VMEM_LIMIT),
         cost_estimate=cost(4),
         name="lay_out",
-    )(core.reshape(1), mine, mine, far, far)
+    )(core.reshape(1), *mine, *far)
 
 
 def lay_squares_kernel(in_ref, *out_refs):
@@ -760,10 +763,11 @@
     )(summed)
 
 
-def settle_kernel(
-    me_ref, old_ref, mem_ref, seg_ref, q_ref, k_ref, v_ref, ks_ref, vs_ref, w_ref, table_ref, dt_ref,
-    sums_ref, gain_ref, shift_ref, small_ref, part_ref, out_ref, total,
-):
+def settle_kernel(heads, me_ref, old_ref, mem_ref, seg_ref, *rest):
+    q_refs, k_refs, v_refs, ks_refs, vs_refs, dt_refs, sums_refs = (
+        rest[i * heads : (i + 1) * heads] for i in range(7)
+    )
+    w_ref, table_ref, gain_ref, shift_ref, small_ref, part_ref, out_ref, total = rest[7 * heads :]
     stream = pl.program_id(0)
     parts, rows, wide = out_ref.shape
     cols = wide // 4
@@ -773,35 +777,35 @@
     def _():
         total[...] = jnp.zeros_like(total)
 
-    total[:cols, :] += mm(q_ref[...], seg_ref[...], TN)
-    for at, grad in ((cols, k_ref), (2 * cols, v_ref)):
-        low = 0
-        for normed in (old_ref, mem_ref, seg_ref):
-            high = low + normed.shape[0]
-            total[at : at + cols, :] += mm(grad[:, low:high], normed[...], NN)
-            low = high
-    three = jnp.concatenate([q_ref[...], ks_ref[...], vs_ref[...]], axis=1)
+    low = old_ref.shape[0]
+    high = low + mem_ref.shape[0]
+    pair = lambda first, last: [ref[:, first:last] for ref in (*k_refs, *v_refs)]
+    total[...] += mm(
+        jnp.concatenate([ref[...].T for ref in q_refs] + pair(high, high + seg_ref.shape[0]), axis=0),
+        seg_ref[...],
+        NN,
+    )
+    total[cols:, :] += mm(jnp.concatenate(pair(low, high), axis=0), mem_ref[...], NN)
+    total[cols:, :] += mm(jnp.concatenate(pair(0, low), axis=0), old_ref[...], NN)
+    three = jnp.concatenate([ref[...] for ref in (*q_refs, *ks_refs, *vs_refs)], axis=1)
     part = mm(three, w_ref[:, : 3 * cols], NT).astype(BF16)
     part_ref[...] = part.reshape(part_ref.shape)
 
     @pl.when(stream == pl.num_programs(0) - 1)
     def _():
-        heads = dt_ref.shape[0]
-        rel = jnp.concatenate(
-            [mm(dt_ref[head].astype(BF16), table_ref[...], NN) for head in range(heads)], axis=0
-        )
+        places = jnp.concatenate([ref[0].astype(BF16) for ref in dt_refs], axis=0)
+        rel = mm(places, table_ref[...], NN)
         line = lambda row: jnp.concatenate(
-            [sums_ref[head, row : row + 1, :] for head in range(heads)], axis=1
+            [ref[0, row : row + 1, :] for ref in sums_refs], axis=1
         )
         row_sums = jnp.concatenate([line(2), line(3), line(4)], axis=1)
+        pieces, rest = [], row_sums
+        for _ in range(3):
+            pieces.append(rest.astype(BF16))
+            rest = rest - pieces[-1].astype(F32)
+        pieces = jnp.concatenate(pieces + [jnp.zeros((13, 3 * cols), BF16)], axis=0)
+        shift_grad = jnp.sum(mm(pieces, w_ref[:, : 3 * cols], NT), axis=0, keepdims=True)
         weight = w_ref[:, : 3 * cols].astype(F32)
-        shift_grad = lax.dot_general(
-            jnp.broadcast_to(row_sums, (8, 3 * cols)),
-            weight,
-            (NT, ((), ())),
-            precision=lax.Precision.HIGHEST,
-            preferred_element_type=F32,
-        )[0:1]
         along = jnp.sum(weight.T * total[...], axis=0, keepdims=True)
         gain_grad = (along - shift_ref[...] * shift_grad) / gain_ref[...]
         for at in range(parts):
@@ -816,26 +820,26 @@
             out_ref[at, cols:, :] = (small_ref[at] + added).astype(BF16)
 
 
-def settle(me, normed, grads, columns, table, table_grad, sums, gain, shift, small, parts):
+def settle(me, normed, grads, columns, table, gain, shift, small, parts):
     group, queries, width = normed[2].shape
     cols = width // parts
     wide = 4 * cols
+    by_kind = list(zip(*grads))
     block = lambda array: pl.BlockSpec((None, *array.shape[1:]), lambda s, *_: (s, 0, 0))
     whole = lambda *shape: pl.BlockSpec(
         shape, lambda s, *_: (0,) * len(shape), pipeline_mode=pl.Buffered(1)
     )
     return pl.pallas_call(
-        settle_kernel,
+        functools.partial(settle_kernel, len(grads)),
         grid_spec=pltpu.PrefetchScalarGridSpec(
             num_scalar_prefetch=1,
             grid=(group,),
             in_specs=[block(rows) for rows in normed]
-            + [block(grad) for grad in grads]
+            + [block(each) for kind in by_kind[:5] for each in kind]
+            + [whole(*each.shape) for kind in by_kind[5:] for each in kind]
             + [
                 whole(*columns.shape),
                 whole(*table.shape),
-                whole(*table_grad.shape),
-                whole(*sums.shape),
                 whole(1, width),
                 whole(1, width),
                 whole(*small.shape),
@@ -855,7 +859,10 @@
         ),
         cost_estimate=cost(14),
         name="settle",
-    )(me.reshape(1), *normed, *grads, columns, table, table_grad, sums, gain, shift, small)
+    )(
+        me.reshape(1), *normed, *[each for kind in by_kind for each in kind], columns, table, gain, shift,
+        small,
+    )
 
 
 def standardise(rows):
@@ -1083,29 +1090,39 @@
     weights, inverse, mixed_heads, content_q, position_q, keys, values = kept[0]
     out_grad = mm(jnp.concatenate(attended), jnp.concatenate(branch_grad), TN)
     out_grad = out_grad.astype(BF16).reshape(parts, cols, width)
-    late_one, small, out_grad, late_two, head_grad = barrier(
-        (late_one, small, out_grad, late_two, head_grad[0])
+    late_one, small, out_grad, late_two, output, head_grad = barrier(
+        (late_one, small, out_grad, late_two, output, head_grad[0])
     )
     late_two = lax.psum_scatter(
         late_two.reshape(-1, width), "seq", scatter_dimension=0, tiled=True
     )
     late_one = exchange(late_one.reshape(layers, -1, width), "z")
-    query_grad, *key_grads, table_grad, sums = pull(
-        weights, inverse, mixed_heads, head_grad, content_q, position_q, keys, values, proj_rev, cuts
-    )
-    late_one, late_two, out_grad, query_grad = barrier((late_one, late_two, out_grad, query_grad))
+    grads = []
+    for head in range(cols // DH):
+        grads.append(
+            list(
+                pull(
+                    head, weights, inverse, mixed_heads, head_grad, content_q, position_q, keys,
+                    values, proj_rev, cuts,
+                )
+            )
+        )
+        if head == 0:
+            late_one, head_grad, grads[0][0] = barrier((late_one, head_grad, grads[0][0]))
+            late_one = collect(add_up(late_one), "z")
+    late_one, late_two, out_grad, grads[-1][0] = barrier(
+        (late_one, late_two, out_grad, grads[-1][0])
+    )
     late_two = exchange(late_two.reshape(layers, -1, width), "z")
-    out_sent = exchange(out_grad, "seq")
-    late_one = add_up(late_one)
+    out_sent = lax.all_to_all(out_grad, "seq", 0, 0, tiled=True)
     seg_part, square_grads = settle(
-        me, normed, (query_grad, *key_grads), columns, table_rev, table_grad, sums, gain_one,
-        shift_one, small, parts,
+        me, normed, grads, columns, table_rev, gain_one, shift_one, small, parts
     )
     late_two, out_sent, square_grads = barrier((late_two, out_sent, square_grads))
     summed = lax.all_to_all(square_grads, "seq", 0, 0, tiled=True)
-    late = collect(jnp.stack([late_one, add_up(late_two)]), "z")
-    out_sent = add_up(out_sent)
-    late, out_sent, summed, seg_part = barrier((late, out_sent, summed, seg_part))
+    late_two = collect(add_up(late_two), "z")
+    out_sent = jnp.sum(out_sent.astype(F32), axis=0).astype(BF16)
+    late_two, out_sent, summed, seg_part = barrier((late_two, out_sent, summed, seg_part))
     squares = parts * (cols + 16)
     summed = jnp.concatenate([summed.reshape(squares, wide), out_sent.reshape(-1, wide)], axis=0)
     summed, packed = barrier((summed, packed))
@@ -1120,8 +1137,8 @@
     rows_grad = standardise_back(unit_seg, rate_seg, seg_grad, gain_one)
     segment_grad = jnp.concatenate(middle_grad, axis=0) + by_stream(rows_grad)
 
-    late = late.reshape(layers, 2, -1, width).transpose(1, 0, 2, 3).reshape(4, unit_cols, width)
-    up_w, down_w = lay_out(core, late, swap(late), parts)
+    halves = [late_one.reshape(2, unit_cols, width), late_two.reshape(2, unit_cols, width)]
+    up_w, down_w = lay_out(core, halves, [swap(rows) for rows in halves], parts)
     down_w = down_w.reshape(4 * unit_cols, width)
     summed, output, segment_grad, new_compressed, up_w, down_w = barrier(
         (summed, output, segment_grad, new_compressed, up_w, down_w)

time: 593 us -> 559 us (0.943)
  waiting for transfers between devices: 196 us -> 158 us
    ppermute x3 -> x6, waiting for transfers between devices: 38.9 us -> 20.3 us  [collect(): lax.ppermute(block, name, [(i, i ^ apart) for i in range(count)])]
    reduce_scatter x1, waiting for transfers between devices: 13.8 us -> 0.01 us  [body(): lax.psum_scatter(late_two.reshape(-1, width), 'seq', scatter_dimension=0,...]
    all_to_all x1, waiting for transfers between devices: 15.6 us -> 7.08 us  [body(): head_grad.append(lax.all_to_all(three, 'seq', 0, 0, tiled=True))]
    ppermute x12 -> x9, waiting for transfers between devices: 40.6 us -> 48.8 us  [exchange(): lax.ppermute(block(me ^ apart), name, [(i, i ^ apart) for i in range(coun...]
    ppermute x12 -> x9, starting transfers between devices: 19 us -> 12.5 us  [exchange(): lax.ppermute(block(me ^ apart), name, [(i, i ^ apart) for i in range(coun...]
    psum x1, waiting for transfers between devices: 14.4 us -> 8.11 us  [body(): summed = lax.psum(summed, ('z', 'core'))]
    pallas_call x1 -> x2, Pallas kernels: 34.8 us -> 38.2 us  [pull(): pl.pallas_call(functools.partial(pull_kernel, cuts), grid_spec=grid_spec,...]
    unnamed x112 -> x106, local copies, waits for them, and re-layouts: 21.3 us -> 24.3 us
  transfers between devices with their start and end apart: 32 -> 34, of which waited for: 12 -> 13; matrix products, arithmetic and copies ran while one was open for 19% -> 20% of each run, Pallas kernels for 33% -> 36%
where the time goes in v1:
time: 559 us; the launch traced here: 551 us
  Pallas kernels  200 us (36%)
  waiting for transfers between devices  158 us (28%)
  local copies, waits for them, and re-layouts  62.2 us (11%)
  other arithmetic  60.6 us (11%)
  starting transfers between devices  50.6 us (9%)
  between operations  15.2 us (3%)
    pallas_call x2, Pallas kernels, forward_back(): pl.pallas_call(functools.partial(forward_back_kernel, last, parts, pair),...  57.9 us
    ppermute x9, waiting for transfers between devices, exchange(): lax.ppermute(block(me ^ apart), name, [(i, i ^ apart) for i in range(coun...  48.8 us
    all_to_all x1, waiting for transfers between devices, body(): got = lax.all_to_all(sent, 'seq', 0, 0, tiled=True)  48.1 us
    pallas_call x2, Pallas kernels, pull(): pl.pallas_call(functools.partial(pull_kernel, cuts), grid_spec=grid_spec,...  38.2 us
    pallas_call x1, Pallas kernels, attend(): pl.pallas_call(functools.partial(attend_kernel, cuts), grid_spec=grid_spe...  29.7 us
    unnamed x106, local copies, waits for them, and re-layouts  24.3 us
    ppermute x6, waiting for transfers between devices, collect(): lax.ppermute(block, name, [(i, i ^ apart) for i in range(count)])  20.3 us
    pallas_call x1, Pallas kernels, settle(): pl.pallas_call(functools.partial(settle_kernel, len(grads)), grid_spec=pl...  20.3 us
  transfers between devices with their start and end apart: 34, of which 13 were waited for; matrix products, arithmetic and copies ran while one was open for 20% of the time, Pallas kernels for 36%

profile of v1, /device:TPU:0, one launch (start us, length us, event | category | flops | bytes accessed | tf_op | source)
XLA Modules:
  0.0 551.4 jit_solution(4070361906297874124)
XLA Ops:
  26.3 3.8 pad_maximum_fusion
  30.1 7.5 %copy.106 = bf16[4,144,2816]{2,1,0:T(8,128)(2,1)} copy(bf16[4,144,2816]{1,2,0:T(8,128)(2,1)} %pad_maximum_fusion) | data formatting | bytes 6488064 | tf_op jit(solution)/shard_map/concatenate | solution.py:967
  37.6 5.3 all-to-all-start
  44.7 48.1 %all-to-all-done = bf16[4,144,2816]{2,1,0:T(8,128)(2,1)S(1)} async-done(((bf16[4,144,2816]{2,1,0:T(8,128)(2,1)}), bf16[4,144,2816]{2,1,0:T(8,128)(2,1)S(1)}, u32[]{:S(2)}, u32[]{:S(2)}) %all-to-all-start) | async-done | bytes 3244064 | tf_op jit(solution)/shard_map/all_to_all | solution.py:968
  98.2 4.5 reshape.349
  109.3 13.8 %fusion = (bf16[1792,512]{1,0:T(8,128)(2,1)S(1)}, bf16[1792,512]{1,0:T(8,128)(2,1)S(1)}) fusion(f32[512]{0:T(512)S(1)} %multiply_exponential_fusion, f32[1792]{0:T(1024)S(1)} %subtract_convert_fusion), kind=kLoop, calls=%fused_computation.6 | loop fusion | flops 2752512 | bytes 3679232 | tf_op jit(solution)/shard_map/convert.5
  137.5 16.5 %all-gather.7.cloned.1.call-done = bf16[12,448,1024]{2,1,0:T(8,128)(2,1)} async-done(((bf16[3,448,1024]{2,1,0:T(8,128)(2,1)}), bf16[12,448,1024]{2,1,0:T(8,128)(2,1)}) %all-gather.7.cloned.1.call-update) | async-done | bytes 11010064 | tf_op jit(solution)/shard_map/all_gather | solution.py:974
  156.4 18.3 %project.1 = (bf16[3,256,1024]{2,1,0:T(8,128)(2,1)}, bf16[3,768,1024]{2,1,0:T(8,128)(2,1)}, bf16[3,768,1024]{2,1,0:T(8,128)(2,1)}, f32[4,3,192,256]{3,2,1,0:T(8,...) custom-call(bf16[4,3,448,1024]{3,2,1,0:T(8,128)(2,1)} %bitcast.165, f32[1,1024]{1,0:T(1,128)} %bitcast.217, ...), custom_call_target="tpu_custom_call" | custom-call | flops 195500000 | tf_op jit(solution)/shard_map/project/pallas_call | solution.py:379
  175.8 29.7 %attend.1 = (bf16[3,2,768,1792]{3,2,1,0:T(8,128)(2,1)}, f32[3,2,768,128]{3,2,1,0:T(8,128)}, bf16[4,3,192,256]{3,2,1,0:T(8,128)(2,1)}, bf16[4,3,192,256]{3,2,1,0:T(8,128)(2,1)}, bf16[4,3,192,256]{3,2,1,0:T(8,128)(2,1)}) custom-call(f32[4,3,192,256]{3,2,1,0:T(8,128)} %get-tuple-element.123.q_ref, f32[1,256]{1,0:T(1,128)} %bitcast.243, f32[1,256]{1,0:T(1,128)} %bitcast.244, ...), custom_call_target="tpu_custom_call" | custom-call | flops 460000000 | tf_op jit(solution)/shard_map/attend/pallas_call | solution.py:189
  205.5 3.5 all-to-all-start.1
  211.6 11.7 %compress.1 = bf16[4,3,64,256]{3,2,1,0:T(8,128)(2,1)} custom-call(bf16[4,3,448,1024]{3,2,1,0:T(8,128)(2,1)} %bitcast.166, bf16[1024,768]{1,0:T(8,128)(2,1)} %slice.159.w_ref, f32[1,256]{1,0:T(1,128)} %bitcast.234), custom_call_target="tpu_custom_call" | custom-call | flops 74750000 | tf_op jit(solution)/shard_map/compress/pallas_call | solution.py:675
  223.3 4.1 all-to-all-done.1.a_ref
  228.5 5.9 %leave.1 = (bf16[3,192,1024]{2,1,0:T(8,128)(2,1)}, f32[3,192,1024]{2,1,0:T(8,128)}, bf16[3,192,1024]{2,1,0:T(8,128)(2,1)}) custom-call(bf16[4,3,192,256]{3,2,1,0:T(8,128)(2,1)} %copy-done.8, bf16[3,192,1024]{2,1,0:T(8,128)(2,1)} %s_ref.1, bf16[1024,1024]{1,0:T(8,128)(2,1)} %get-tuple-element.132.w_ref, f32[1,1024]{1,0:T(1,128)} %bitcast.227, ...), custom_call_target="tpu_custom_call" | custom-call | flops 69000000 | tf_op jit(solution)/shard_map/leave/pallas_call | solution.py:568
  240.3 28.2 %forward_back.2 = (f32[1152,1024]{1,0:T(8,128)}, f32[1152,1024]{1,0:T(8,128)}, bf16[4,512,1024]{2,1,0:T(8,128)(2,1)}, f32[1,1024]{1,0:T(1,128)}) custom-call(bf16[1152,1024]{1,0:T(8,128)(2,1)} %pad_maximum_fusion.5.n_ref, bf16[1152,1024]{1,0:T(8,128)(2,1)} %pad_maximum_fusion.4.c_ref, bf16[4,512,1024]{2,1,0:T(8,128)(2,1)} %bitcast.159, ...), custom_call_target="tpu_custom_call" | custom-call | flops 333500000 | tf_op jit(solution)/shard_map/forward_back/pallas_call | solution.py:511
  269.1 29.7 %forward_back.3 = (f32[576,1024]{1,0:T(8,128)}, bf16[576,1024]{1,0:T(8,128)(2,1)}, f32[576,1024]{1,0:T(8,128)}, bf16[576,1024]{1,0:T(8,128)(2,1)}, bf16[4,512,1024]{2,1,0:T(8,128)(2,1)}, /*index=5*/f32[1,1024]{1,0:T(1,128)}) custom-call(bf16[1152,1024]{1,0:T(8,128)(2,1)} %pad_maximum_fusion.5.n_ref, bf16[1152,1024]{1,0:T(8,128)(2,1)} %pad_maximum_fusion.4.c_ref, ...), custom_call_target="tpu_custom_call" | custom-call | flops 333500000 | tf_op jit(solution)/shard_map/forward_back/pallas_call | solution.py:511
  303.3 8.9 %enter.1 = (f32[3,192,1024]{2,1,0:T(8,128)}, bf16[3,192,1024]{2,1,0:T(8,128)(2,1)}, bf16[4,3,192,256]{3,2,1,0:T(8,128)(2,1)}, f32[8,1024]{1,0:T(8,128)}) custom-call(f32[3,192,1024]{2,1,0:T(8,128)} %get-tuple-element.137.m_ref, f32[3,192,1024]{2,1,0:T(8,128)} %bitcast.185, bf16[3,192,1024]{2,1,0:T(8,128)(2,1)} %bitcast.195, bf16[3,192,1024]{2,1,0:T(8,128)(2,1)} %c_ref.1, ...), custom_call_target="tpu_custom_call" | custom-call | flops 80500000 | tf_op jit(solution)/shard_map/enter/pallas_call | solution.py:624
  314.6 3.5 all-to-all-start.2
  319.7 3.7 fusion.11
  326.6 7.1 %all-to-all-done.2.g_ref = bf16[4,3,192,256]{3,2,1,0:T(8,128)(2,1)S(1)} async-done(((bf16[4,3,192,256]{3,2,1,0:T(8,128)(2,1)}), bf16[4,3,192,256]{3,2,1,0:T(8,128)(2,1)S(1)}, u32[]{:S(2)}, u32[]{:S(2)}) %all-to-all-start.2) | async-done | bytes 1179680 | tf_op jit(solution)/shard_map/all_to_all | solution.py:1066
  339.9 19.3 %pull.2 = (bf16[3,768,128]{2,1,0:T(8,128)(2,1)}, bf16[3,128,1792]{2,1,0:T(8,128)(2,1)}, bf16[3,128,1792]{2,1,0:T(8,128)(2,1)}, bf16[3,768,128]{2,1,0:T(8,128)(2,...) custom-call(bf16[3,2,768,1792]{3,2,1,0:T(8,128)(2,1)} %get-tuple-element.155.e_ref, ...), custom_call_target="tpu_custom_call" | custom-call | flops 448500000 | tf_op jit(solution)/shard_map/pull/pallas_call | solution.py:332
  359.5 3.7 collective-permute-start.10
  364.4 18.8 %pull.3 = (bf16[3,768,128]{2,1,0:T(8,128)(2,1)}, bf16[3,128,1792]{2,1,0:T(8,128)(2,1)}, bf16[3,128,1792]{2,1,0:T(8,128)(2,1)}, bf16[3,768,128]{2,1,0:T(8,128)(2,...) custom-call(bf16[3,2,768,1792]{3,2,1,0:T(8,128)(2,1)} %get-tuple-element.155.e_ref, ...), custom_call_target="tpu_custom_call" | custom-call | flops 448500000 | tf_op jit(solution)/shard_map/pull/pallas_call | solution.py:332
  386.7 4.7 all-to-all-start.3
  396.0 20.3 %settle.1 = (bf16[4,3,192,1024]{3,2,1,0:T(8,128)(2,1)}, bf16[4,272,1024]{2,1,0:T(8,128)(2,1)}) custom-call(s32[1]{0:T(128)} %bitcast.47.me_ref, bf16[3,256,1024]{2,1,0:T(8,128)(2,1)} %get-tuple-element.170.old_ref, bf16[3,768,1024]{2,1,0:T(8,128)(2,1)} %get-tuple-element.171.mem_ref, bf16[3,768,1024]{2,1,0:T(8,128)(2,1)} %get-tuple-element.172.seg_ref, ...), custom_call_target="tpu_custom_call" | custom-call | flops 161000000 | tf_op jit(solution)/shard_map/settle/pallas_call | solution.py:832
  417.0 4.2 all-to-all-start.4
  429.7 3.8 collective-permute-done.16
  433.5 14.4 %collective-permute-done.15 = bf16[128,1024]{1,0:T(8,128)(2,1)S(1)} collective-permute-done((bf16[128,1024]{1,0:T(8,128)(2,1)S(1)}, bf16[128,1024]{1,0:T(8,128)(2,1)S(1)}, u32[]{:S(2)}, u32[]{:S(2)}) %collective-permute-start.15) | collective-permute-done | bytes 262176 | tf_op jit(solution)/shard_map/ppermute | solution.py:915
  449.2 5.1 all-to-all-start.5
  463.2 48.5 %collective-permute-done.19 = bf16[3,64,256]{2,1,0:T(8,128)(2,1)S(1)} collective-permute-done((bf16[3,64,256]{2,1,0:T(8,128)(2,1)S(1)}, bf16[3,64,256]{2,1,0:T(8,128)(2,1)S(1)}, u32[]{:S(2)}, u32[]{:S(2)}) %collective-permute-start.19) | collective-permute-done | bytes 98336 | tf_op jit(solution)/shard_map/ppermute | solution.py:904
  512.8 5.9 %lay_out.1 = (f32[256,4096]{1,0:T(8,128)}, f32[4,256,1024]{2,1,0:T(8,128)}) custom-call(s32[1]{0:T(128)} %bitcast.63.core_ref, bf16[2,256,1024]{2,1,0:T(8,128)(2,1)} %bitcast.179, bf16[2,256,1024]{2,1,0:T(8,128)(2,1)} %bitcast.181, bf16[2,256,1024]{2,1,0:T(8,128)(2,1)} %collective-permute-done.20.c_ref, bf16[2,256,1024]{2,1,0:T(8,128)(2,1)} %collective-permute-done.21.d_ref), custom_call_target="tpu_custom_call" | custom-call | flops 46000000 | tf_op jit(solution)/shard_map/lay_out/pallas_call | solution.py:717
  518.7 3.8 convert_reduce_fusion
  526.4 8.1 %all-reduce.7.cloned.1.call-done = bf16[1344,1024]{1,0:T(8,128)(2,1)} async-done(((bf16[1344,1024]{1,0:T(8,128)(2,1)}), bf16[1344,1024]{1,0:T(8,128)(2,1)}) %all-reduce.7.cloned.1.call-update) | async-done | bytes 2752528 | tf_op jit(solution)/shard_map/psum | solution.py:1129
  (256 shorter events, 121.8 us)
Async XLA Ops:
  7.2 146.8 %all-gather.7.cloned.1.call-start = ((), (), s32[]{:S(2)}) async-start(), calls=%async_computation.11 | async-start | bytes 13762560 | tf_op jit(solution)/shard_map/all_gather | solution.py:974
  37.6 55.2 %all-to-all-start = ((bf16[4,144,2816]{2,1,0:T(8,128)(2,1)}), bf16[4,144,2816]{2,1,0:T(8,128)(2,1)S(1)}, u32[]{:S(2)}, u32[]{:S(2)}) async-start(bf16[4,144,2816]{2,1,0:T(8,128)(2,1)} %copy.106), calls=%async_computation | async-start | bytes 6488064 | tf_op jit(solution)/shard_map/all_to_all | solution.py:968
  42.8 197.5 %all-gather.9.cloned.1.call-start = ((), (), s32[]{:S(2)}) async-start(), calls=%async_computation.12 | async-start | bytes 5242880 | tf_op jit(solution)/shard_map/all_gather | solution.py:1019
  43.1 82.3 %collective-permute-start.1 = (bf16[576,1024]{1,0:T(8,128)(2,1)}, bf16[576,1024]{1,0:T(8,128)(2,1)}, u32[]{:S(2)}, u32[]{:S(2)}) collective-permute-start(bf16[576,1024]{1,0:T(8,128)(2,1)} %bitcast.176), channel_id=1, source_target_pairs={{0,4},{4,0},{1,5},{5,1},{2,6},{6,2},{3,7},{7,3},{8,12},{12,8},{9,1... | collective-permute-start | bytes 3538952 | tf_op jit(solution)/shard_map/ppermute | solution.py:896
  94.9 33.5 %collective-permute-start = (bf16[4,128,2816]{2,1,0:T(8,128)(2,1)}, bf16[4,128,2816]{2,1,0:T(8,128)(2,1)}, u32[]{:S(2)}, u32[]{:S(2)}) collective-permute-start(bf16[4,128,2816]{2,1,0:T(8,128)(2,1)} %slice.155), channel_id=1, source_target_pairs={{0,4},{4,0},{1,5},{5,1},{2,6},{6,2},{3,7},{7,3},{8,12},{12,8},{9,1... | collective-permute-start | bytes 8650760 | tf_op jit(solution)/shard_map/ppermute | solution.py:896
  154.0 115.1 %all-gather.11.cloned.1.call-start = ((), (), s32[]{:S(2)}) async-start(), calls=%async_computation.13 | async-start | bytes 5242880 | tf_op jit(solution)/shard_map/all_gather | solution.py:1022
  205.5 22.0 %all-to-all-start.1 = ((bf16[4,3,192,256]{3,2,1,0:T(8,128)(2,1)}), bf16[4,3,192,256]{3,2,1,0:T(8,128)(2,1)S(1)}, u32[]{:S(2)}, u32[]{:S(2)}) async-start(bf16[4,3,192,256]{3,2,1,0:T(8,128)(2,1)} %get-tuple-element.128.o_ref), calls=%async_computation.1 | async-start | bytes 2359296 | tf_op jit(solution)/shard_map/all_to_all | solution.py:1034
  209.0 124.7 %reduce-scatter.3.cloned.1.call-start = ((), (), s32[]{:S(2)}) async-start(), calls=%async_computation.8 | async-start | bytes 5242880 | tf_op jit(solution)/shard_map/reduce_scatter | solution.py:1050
  299.0 20.6 %collective-permute-start.4 = (bf16[576,1024]{1,0:T(8,128)(2,1)}, bf16[576,1024]{1,0:T(8,128)(2,1)}, u32[]{:S(2)}, u32[]{:S(2)}) collective-permute-start(bf16[576,1024]{1,0:T(8,128)(2,1)} %get-tuple-element.150), channel_id=1, source_target_pairs={{0,4},{4,0},{1,5},{5,1},{2,6},{6,2},{3,7},{7,3},{8,12},{12,8},{9,1... | collective-permute-start | bytes 3538952 | tf_op jit(solution)/shard_map/ppermute | solution.py:896
  314.6 19.1 %all-to-all-start.2 = ((bf16[4,3,192,256]{3,2,1,0:T(8,128)(2,1)}), bf16[4,3,192,256]{3,2,1,0:T(8,128)(2,1)S(1)}, u32[]{:S(2)}, u32[]{:S(2)}) async-start(bf16[4,3,192,256]{3,2,1,0:T(8,128)(2,1)} %get-tuple-element.152), calls=%async_computation.3 | async-start | bytes 2359296 | tf_op jit(solution)/shard_map/all_to_all | solution.py:1066
  318.1 68.5 %reduce-scatter.5.cloned.1.call-start = ((), (), s32[]{:S(2)}) async-start(), calls=%async_computation.9 | async-start | bytes 5242880 | tf_op jit(solution)/shard_map/reduce_scatter | solution.py:1096
  335.5 23.8 %collective-permute-start.5 = (bf16[128,1024]{1,0:T(8,128)(2,1)S(1)}, bf16[128,1024]{1,0:T(8,128)(2,1)S(1)}, u32[]{:S(2)}, u32[]{:S(2)}) collective-permute-start(bf16[128,1024]{1,0:T(8,128)(2,1)S(1)} %get-tuple-element.245), channel_id=1, source_target_pairs={{0,8},{8,0},{16,24},{24,16},{1,9},{9,1},{17,25},{25,17},{2,10},{10... | collective-permute-start | bytes 786440 | tf_op jit(solution)/shard_map/ppermute | solution.py:904
  337.1 22.2 %collective-permute-start.6 = (bf16[128,1024]{1,0:T(8,128)(2,1)S(1)}, bf16[128,1024]{1,0:T(8,128)(2,1)S(1)}, u32[]{:S(2)}, u32[]{:S(2)}) collective-permute-start(bf16[128,1024]{1,0:T(8,128)(2,1)S(1)} %get-tuple-element.244), channel_id=1, source_target_pairs={{0,16},{8,24},{16,0},{24,8},{1,17},{9,25},{17,1},{25,9},{2,18},{10... | collective-permute-start | bytes 786440 | tf_op jit(solution)/shard_map/ppermute | solution.py:904
  339.5 19.8 %collective-permute-start.7 = (bf16[128,1024]{1,0:T(8,128)(2,1)S(1)}, bf16[128,1024]{1,0:T(8,128)(2,1)S(1)}, u32[]{:S(2)}, u32[]{:S(2)}) collective-permute-start(bf16[128,1024]{1,0:T(8,128)(2,1)S(1)} %get-tuple-element.243), channel_id=1, source_target_pairs={{0,24},{8,16},{16,8},{24,0},{1,25},{9,17},{17,9},{25,1},{2,26},{10... | collective-permute-start | bytes 786440 | tf_op jit(solution)/shard_map/ppermute | solution.py:904
  359.5 23.8 %collective-permute-start.10 = (bf16[128,1024]{1,0:T(8,128)(2,1)S(1)}, bf16[128,1024]{1,0:T(8,128)(2,1)S(1)}, u32[]{:S(2)}, u32[]{:S(2)}) collective-permute-start(bf16[128,1024]{1,0:T(8,128)(2,1)S(1)} %add_convert_fusion.1), channel_id=1, source_target_pairs={{0,24},{8,16},{16,8},{24,0},{1,25},{9,17},{17,9},{25,1},{2,26},{10... | collective-permute-start | bytes 786440 | tf_op jit(solution)/shard_map/ppermute | solution.py:915
  363.1 22.2 %collective-permute-start.9 = (bf16[128,1024]{1,0:T(8,128)(2,1)S(1)}, bf16[128,1024]{1,0:T(8,128)(2,1)S(1)}, u32[]{:S(2)}, u32[]{:S(2)}) collective-permute-start(bf16[128,1024]{1,0:T(8,128)(2,1)S(1)} %add_convert_fusion.1), channel_id=1, source_target_pairs={{0,16},{8,24},{16,0},{24,8},{1,17},{9,25},{17,1},{25,9},{2,18},{10... | collective-permute-start | bytes 786440 | tf_op jit(solution)/shard_map/ppermute | solution.py:915
  364.4 21.0 %collective-permute-start.8 = (bf16[128,1024]{1,0:T(8,128)(2,1)S(1)}, bf16[128,1024]{1,0:T(8,128)(2,1)S(1)}, u32[]{:S(2)}, u32[]{:S(2)}) collective-permute-start(bf16[128,1024]{1,0:T(8,128)(2,1)S(1)} %add_convert_fusion.1), channel_id=1, source_target_pairs={{0,8},{8,0},{16,24},{24,16},{1,9},{9,1},{17,25},{25,17},{2,10},{10... | collective-permute-start | bytes 786440 | tf_op jit(solution)/shard_map/ppermute | solution.py:915
  386.7 30.1 %all-to-all-start.3 = ((bf16[4,256,1024]{2,1,0:T(8,128)(2,1)}), bf16[4,256,1024]{2,1,0:T(8,128)(2,1)}, u32[]{:S(2)}, u32[]{:S(2)}) async-start(bf16[4,256,1024]{2,1,0:T(8,128)(2,1)} %bitcast.29), calls=%async_computation.5 | async-start | bytes 4194304 | tf_op jit(solution)/shard_map/all_to_all | solution.py:1117
  391.5 24.8 %collective-permute-start.11 = (bf16[128,1024]{1,0:T(8,128)(2,1)S(1)}, bf16[128,1024]{1,0:T(8,128)(2,1)S(1)}, u32[]{:S(2)}, u32[]{:S(2)}) collective-permute-start(bf16[128,1024]{1,0:T(8,128)(2,1)S(1)} %get-tuple-element.237), channel_id=1, source_target_pairs={{0,8},{8,0},{16,24},{24,16},{1,9},{9,1},{17,25},{25,17},{2,10},{10... | collective-permute-start | bytes 786440 | tf_op jit(solution)/shard_map/ppermute | solution.py:904
  393.0 23.3 %collective-permute-start.12 = (bf16[128,1024]{1,0:T(8,128)(2,1)S(1)}, bf16[128,1024]{1,0:T(8,128)(2,1)S(1)}, u32[]{:S(2)}, u32[]{:S(2)}) collective-permute-start(bf16[128,1024]{1,0:T(8,128)(2,1)S(1)} %get-tuple-element.236), channel_id=1, source_target_pairs={{0,16},{8,24},{16,0},{24,8},{1,17},{9,25},{17,1},{25,9},{2,18},{10... | collective-permute-start | bytes 786440 | tf_op jit(solution)/shard_map/ppermute | solution.py:904
  395.5 20.9 %collective-permute-start.13 = (bf16[128,1024]{1,0:T(8,128)(2,1)S(1)}, bf16[128,1024]{1,0:T(8,128)(2,1)S(1)}, u32[]{:S(2)}, u32[]{:S(2)}) collective-permute-start(bf16[128,1024]{1,0:T(8,128)(2,1)S(1)} %get-tuple-element.235), channel_id=1, source_target_pairs={{0,24},{8,16},{16,8},{24,0},{1,25},{9,17},{17,9},{25,1},{2,26},{10... | collective-permute-start | bytes 786440 | tf_op jit(solution)/shard_map/ppermute | solution.py:904
  417.0 32.2 %all-to-all-start.4 = ((bf16[4,272,1024]{2,1,0:T(8,128)(2,1)}), bf16[4,272,1024]{2,1,0:T(8,128)(2,1)S(1)}, u32[]{:S(2)}, u32[]{:S(2)}) async-start(bf16[4,272,1024]{2,1,0:T(8,128)(2,1)} %get-tuple-element.195), calls=%async_computation.6 | async-start | bytes 4456448 | tf_op jit(solution)/shard_map/all_to_all | solution.py:1122
  422.3 11.2 %collective-permute-start.16 = (bf16[128,1024]{1,0:T(8,128)(2,1)S(1)}, bf16[128,1024]{1,0:T(8,128)(2,1)S(1)}, u32[]{:S(2)}, u32[]{:S(2)}) collective-permute-start(bf16[128,1024]{1,0:T(8,128)(2,1)S(1)} %add_convert_fusion), channel_id=1, source_target_pairs={{0,24},{8,16},{16,8},{24,0},{1,25},{9,17},{17,9},{25,1},{2,26},{10... | collective-permute-start | bytes 786440 | tf_op jit(solution)/shard_map/ppermute | solution.py:915
  425.7 22.2 %collective-permute-start.15 = (bf16[128,1024]{1,0:T(8,128)(2,1)S(1)}, bf16[128,1024]{1,0:T(8,128)(2,1)S(1)}, u32[]{:S(2)}, u32[]{:S(2)}) collective-permute-start(bf16[128,1024]{1,0:T(8,128)(2,1)S(1)} %add_convert_fusion), channel_id=1, source_target_pairs={{0,16},{8,24},{16,0},{24,8},{1,17},{9,25},{17,1},{25,9},{2,18},{10... | collective-permute-start | bytes 786440 | tf_op jit(solution)/shard_map/ppermute | solution.py:915
  426.4 21.5 %collective-permute-start.14 = (bf16[128,1024]{1,0:T(8,128)(2,1)S(1)}, bf16[128,1024]{1,0:T(8,128)(2,1)S(1)}, u32[]{:S(2)}, u32[]{:S(2)}) collective-permute-start(bf16[128,1024]{1,0:T(8,128)(2,1)S(1)} %add_convert_fusion), channel_id=1, source_target_pairs={{0,8},{8,0},{16,24},{24,16},{1,9},{9,1},{17,25},{25,17},{2,10},{10... | collective-permute-start | bytes 786440 | tf_op jit(solution)/shard_map/ppermute | solution.py:915
  449.2 69.5 %all-to-all-start.5 = ((bf16[4,3,192,1024]{3,2,1,0:T(8,128)(2,1)}), bf16[4,3,192,1024]{3,2,1,0:T(8,128)(2,1)}, u32[]{:S(2)}, u32[]{:S(2)}) async-start(bf16[4,3,192,1024]{3,2,1,0:T(8,128)(2,1)} %get-tuple-element.203), calls=%async_computation.7 | async-start | bytes 9437184 | tf_op jit(solution)/shard_map/all_to_all | solution.py:1134
  454.3 80.2 %all-reduce.7.cloned.1.call-start = ((), (), s32[]{:S(2)}) async-start(), calls=%async_computation.10 | async-start | bytes 5505024 | tf_op jit(solution)/shard_map/psum | solution.py:1129
  454.6 58.2 %collective-permute-start.20 = (bf16[2,256,1024]{2,1,0:T(8,128)(2,1)}, bf16[2,256,1024]{2,1,0:T(8,128)(2,1)}, u32[]{:S(2)}, u32[]{:S(2)}) collective-permute-start(bf16[2,256,1024]{2,1,0:T(8,128)(2,1)} %bitcast.178), channel_id=1, source_target_pairs={{0,4},{4,0},{1,5},{5,1},{2,6},{6,2},{3,7},{7,3},{8,12},{12,8},{9,1... | collective-permute-start | bytes 3145736 | tf_op jit(solution)/shard_map/ppermute | solution.py:896
  454.7 58.1 %collective-permute-start.21 = (bf16[2,256,1024]{2,1,0:T(8,128)(2,1)}, bf16[2,256,1024]{2,1,0:T(8,128)(2,1)}, u32[]{:S(2)}, u32[]{:S(2)}) collective-permute-start(bf16[2,256,1024]{2,1,0:T(8,128)(2,1)} %bitcast.180), channel_id=1, source_target_pairs={{0,4},{4,0},{1,5},{5,1},{2,6},{6,2},{3,7},{7,3},{8,12},{12,8},{9,1... | collective-permute-start | bytes 3145736 | tf_op jit(solution)/shard_map/ppermute | solution.py:896
  459.6 52.1 %collective-permute-start.19 = (bf16[3,64,256]{2,1,0:T(8,128)(2,1)S(1)}, bf16[3,64,256]{2,1,0:T(8,128)(2,1)S(1)}, u32[]{:S(2)}, u32[]{:S(2)}) collective-permute-start(bf16[3,64,256]{2,1,0:T(8,128)(2,1)S(1)} %get-tuple-element.254), channel_id=1, source_target_pairs={{0,3},{1,2},{2,1},{3,0},{4,7},{5,6},{6,5},{7,4},{8,11},{9,10},{10,... | collective-permute-start | bytes 294920 | tf_op jit(solution)/shard_map/ppermute | solution.py:904
  462.5 49.5 %collective-permute-start.18 = (bf16[3,64,256]{2,1,0:T(8,128)(2,1)S(1)}, bf16[3,64,256]{2,1,0:T(8,128)(2,1)S(1)}, u32[]{:S(2)}, u32[]{:S(2)}) collective-permute-start(bf16[3,64,256]{2,1,0:T(8,128)(2,1)S(1)} %get-tuple-element.255), channel_id=1, source_target_pairs={{0,2},{1,3},{2,0},{3,1},{4,6},{5,7},{6,4},{7,5},{8,10},{9,11},{10,... | collective-permute-start | bytes 294920 | tf_op jit(solution)/shard_map/ppermute | solution.py:904
  463.0 48.9 %collective-permute-start.17 = (bf16[3,64,256]{2,1,0:T(8,128)(2,1)S(1)}, bf16[3,64,256]{2,1,0:T(8,128)(2,1)S(1)}, u32[]{:S(2)}, u32[]{:S(2)}) collective-permute-start(bf16[3,64,256]{2,1,0:T(8,128)(2,1)S(1)} %get-tuple-element.256), channel_id=1, source_target_pairs={{0,1},{1,0},{2,3},{3,2},{4,5},{5,4},{6,7},{7,6},{8,9},{9,8},{10,11... | collective-permute-start | bytes 294920 | tf_op jit(solution)/shard_map/ppermute | solution.py:904
  (38 other events, 188.1 us)
Sparse Core Ops, SparseCore 0:
  12.8 141.1 all-gather.6
  156.4 52.6 all-gather.8
  211.6 54.5 all-gather.10
  269.6 52.6 reduce-scatter.2
  333.9 52.7 reduce-scatter.4
  463.3 71.1 all-reduce.6

commit v2 on v1

--- a/solution.py
+++ b/solution.py
@@ -455,18 +455,15 @@
             part_ref[...] = jnp.zeros_like(part_ref)
             grad_ref[...] = jnp.zeros_like(grad_ref)
 
-    chunk = 288 if rows % 288 == 0 else rows
-    for base in range(0, rows, chunk):
-        at = slice(base, base + chunk)
-        pre[at, :] = mm(n_ref[at, :], up_weight, NN)
-        slope[at, :] = mm(c_ref[at, :], down_weight, NT)
-        for low in range(base, base + chunk, 16):
-            some = slice(low, low + 16)
-            value, change = gelu_both(pre[some, :] + shift_ref[...])
-            hidden[some, :] = value.astype(BF16)
-            act[some, :] = (change * slope[some, :]).astype(BF16)
-        part_ref[at, :] += mm(hidden[at, :], down_weight, NN)
-        grad_ref[at, :] += mm(act[at, :], up_weight, NT)
+    pre[...] = mm(n_ref[...], up_weight, NN)
+    slope[...] = mm(c_ref[...], down_weight, NT)
+    for low in range(0, rows, 16):
+        some = slice(low, low + 16)
+        value, change = gelu_both(pre[some, :] + shift_ref[...])
+        hidden[some, :] = value.astype(BF16)
+        act[some, :] = (change * slope[some, :]).astype(BF16)
+    part_ref[...] += mm(hidden[...], down_weight, NN)
+    grad_ref[...] += mm(act[...], up_weight, NT)
     sums_ref[...] = jnp.sum(act[...].astype(F32), axis=0, keepdims=True)
 
     @pl.when(tile >= 2)
@@ -595,7 +592,7 @@
 
     parts = a_ref.shape[0]
     rows, width = m_ref.shape
-    step = 16
+    step = 32
     total = [jnp.zeros((1, width), F32) for _ in range(4)]
     for low in range(0, rows, step):
         at = slice(low, low + step)
@@ -959,30 +956,28 @@
     )
     vectors = jnp.pad(vectors.reshape(2, wide), ((0, 14), (0, 0)))
     half = cols // 2
-    sent = by_columns(jnp.concatenate([jnp.stack([w_query, w_key, w_value, w_rel]), conv_weight]))
-    sent = lax.dynamic_slice_in_dim(sent, core * half, half, 1)
-    out_half = lax.dynamic_slice_in_dim(w_out, core * half, half, 0)
-    sent = jnp.concatenate([sent, jnp.broadcast_to(out_half, (parts, half, width))], axis=2)
-    vectors = jnp.pad(vectors, ((0, 0), (0, 3 * cols + width)))
+
+    def my_half(blocks):
+        return lax.dynamic_slice_in_dim(blocks, core * half, half, 1)
+
+    def join(mine):
+        far = swap(mine)
+        both = [jnp.where(core == 0, mine, far), jnp.where(core == 0, far, mine)]
+        return jnp.stack(both, axis=1).reshape(width, mine.shape[2])
+
+    sent = my_half(by_columns(jnp.stack([w_query, w_key, w_value, w_rel])))
     sent = jnp.concatenate([sent, jnp.broadcast_to(vectors, (parts, *vectors.shape))], axis=1)
     got = lax.all_to_all(sent, "seq", 0, 0, tiled=True)
+    out_sent = jnp.broadcast_to(lax.dynamic_slice_in_dim(w_out, core * half, half, 0), (parts, half, width))
+    others = jnp.concatenate([my_half(by_columns(conv_weight)), out_sent], axis=2)
     spans = [(0, group)]
     local = [
         jnp.concatenate([compressed[low:high], memory[low:high], segment[low:high]], axis=1)
         for low, high in spans
     ]
     rows_all = [lax.all_gather(local[0], "seq")]
-    mine = got[:, :half]
-    far = swap(mine)
-    columns = jnp.stack(
-        [jnp.where(core == 0, mine, far), jnp.where(core == 0, far, mine)], axis=1
-    ).reshape(width, 7 * cols + width)
-    columns, conv_columns, out_full = (
-        columns[:, :wide],
-        columns[:, wide : 7 * cols],
-        columns[:, 7 * cols :],
-    )
-    vectors = got[:, half : half + 2, :wide].reshape(parts, 2 * wide).astype(F32)
+    columns = join(got[:, :half])
+    vectors = got[:, half : half + 2].reshape(parts, 2 * wide).astype(F32)
     gain_one, shift_one, out_shift, gain_two, shift_two, down_shift = (
         vectors[:, cols * i : cols * (i + 1)].reshape(1, width) for i in range(6)
     )
@@ -1007,9 +1002,10 @@
     shade = jnp.where((start == 0) & (reset[:, None] == 0), 0.0, MASKED)
     info = jnp.stack([start.astype(F32), shade], axis=2)
     info = jnp.pad(info, ((0, 0), (0, 0), (0, LANES - 2)))
-    rows_all[0], proj_rev, info, cot_both, table_rev, columns, conv_columns, out_full, *local = barrier(
-        (rows_all[0], proj_rev, info, cot_both, table_rev, columns, conv_columns, out_full, *local)
-    )
+    rows_all[0], proj_rev, info, cot_both, table_rev, columns, others, *local = barrier(
+        (rows_all[0], proj_rev, info, cot_both, table_rev, columns, others, *local)
+    )
+    others = lax.all_to_all(others, "seq", 0, 0, tiled=True)
     rows_all = [rows_all[0]] + [lax.all_gather(rows, "seq") for rows in local[1:]]
 
     kept, heads = [], []
@@ -1018,7 +1014,7 @@
             rows_all[batch], first, *heads = barrier((rows_all[batch], first, *heads))
             first = lax.all_gather(first, "seq")
         *normed, query, keys, values = project(rows_all[batch], gain_one, shift_one, columns, cuts)
-        second, query = barrier((second, query))
+        second, others, query = barrier((second, others, query))
         second = lax.all_gather(second, "seq")
         weights, inverse, mixed_heads, content_q, position_q = attend(
             query,
@@ -1033,7 +1029,9 @@
         kept.append((weights, inverse, mixed_heads, content_q, position_q, keys, values))
         heads.append(lax.all_to_all(mixed_heads, "seq", 0, 0, tiled=True))
 
-    mixed_heads, conv_columns = barrier((mixed_heads, conv_columns))
+    mixed_heads, others = barrier((mixed_heads, others))
+    others = join(others)
+    conv_columns, out_full = others[:, : 3 * cols], others[:, 3 * cols :]
     packed = compress(
         rows_all[0], conv_columns, conv_bias.astype(F32).reshape(1, cols), old, mem // 3
     )
@@ -1118,15 +1116,13 @@
     seg_part, square_grads = settle(
         me, normed, grads, columns, table_rev, gain_one, shift_one, small, parts
     )
-    late_two, out_sent, square_grads = barrier((late_two, out_sent, square_grads))
-    summed = lax.all_to_all(square_grads, "seq", 0, 0, tiled=True)
+    summed = lax.psum(square_grads, ("z", "core"))
+    late_two, out_sent, seg_part = barrier((late_two, out_sent, seg_part))
     late_two = collect(add_up(late_two), "z")
     out_sent = jnp.sum(out_sent.astype(F32), axis=0).astype(BF16)
-    late_two, out_sent, summed, seg_part = barrier((late_two, out_sent, summed, seg_part))
-    squares = parts * (cols + 16)
-    summed = jnp.concatenate([summed.reshape(squares, wide), out_sent.reshape(-1, wide)], axis=0)
-    summed, packed = barrier((summed, packed))
-    summed = lax.psum(summed, ("z", "core"))
+    summed, out_sent, packed = barrier((summed, out_sent, packed))
+    summed = lax.all_to_all(summed, "seq", 0, 0, tiled=True)
+    out_w = lax.psum(out_sent, ("z", "core"))
     packed = jnp.stack(exchange(packed, "seq"))
     new_compressed = jnp.concatenate(
         [lax.dynamic_index_in_dim(packed, p ^ me, 0, keepdims=False) for p in range(parts)], axis=2
@@ -1140,11 +1136,10 @@
     halves = [late_one.reshape(2, unit_cols, width), late_two.reshape(2, unit_cols, width)]
     up_w, down_w = lay_out(core, halves, [swap(rows) for rows in halves], parts)
     down_w = down_w.reshape(4 * unit_cols, width)
-    summed, output, segment_grad, new_compressed, up_w, down_w = barrier(
-        (summed, output, segment_grad, new_compressed, up_w, down_w)
-    )
-    out_w = summed[squares:].reshape(cols, width).astype(F32)
-    summed = summed[:squares].reshape(parts, cols + 16, wide)
+    summed, out_w, output, segment_grad, new_compressed, up_w, down_w = barrier(
+        (summed, out_w, output, segment_grad, new_compressed, up_w, down_w)
+    )
+    out_w = out_w.astype(F32)
     query_w, key_w, value_w, rel_w = lay_squares(summed, cols)
     small = jnp.sum(summed[:, cols : cols + 3].astype(F32), axis=0)
     piece = lambda row, i: small[row, cols * i : cols * (i + 1)]

time: 559 us -> 596 us (1.066)
  waiting for transfers between devices: 158 us -> 190 us
  starting transfers between devices: 50.6 us -> 59.6 us
    psum x1 -> x2, waiting for transfers between devices: 8.11 us -> 79.7 us  [the longest x1 42.8 us: body(): summed = lax.psum(square_grads, ('z', 'core'))]
    ppermute x9, waiting for transfers between devices: 48.8 us -> 0.02 us  [exchange(): lax.ppermute(block(me ^ apart), name, [(i, i ^ apart) for i in range(coun...]
    all_to_all x1, waiting for transfers between devices: 48.1 us -> 0.01 us  [body(): got = lax.all_to_all(sent, 'seq', 0, 0, tiled=True)]
    all_gather x1, waiting for transfers between devices: 16.5 us -> 50.6 us  [body(): rows_all = [lax.all_gather(local[0], 'seq')]]
    all_to_all x1 -> x2, waiting for transfers between devices: 0.01 us -> 11.7 us  [the longest x1 11.7 us: body(): others = lax.all_to_all(others, 'seq', 0, 0, tiled=True)]
    concatenate x3 -> x0, local copies, waits for them, and re-layouts: 7.68 us -> none  [the longest x1 7.47 us: body(): jnp.concatenate([sent, jnp.broadcast_to(vectors, (parts, *vectors.shape))...]
    unnamed x106 -> x109, local copies, waits for them, and re-layouts: 24.3 us -> 21.5 us
    another operation x5 -> x7, other arithmetic: 17.6 us -> 18.6 us
  transfers between devices with their start and end apart: 34 -> 37, of which waited for: 13 -> 11; matrix products, arithmetic and copies ran while one was open for 20% -> 18% of each run, Pallas kernels for 36% -> 33%
where the time goes in v2:
time: 596 us; the launch traced here: 588 us
  Pallas kernels  198 us (33%)
  waiting for transfers between devices  190 us (32%)
  other arithmetic  62.7 us (11%)
  starting transfers between devices  59.6 us (10%)
  local copies, waits for them, and re-layouts  56.8 us (10%)
  between operations  15.5 us (3%)
    pallas_call x2, Pallas kernels, forward_back(): pl.pallas_call(functools.partial(forward_back_kernel, last, parts, pair),...  56.3 us
    all_gather x1, waiting for transfers between devices, body(): rows_all = [lax.all_gather(local[0], 'seq')]  50.6 us
    psum x1, waiting for transfers between devices, body(): summed = lax.psum(square_grads, ('z', 'core'))  42.8 us
    pallas_call x2, Pallas kernels, pull(): pl.pallas_call(functools.partial(pull_kernel, cuts), grid_spec=grid_spec,...  38.1 us
    psum x1, waiting for transfers between devices, body(): out_w = lax.psum(out_sent, ('z', 'core'))  36.9 us
    pallas_call x1, Pallas kernels, attend(): pl.pallas_call(functools.partial(attend_kernel, cuts), grid_spec=grid_spe...  29.8 us
    ppermute x6, waiting for transfers between devices, collect(): lax.ppermute(block, name, [(i, i ^ apart) for i in range(count)])  26.2 us
    unnamed x109, local copies, waits for them, and re-layouts  21.5 us
  transfers between devices with their start and end apart: 37, of which 11 were waited for; matrix products, arithmetic and copies ran while one was open for 18% of the time, Pallas kernels for 33%

profile of v2, /device:TPU:0, one launch (start us, length us, event | category | flops | bytes accessed | tf_op | source)
XLA Modules:
  0.0 588.0 jit_solution(13588570488613916977)
XLA Ops:
  25.9 5.0 all-to-all-start
  37.6 4.5 reshape.354
  57.3 15.0 %fusion = (bf16[1792,512]{1,0:T(8,128)(2,1)S(1)}, bf16[1792,512]{1,0:T(8,128)(2,1)}) fusion(f32[512]{0:T(512)S(1)} %multiply_exponential_fusion, f32[1792]{0:T(1024)S(1)} %subtract_convert_fusion), kind=kLoop, calls=%fused_computation.4 | loop fusion | flops 2752512 | bytes 3679232 | tf_op jit(solution)/shard_map/convert.5
  87.1 50.6 %all-gather.7.cloned.1.call-done = bf16[12,448,1024]{2,1,0:T(8,128)(2,1)} async-done(((bf16[3,448,1024]{2,1,0:T(8,128)(2,1)}), bf16[12,448,1024]{2,1,0:T(8,128)(2,1)}) %all-gather.7.cloned.1.call-update) | async-done | bytes 11010064 | tf_op jit(solution)/shard_map/all_gather | solution.py:978
  137.7 3.7 all-to-all-start.1
  145.0 18.2 %project.1 = (bf16[3,256,1024]{2,1,0:T(8,128)(2,1)}, bf16[3,768,1024]{2,1,0:T(8,128)(2,1)}, bf16[3,768,1024]{2,1,0:T(8,128)(2,1)}, f32[4,3,192,256]{3,2,1,0:T(8,...) custom-call(bf16[4,3,448,1024]{3,2,1,0:T(8,128)(2,1)} %bitcast.171, f32[1,1024]{1,0:T(1,128)} %bitcast.214, ...), custom_call_target="tpu_custom_call" | custom-call | flops 195500000 | tf_op jit(solution)/shard_map/project/pallas_call | solution.py:379
  163.2 11.7 %all-to-all-done.1 = bf16[4,128,1792]{2,1,0:T(8,128)(2,1)S(1)} async-done(((bf16[4,128,1792]{2,1,0:T(8,128)(2,1)}), bf16[4,128,1792]{2,1,0:T(8,128)(2,1)S(1)}, u32[]{:S(2)}, u32[]{:S(2)}) %all-to-all-start.1) | async-done | bytes 1835040 | tf_op jit(solution)/shard_map/all_to_all | solution.py:1008
  176.1 29.8 %attend.1 = (bf16[3,2,768,1792]{3,2,1,0:T(8,128)(2,1)}, f32[3,2,768,128]{3,2,1,0:T(8,128)}, bf16[4,3,192,256]{3,2,1,0:T(8,128)(2,1)}, bf16[4,3,192,256]{3,2,1,0:T(8,128)(2,1)}, bf16[4,3,192,256]{3,2,1,0:T(8,128)(2,1)}) custom-call(f32[4,3,192,256]{3,2,1,0:T(8,128)} %get-tuple-element.125.q_ref, f32[1,256]{1,0:T(1,128)} %bitcast.240, f32[1,256]{1,0:T(1,128)} %bitcast.241, ...), custom_call_target="tpu_custom_call" | custom-call | flops 460000000 | tf_op jit(solution)/shard_map/attend/pallas_call | solution.py:189
  208.3 3.5 all-to-all-start.2
  217.3 11.5 %compress.1 = bf16[4,3,64,256]{3,2,1,0:T(8,128)(2,1)} custom-call(bf16[4,3,448,1024]{3,2,1,0:T(8,128)(2,1)} %bitcast.172, bf16[1024,768]{1,0:T(8,128)(2,1)} %slice.150.w_ref, f32[1,256]{1,0:T(1,128)} %bitcast.231), custom_call_target="tpu_custom_call" | custom-call | flops 74750000 | tf_op jit(solution)/shard_map/compress/pallas_call | solution.py:672
  228.8 8.7 %all-to-all-done.2.a_ref = bf16[4,3,192,256]{3,2,1,0:T(8,128)(2,1)S(1)} async-done(((bf16[4,3,192,256]{3,2,1,0:T(8,128)(2,1)}), bf16[4,3,192,256]{3,2,1,0:T(8,128)(2,1)S(1)}, u32[]{:S(2)}, u32[]{:S(2)}) %all-to-all-start.2) | async-done | bytes 1179680 | tf_op jit(solution)/shard_map/all_to_all | solution.py:1030
  238.6 5.9 %leave.1 = (bf16[3,192,1024]{2,1,0:T(8,128)(2,1)}, f32[3,192,1024]{2,1,0:T(8,128)}, bf16[3,192,1024]{2,1,0:T(8,128)(2,1)}) custom-call(bf16[4,3,192,256]{3,2,1,0:T(8,128)(2,1)} %copy-done.11, bf16[3,192,1024]{2,1,0:T(8,128)(2,1)} %s_ref.1, bf16[1024,1024]{1,0:T(8,128)(2,1)} %slice.151.w_ref, f32[1,1024]{1,0:T(1,128)} %bitcast.224, f32[1,1024]{1,0:T(1,128)} %bitcast.212, ...), custom_call_target="tpu_custom_call" | custom-call | flops 69000000 | tf_op jit(solution)/shard_map/leave/pallas_call | solution.py:565
  250.4 27.0 %forward_back.2 = (f32[1152,1024]{1,0:T(8,128)}, f32[1152,1024]{1,0:T(8,128)}, bf16[4,512,1024]{2,1,0:T(8,128)(2,1)}, f32[1,1024]{1,0:T(1,128)}) custom-call(bf16[1152,1024]{1,0:T(8,128)(2,1)} %pad_maximum_fusion.3.n_ref, bf16[1152,1024]{1,0:T(8,128)(2,1)} %pad_maximum_fusion.2.c_ref, bf16[4,512,1024]{2,1,0:T(8,128)(2,1)} %bitcast.165, ...), custom_call_target="tpu_custom_call" | custom-call | flops 333500000 | tf_op jit(solution)/shard_map/forward_back/pallas_call | solution.py:508
  278.0 29.3 %forward_back.3 = (f32[576,1024]{1,0:T(8,128)}, bf16[576,1024]{1,0:T(8,128)(2,1)}, f32[576,1024]{1,0:T(8,128)}, bf16[576,1024]{1,0:T(8,128)(2,1)}, bf16[4,512,1024]{2,1,0:T(8,128)(2,1)}, /*index=5*/f32[1,1024]{1,0:T(1,128)}) custom-call(bf16[1152,1024]{1,0:T(8,128)(2,1)} %pad_maximum_fusion.3.n_ref, bf16[1152,1024]{1,0:T(8,128)(2,1)} %pad_maximum_fusion.2.c_ref, ...), custom_call_target="tpu_custom_call" | custom-call | flops 333500000 | tf_op jit(solution)/shard_map/forward_back/pallas_call | solution.py:508
  311.4 8.5 %enter.1 = (f32[3,192,1024]{2,1,0:T(8,128)}, bf16[3,192,1024]{2,1,0:T(8,128)(2,1)}, bf16[4,3,192,256]{3,2,1,0:T(8,128)(2,1)}, f32[8,1024]{1,0:T(8,128)}) custom-call(f32[3,192,1024]{2,1,0:T(8,128)} %get-tuple-element.138.m_ref, f32[3,192,1024]{2,1,0:T(8,128)} %bitcast.185, bf16[3,192,1024]{2,1,0:T(8,128)(2,1)} %bitcast.192, bf16[3,192,1024]{2,1,0:T(8,128)(2,1)} %c_ref.1, ...), custom_call_target="tpu_custom_call" | custom-call | flops 80500000 | tf_op jit(solution)/shard_map/enter/pallas_call | solution.py:621
  321.0 3.5 all-to-all-start.3
  325.3 4.3 fusion.11
  332.8 8.5 %all-to-all-done.3.g_ref = bf16[4,3,192,256]{3,2,1,0:T(8,128)(2,1)S(1)} async-done(((bf16[4,3,192,256]{3,2,1,0:T(8,128)(2,1)}), bf16[4,3,192,256]{3,2,1,0:T(8,128)(2,1)S(1)}, u32[]{:S(2)}, u32[]{:S(2)}) %all-to-all-start.3) | async-done | bytes 1179680 | tf_op jit(solution)/shard_map/all_to_all | solution.py:1064
  347.5 19.2 %pull.2 = (bf16[3,768,128]{2,1,0:T(8,128)(2,1)}, bf16[3,128,1792]{2,1,0:T(8,128)(2,1)}, bf16[3,128,1792]{2,1,0:T(8,128)(2,1)}, bf16[3,768,128]{2,1,0:T(8,128)(2,...) custom-call(bf16[3,2,768,1792]{3,2,1,0:T(8,128)(2,1)} %get-tuple-element.156.e_ref, ...), custom_call_target="tpu_custom_call" | custom-call | flops 448500000 | tf_op jit(solution)/shard_map/pull/pallas_call | solution.py:332
  367.0 3.7 collective-permute-start.11
  372.5 18.9 %pull.3 = (bf16[3,768,128]{2,1,0:T(8,128)(2,1)}, bf16[3,128,1792]{2,1,0:T(8,128)(2,1)}, bf16[3,128,1792]{2,1,0:T(8,128)(2,1)}, bf16[3,768,128]{2,1,0:T(8,128)(2,...) custom-call(bf16[3,2,768,1792]{3,2,1,0:T(8,128)(2,1)} %get-tuple-element.156.e_ref, ...), custom_call_target="tpu_custom_call" | custom-call | flops 448500000 | tf_op jit(solution)/shard_map/pull/pallas_call | solution.py:332
  394.7 9.4 %all-to-all-start.4 = ((bf16[4,256,1024]{2,1,0:T(8,128)(2,1)}), bf16[4,256,1024]{2,1,0:T(8,128)(2,1)S(1)}, u32[]{:S(2)}, u32[]{:S(2)}) async-start(bf16[4,256,1024]{2,1,0:T(8,128)(2,1)} %bitcast.186), calls=%async_computation.6 | async-start | bytes 4194304 | tf_op jit(solution)/shard_map/all_to_all | solution.py:1115
  410.6 20.3 %settle.1 = (bf16[4,3,192,1024]{3,2,1,0:T(8,128)(2,1)}, bf16[4,272,1024]{2,1,0:T(8,128)(2,1)}) custom-call(s32[1]{0:T(128)} %bitcast.me_ref, bf16[3,256,1024]{2,1,0:T(8,128)(2,1)} %get-tuple-element.120.old_ref, bf16[3,768,1024]{2,1,0:T(8,128)(2,1)} %get-tuple-element.121.mem_ref, bf16[3,768,1024]{2,1,0:T(8,128)(2,1)} %get-tuple-element.122.seg_ref, ...), custom_call_target="tpu_custom_call" | custom-call | flops 161000000 | tf_op jit(solution)/shard_map/settle/pallas_call | solution.py:829
  432.2 4.9 all-to-all-start.6
  442.8 4.7 collective-permute-done.20
  447.5 19.5 %collective-permute-done.19 = bf16[128,1024]{1,0:T(8,128)(2,1)S(1)} collective-permute-done((bf16[128,1024]{1,0:T(8,128)(2,1)S(1)}, bf16[128,1024]{1,0:T(8,128)(2,1)S(1)}, u32[]{:S(2)}, u32[]{:S(2)}) %collective-permute-start.19) | collective-permute-done | bytes 262176 | tf_op jit(solution)/shard_map/ppermute | solution.py:912
  471.7 42.8 %all-reduce.7.cloned.1.call-done = bf16[4,272,1024]{2,1,0:T(8,128)(2,1)} async-done(((bf16[4,272,1024]{2,1,0:T(8,128)(2,1)}), bf16[4,272,1024]{2,1,0:T(8,128)(2,1)}) %all-reduce.7.cloned.1.call-update) | async-done | bytes 2228240 | tf_op jit(solution)/shard_map/psum | solution.py:1119
  518.2 4.5 all-to-all-start.5
  523.7 5.8 lay_out.1
  529.5 3.8 convert_reduce_fusion
  537.2 36.9 %all-reduce.9.cloned.1.call-done = bf16[256,1024]{1,0:T(8,128)(2,1)} async-done(((bf16[256,1024]{1,0:T(8,128)(2,1)}), bf16[256,1024]{1,0:T(8,128)(2,1)}) %all-reduce.9.cloned.1.call-update) | async-done | bytes 524304 | tf_op jit(solution)/shard_map/psum | solution.py:1125
  575.1 3.3 lay_squares.1
  (272 shorter events, 125.4 us)
Async XLA Ops:
  7.2 130.4 %all-gather.7.cloned.1.call-start = ((), (), s32[]{:S(2)}) async-start(), calls=%async_computation.13 | async-start | bytes 13762560 | tf_op jit(solution)/shard_map/all_gather | solution.py:978
  25.9 46.4 %all-to-all-start = ((bf16[4,144,1024]{2,1,0:T(8,128)(2,1)}), bf16[4,144,1024]{2,1,0:T(8,128)(2,1)S(1)}, u32[]{:S(2)}, u32[]{:S(2)}) async-start(bf16[4,144,1024]{2,1,0:T(8,128)(2,1)} %pad_maximum_fusion.6), calls=%async_computation | async-start | bytes 2359296 | tf_op jit(solution)/shard_map/all_to_all | solution.py:970
  31.0 219.4 %all-gather.9.cloned.1.call-start = ((), (), s32[]{:S(2)}) async-start(), calls=%async_computation.14 | async-start | bytes 5242880 | tf_op jit(solution)/shard_map/all_gather | solution.py:1015
  31.2 48.0 %collective-permute-start.1 = (bf16[576,1024]{1,0:T(8,128)(2,1)}, bf16[576,1024]{1,0:T(8,128)(2,1)}, u32[]{:S(2)}, u32[]{:S(2)}) collective-permute-start(bf16[576,1024]{1,0:T(8,128)(2,1)} %bitcast.7), channel_id=1, source_target_pairs={{0,4},{4,0},{1,5},{5,1},{2,6},{6,2},{3,7},{7,3},{8,12},{12,8},{9,1... | collective-permute-start | bytes 3538952 | tf_op jit(solution)/shard_map/ppermute | solution.py:893
  72.4 10.0 %collective-permute-start = (bf16[4,128,1024]{2,1,0:T(8,128)(2,1)S(1)}, bf16[4,128,1024]{2,1,0:T(8,128)(2,1)S(1)}, u32[]{:S(2)}, u32[]{:S(2)}) collective-permute-start(bf16[4,128,1024]{2,1,0:T(8,128)(2,1)S(1)} %slice.142), channel_id=1, source_target_pairs={{0,4},{4,0},{1,5},{5,1},{2,6},{6,2},{3,7},{7,3},{8,12},{12,8},{9,1... | collective-permute-start | bytes 3145736 | tf_op jit(solution)/shard_map/ppermute | solution.py:893
  137.7 37.3 %all-to-all-start.1 = ((bf16[4,128,1792]{2,1,0:T(8,128)(2,1)}), bf16[4,128,1792]{2,1,0:T(8,128)(2,1)S(1)}, u32[]{:S(2)}, u32[]{:S(2)}) async-start(bf16[4,128,1792]{2,1,0:T(8,128)(2,1)} %pad_maximum_fusion.5), calls=%async_computation.1 | async-start | bytes 3670016 | tf_op jit(solution)/shard_map/all_to_all | solution.py:1008
  141.4 136.6 %all-gather.11.cloned.1.call-start = ((), (), s32[]{:S(2)}) async-start(), calls=%async_computation.15 | async-start | bytes 5242880 | tf_op jit(solution)/shard_map/all_gather | solution.py:1018
  208.3 29.2 %all-to-all-start.2 = ((bf16[4,3,192,256]{3,2,1,0:T(8,128)(2,1)}), bf16[4,3,192,256]{3,2,1,0:T(8,128)(2,1)S(1)}, u32[]{:S(2)}, u32[]{:S(2)}) async-start(bf16[4,3,192,256]{3,2,1,0:T(8,128)(2,1)} %get-tuple-element.130.o_ref), calls=%async_computation.2 | async-start | bytes 2359296 | tf_op jit(solution)/shard_map/all_to_all | solution.py:1030
  211.8 129.5 %reduce-scatter.3.cloned.1.call-start = ((), (), s32[]{:S(2)}) async-start(), calls=%async_computation.9 | async-start | bytes 5242880 | tf_op jit(solution)/shard_map/reduce_scatter | solution.py:1048
  307.4 17.9 %collective-permute-start.5 = (bf16[576,1024]{1,0:T(8,128)(2,1)}, bf16[576,1024]{1,0:T(8,128)(2,1)S(1)}, u32[]{:S(2)}, u32[]{:S(2)}) collective-permute-start(bf16[576,1024]{1,0:T(8,128)(2,1)} %get-tuple-element.151), channel_id=1, source_target_pairs={{0,4},{4,0},{1,5},{5,1},{2,6},{6,2},{3,7},{7,3},{8,12},{12,8},{9,1... | collective-permute-start | bytes 3538952 | tf_op jit(solution)/shard_map/ppermute | solution.py:893
  321.0 20.4 %all-to-all-start.3 = ((bf16[4,3,192,256]{3,2,1,0:T(8,128)(2,1)}), bf16[4,3,192,256]{3,2,1,0:T(8,128)(2,1)S(1)}, u32[]{:S(2)}, u32[]{:S(2)}) async-start(bf16[4,3,192,256]{3,2,1,0:T(8,128)(2,1)} %get-tuple-element.153), calls=%async_computation.4 | async-start | bytes 2359296 | tf_op jit(solution)/shard_map/all_to_all | solution.py:1064
  324.5 70.2 %reduce-scatter.5.cloned.1.call-start = ((), (), s32[]{:S(2)}) async-start(), calls=%async_computation.10 | async-start | bytes 5242880 | tf_op jit(solution)/shard_map/reduce_scatter | solution.py:1094
  343.1 23.7 %collective-permute-start.6 = (bf16[128,1024]{1,0:T(8,128)(2,1)S(1)}, bf16[128,1024]{1,0:T(8,128)(2,1)S(1)}, u32[]{:S(2)}, u32[]{:S(2)}) collective-permute-start(bf16[128,1024]{1,0:T(8,128)(2,1)S(1)} %get-tuple-element.241), channel_id=1, source_target_pairs={{0,8},{8,0},{16,24},{24,16},{1,9},{9,1},{17,25},{25,17},{2,10},{10... | collective-permute-start | bytes 786440 | tf_op jit(solution)/shard_map/ppermute | solution.py:901
  344.6 22.2 %collective-permute-start.7 = (bf16[128,1024]{1,0:T(8,128)(2,1)S(1)}, bf16[128,1024]{1,0:T(8,128)(2,1)S(1)}, u32[]{:S(2)}, u32[]{:S(2)}) collective-permute-start(bf16[128,1024]{1,0:T(8,128)(2,1)S(1)} %get-tuple-element.240), channel_id=1, source_target_pairs={{0,16},{8,24},{16,0},{24,8},{1,17},{9,25},{17,1},{25,9},{2,18},{10... | collective-permute-start | bytes 786440 | tf_op jit(solution)/shard_map/ppermute | solution.py:901
  347.0 19.8 %collective-permute-start.8 = (bf16[128,1024]{1,0:T(8,128)(2,1)S(1)}, bf16[128,1024]{1,0:T(8,128)(2,1)S(1)}, u32[]{:S(2)}, u32[]{:S(2)}) collective-permute-start(bf16[128,1024]{1,0:T(8,128)(2,1)S(1)} %get-tuple-element.239), channel_id=1, source_target_pairs={{0,24},{8,16},{16,8},{24,0},{1,25},{9,17},{17,9},{25,1},{2,26},{10... | collective-permute-start | bytes 786440 | tf_op jit(solution)/shard_map/ppermute | solution.py:901
  367.0 24.4 %collective-permute-start.11 = (bf16[128,1024]{1,0:T(8,128)(2,1)S(1)}, bf16[128,1024]{1,0:T(8,128)(2,1)S(1)}, u32[]{:S(2)}, u32[]{:S(2)}) collective-permute-start(bf16[128,1024]{1,0:T(8,128)(2,1)S(1)} %add_convert_fusion.1), channel_id=1, source_target_pairs={{0,24},{8,16},{16,8},{24,0},{1,25},{9,17},{17,9},{25,1},{2,26},{10... | collective-permute-start | bytes 786440 | tf_op jit(solution)/shard_map/ppermute | solution.py:912
  370.6 22.7 %collective-permute-start.10 = (bf16[128,1024]{1,0:T(8,128)(2,1)S(1)}, bf16[128,1024]{1,0:T(8,128)(2,1)S(1)}, u32[]{:S(2)}, u32[]{:S(2)}) collective-permute-start(bf16[128,1024]{1,0:T(8,128)(2,1)S(1)} %add_convert_fusion.1), channel_id=1, source_target_pairs={{0,16},{8,24},{16,0},{24,8},{1,17},{9,25},{17,1},{25,9},{2,18},{10... | collective-permute-start | bytes 786440 | tf_op jit(solution)/shard_map/ppermute | solution.py:912
  372.4 20.9 %collective-permute-start.9 = (bf16[128,1024]{1,0:T(8,128)(2,1)S(1)}, bf16[128,1024]{1,0:T(8,128)(2,1)S(1)}, u32[]{:S(2)}, u32[]{:S(2)}) collective-permute-start(bf16[128,1024]{1,0:T(8,128)(2,1)S(1)} %add_convert_fusion.1), channel_id=1, source_target_pairs={{0,8},{8,0},{16,24},{24,16},{1,9},{9,1},{17,25},{25,17},{2,10},{10... | collective-permute-start | bytes 786440 | tf_op jit(solution)/shard_map/ppermute | solution.py:912
  394.7 36.2 %all-to-all-start.4 = ((bf16[4,256,1024]{2,1,0:T(8,128)(2,1)}), bf16[4,256,1024]{2,1,0:T(8,128)(2,1)S(1)}, u32[]{:S(2)}, u32[]{:S(2)}) async-start(bf16[4,256,1024]{2,1,0:T(8,128)(2,1)} %bitcast.186), calls=%async_computation.6 | async-start | bytes 4194304 | tf_op jit(solution)/shard_map/all_to_all | solution.py:1115
  406.2 24.7 %collective-permute-start.12 = (bf16[128,1024]{1,0:T(8,128)(2,1)}, bf16[128,1024]{1,0:T(8,128)(2,1)S(1)}, u32[]{:S(2)}, u32[]{:S(2)}) collective-permute-start(bf16[128,1024]{1,0:T(8,128)(2,1)} %get-tuple-element.233), channel_id=1, source_target_pairs={{0,8},{8,0},{16,24},{24,16},{1,9},{9,1},{17,25},{25,17},{2,10},{10... | collective-permute-start | bytes 786440 | tf_op jit(solution)/shard_map/ppermute | solution.py:901
  408.2 22.7 %collective-permute-start.13 = (bf16[128,1024]{1,0:T(8,128)(2,1)}, bf16[128,1024]{1,0:T(8,128)(2,1)S(1)}, u32[]{:S(2)}, u32[]{:S(2)}) collective-permute-start(bf16[128,1024]{1,0:T(8,128)(2,1)} %get-tuple-element.232), channel_id=1, source_target_pairs={{0,16},{8,24},{16,0},{24,8},{1,17},{9,25},{17,1},{25,9},{2,18},{10... | collective-permute-start | bytes 786440 | tf_op jit(solution)/shard_map/ppermute | solution.py:901
  408.9 22.0 %collective-permute-start.14 = (bf16[128,1024]{1,0:T(8,128)(2,1)S(1)}, bf16[128,1024]{1,0:T(8,128)(2,1)S(1)}, u32[]{:S(2)}, u32[]{:S(2)}) collective-permute-start(bf16[128,1024]{1,0:T(8,128)(2,1)S(1)} %get-tuple-element.231), channel_id=1, source_target_pairs={{0,24},{8,16},{16,8},{24,0},{1,25},{9,17},{17,9},{25,1},{2,26},{10... | collective-permute-start | bytes 786440 | tf_op jit(solution)/shard_map/ppermute | solution.py:901
  432.2 86.0 %all-to-all-start.6 = ((bf16[4,3,192,1024]{3,2,1,0:T(8,128)(2,1)}), bf16[4,3,192,1024]{3,2,1,0:T(8,128)(2,1)}, u32[]{:S(2)}, u32[]{:S(2)}) async-start(bf16[4,3,192,1024]{3,2,1,0:T(8,128)(2,1)} %get-tuple-element.195), calls=%async_computation.8 | async-start | bytes 9437184 | tf_op jit(solution)/shard_map/all_to_all | solution.py:1130
  437.2 77.3 %all-reduce.7.cloned.1.call-start = ((), (), s32[]{:S(2)}) async-start(), calls=%async_computation.11 | async-start | bytes 4456448 | tf_op jit(solution)/shard_map/psum | solution.py:1119
  437.8 136.3 %all-reduce.9.cloned.1.call-start = ((), (), s32[]{:S(2)}) async-start(), calls=%async_computation.12 | async-start | bytes 1048576 | tf_op jit(solution)/shard_map/psum | solution.py:1125
  438.0 9.5 %collective-permute-start.20 = (bf16[128,1024]{1,0:T(8,128)(2,1)S(1)}, bf16[128,1024]{1,0:T(8,128)(2,1)S(1)}, u32[]{:S(2)}, u32[]{:S(2)}) collective-permute-start(bf16[128,1024]{1,0:T(8,128)(2,1)S(1)} %add_convert_fusion), channel_id=1, source_target_pairs={{0,24},{8,16},{16,8},{24,0},{1,25},{9,17},{17,9},{25,1},{2,26},{10... | collective-permute-start | bytes 786440 | tf_op jit(solution)/shard_map/ppermute | solution.py:912
  440.2 26.8 %collective-permute-start.19 = (bf16[128,1024]{1,0:T(8,128)(2,1)S(1)}, bf16[128,1024]{1,0:T(8,128)(2,1)S(1)}, u32[]{:S(2)}, u32[]{:S(2)}) collective-permute-start(bf16[128,1024]{1,0:T(8,128)(2,1)S(1)} %add_convert_fusion), channel_id=1, source_target_pairs={{0,16},{8,24},{16,0},{24,8},{1,17},{9,25},{17,1},{25,9},{2,18},{10... | collective-permute-start | bytes 786440 | tf_op jit(solution)/shard_map/ppermute | solution.py:912
  440.6 26.3 %collective-permute-start.18 = (bf16[128,1024]{1,0:T(8,128)(2,1)S(1)}, bf16[128,1024]{1,0:T(8,128)(2,1)S(1)}, u32[]{:S(2)}, u32[]{:S(2)}) collective-permute-start(bf16[128,1024]{1,0:T(8,128)(2,1)S(1)} %add_convert_fusion), channel_id=1, source_target_pairs={{0,8},{8,0},{16,24},{24,16},{1,9},{9,1},{17,25},{25,17},{2,10},{10... | collective-permute-start | bytes 786440 | tf_op jit(solution)/shard_map/ppermute | solution.py:912
  442.7 81.0 %collective-permute-start.21 = (bf16[2,256,1024]{2,1,0:T(8,128)(2,1)S(1)}, bf16[2,256,1024]{2,1,0:T(8,128)(2,1)}, u32[]{:S(2)}, u32[]{:S(2)}) collective-permute-start(bf16[2,256,1024]{2,1,0:T(8,128)(2,1)S(1)} %bitcast.180), channel_id=1, source_target_pairs={{0,4},{4,0},{1,5},{5,1},{2,6},{6,2},{3,7},{7,3},{8,12},{12,8},{9,1... | collective-permute-start | bytes 3145736 | tf_op jit(solution)/shard_map/ppermute | solution.py:893
  468.3 55.4 %collective-permute-start.22 = (bf16[2,256,1024]{2,1,0:T(8,128)(2,1)}, bf16[2,256,1024]{2,1,0:T(8,128)(2,1)}, u32[]{:S(2)}, u32[]{:S(2)}) collective-permute-start(bf16[2,256,1024]{2,1,0:T(8,128)(2,1)} %bitcast.66.b_ref), channel_id=1, source_target_pairs={{0,4},{4,0},{1,5},{5,1},{2,6},{6,2},{3,7},{7,3},{8,12},{12,8},{9,1... | collective-permute-start | bytes 3145736 | tf_op jit(solution)/shard_map/ppermute | solution.py:893
  514.6 8.2 %collective-permute-start.17 = (bf16[3,64,256]{2,1,0:T(8,128)(2,1)S(1)}, bf16[3,64,256]{2,1,0:T(8,128)(2,1)S(1)}, u32[]{:S(2)}, u32[]{:S(2)}) collective-permute-start(bf16[3,64,256]{2,1,0:T(8,128)(2,1)S(1)} %get-tuple-element.250), channel_id=1, source_target_pairs={{0,3},{1,2},{2,1},{3,0},{4,7},{5,6},{6,5},{7,4},{8,11},{9,10},{10,... | collective-permute-start | bytes 294920 | tf_op jit(solution)/shard_map/ppermute | solution.py:901
  518.2 55.9 %all-to-all-start.5 = ((bf16[4,272,1024]{2,1,0:T(8,128)(2,1)}), bf16[4,272,1024]{2,1,0:T(8,128)(2,1)}, u32[]{:S(2)}, u32[]{:S(2)}) async-start(bf16[4,272,1024]{2,1,0:T(8,128)(2,1)} %all-reduce.7.cloned.1.call-done), calls=%async_computation.7 | async-start | bytes 4456448 | tf_op jit(solution)/shard_map/all_to_all | solution.py:1124
  (47 other events, 403.4 us)
Sparse Core Ops, SparseCore 0:
  12.8 124.7 all-gather.6
  140.1 65.2 all-gather.8
  207.8 61.6 all-gather.10
  277.5 59.9 reduce-scatter.2
  341.5 52.6 reduce-scatter.4
  440.7 73.8 all-reduce.6
  518.3 55.7 all-reduce.8

commit v3 on v1

--- a/solution.py
+++ b/solution.py
@@ -455,18 +455,15 @@
             part_ref[...] = jnp.zeros_like(part_ref)
             grad_ref[...] = jnp.zeros_like(grad_ref)
 
-    chunk = 288 if rows % 288 == 0 else rows
-    for base in range(0, rows, chunk):
-        at = slice(base, base + chunk)
-        pre[at, :] = mm(n_ref[at, :], up_weight, NN)
-        slope[at, :] = mm(c_ref[at, :], down_weight, NT)
-        for low in range(base, base + chunk, 16):
-            some = slice(low, low + 16)
-            value, change = gelu_both(pre[some, :] + shift_ref[...])
-            hidden[some, :] = value.astype(BF16)
-            act[some, :] = (change * slope[some, :]).astype(BF16)
-        part_ref[at, :] += mm(hidden[at, :], down_weight, NN)
-        grad_ref[at, :] += mm(act[at, :], up_weight, NT)
+    pre[...] = mm(n_ref[...], up_weight, NN)
+    slope[...] = mm(c_ref[...], down_weight, NT)
+    for low in range(0, rows, 16):
+        some = slice(low, low + 16)
+        value, change = gelu_both(pre[some, :] + shift_ref[...])
+        hidden[some, :] = value.astype(BF16)
+        act[some, :] = (change * slope[some, :]).astype(BF16)
+    part_ref[...] += mm(hidden[...], down_weight, NN)
+    grad_ref[...] += mm(act[...], up_weight, NT)
     sums_ref[...] = jnp.sum(act[...].astype(F32), axis=0, keepdims=True)
 
     @pl.when(tile >= 2)
@@ -595,7 +592,7 @@
 
     parts = a_ref.shape[0]
     rows, width = m_ref.shape
-    step = 16
+    step = 32
     total = [jnp.zeros((1, width), F32) for _ in range(4)]
     for low in range(0, rows, step):
         at = slice(low, low + step)
@@ -735,39 +732,44 @@
     )(core.reshape(1), *mine, *far)
 
 
-def lay_squares_kernel(in_ref, *out_refs):
-    parts = in_ref.shape[0]
-    cols = in_ref.shape[2] // len(out_refs)
-    for at, out_ref in enumerate(out_refs):
-        for part in range(parts):
-            out_ref[:, part * cols : (part + 1) * cols] = in_ref[
-                part, :, at * cols : (at + 1) * cols
-            ].astype(F32)
-
-
-def lay_squares(summed, rows):
-    parts, _, wide = summed.shape
+def lay_squares_kernel(where_ref, mine_ref, far_ref, *out_refs):
+    parts = mine_ref.shape[0]
+    cols = mine_ref.shape[2] // len(out_refs)
+    own = pl.program_id(0) == where_ref[0]
+    for part in range(parts):
+        value = jnp.where(own, mine_ref[part].astype(F32), far_ref[part].astype(F32))
+        for at, out_ref in enumerate(out_refs):
+            out_ref[:, part * cols : (part + 1) * cols] = value[:, at * cols : (at + 1) * cols]
+
+
+def lay_squares(where, mine, far):
+    layers, parts, rows, wide = mine.shape
     width = parts * wide // 4
-    step = rows // 2
+    pieces = pl.BlockSpec((None, parts, rows, wide), lambda c, z, at: (z ^ at[1], 0, 0, 0))
     return pl.pallas_call(
         lay_squares_kernel,
-        grid_spec=pl.GridSpec(
-            grid=(2,),
-            in_specs=[pl.BlockSpec((parts, step, wide), lambda i: (0, i, 0))],
-            out_specs=[pl.BlockSpec((step, width), lambda i: (i, 0)) for _ in range(4)],
-        ),
-        out_shape=[jax.ShapeDtypeStruct((rows, width), F32) for _ in range(4)],
+        grid_spec=pltpu.PrefetchScalarGridSpec(
+            num_scalar_prefetch=1,
+            grid=(2, layers),
+            in_specs=[pieces, pieces],
+            out_specs=[
+                pl.BlockSpec((rows, width), lambda c, z, at: (c * layers + z, 0)) for _ in range(4)
+            ],
+        ),
+        out_shape=[jax.ShapeDtypeStruct((2 * layers * rows, width), F32) for _ in range(4)],
         compiler_params=pltpu.CompilerParams(vmem_limit_bytes=VMEM_LIMIT),
         cost_estimate=cost(2.5),
         name="lay_squares",
-    )(summed)
+    )(where, mine, far)
 
 
 def settle_kernel(heads, me_ref, old_ref, mem_ref, seg_ref, *rest):
     q_refs, k_refs, v_refs, ks_refs, vs_refs, dt_refs, sums_refs = (
         rest[i * heads : (i + 1) * heads] for i in range(7)
     )
-    w_ref, table_ref, gain_ref, shift_ref, small_ref, part_ref, out_ref, total = rest[7 * heads :]
+    w_ref, table_ref, gain_ref, shift_ref, small_ref, part_ref, out_ref, row_ref, total = rest[
+        7 * heads :
+    ]
     stream = pl.program_id(0)
     parts, rows, wide = out_ref.shape
     cols = wide // 4
@@ -810,14 +812,14 @@
         gain_grad = (along - shift_ref[...] * shift_grad) / gain_ref[...]
         for at in range(parts):
             low, high = at * cols, (at + 1) * cols
-            out_ref[at, :cols, : 3 * cols] = total[:, low:high].T.astype(BF16)
-            out_ref[at, :cols, 3 * cols :] = rel[:, low:high].T.astype(BF16)
+            out_ref[at, :, : 3 * cols] = total[:, low:high].T.astype(BF16)
+            out_ref[at, :, 3 * cols :] = rel[:, low:high].T.astype(BF16)
             mine = (me_ref[0] == at).astype(F32)
             none = jnp.zeros((1, 2 * cols), F32)
             first = jnp.concatenate([gain_grad[:, low:high], shift_grad[:, low:high], none], axis=1)
             second = jnp.concatenate([none, mine * line(0), mine * line(1)], axis=1)
             added = jnp.concatenate([first, second, jnp.zeros((14, wide), F32)], axis=0)
-            out_ref[at, cols:, :] = (small_ref[at] + added).astype(BF16)
+            row_ref[at] = (small_ref[at] + added).astype(BF16)
 
 
 def settle(me, normed, grads, columns, table, gain, shift, small, parts):
@@ -846,13 +848,15 @@
             ],
             out_specs=[
                 pl.BlockSpec((parts, None, queries // parts, width), lambda s, *_: (0, s, 0, 0)),
-                whole(parts, cols + 16, wide),
+                whole(parts, cols, wide),
+                whole(parts, 16, wide),
             ],
             scratch_shapes=[pltpu.VMEM((3 * cols, width), F32)],
         ),
         out_shape=[
             jax.ShapeDtypeStruct((parts, group, queries // parts, width), BF16),
-            jax.ShapeDtypeStruct((parts, cols + 16, wide), BF16),
+            jax.ShapeDtypeStruct((parts, cols, wide), BF16),
+            jax.ShapeDtypeStruct((parts, 16, wide), BF16),
         ],
         compiler_params=pltpu.CompilerParams(
             dimension_semantics=("arbitrary",), vmem_limit_bytes=VMEM_LIMIT
@@ -906,16 +910,21 @@
     ]
 
 
-def collect(block, name):
+def spread(block, name):
     count = lax.axis_size(name)
-    me = lax.axis_index(name)
-    found = jnp.stack(
+    return jnp.stack(
         [block]
         + [
             lax.ppermute(block, name, [(i, i ^ apart) for i in range(count)])
             for apart in range(1, count)
         ]
     )
+
+
+def collect(block, name):
+    count = lax.axis_size(name)
+    me = lax.axis_index(name)
+    found = spread(block, name)
     return jnp.stack(
         [lax.dynamic_index_in_dim(found, me ^ i, 0, keepdims=False) for i in range(count)]
     )
@@ -936,6 +945,7 @@
     parts = lax.axis_size("seq")
     layers = lax.axis_size("z")
     core = lax.axis_index("core")
+    layer = lax.axis_index("z")
     me = lax.axis_index("seq")
     group, seg, width = segment.shape
     mem, old = memory.shape[1], compressed.shape[1]
@@ -1115,18 +1125,28 @@
     )
     late_two = exchange(late_two.reshape(layers, -1, width), "z")
     out_sent = lax.all_to_all(out_grad, "seq", 0, 0, tiled=True)
-    seg_part, square_grads = settle(
+    seg_part, squares, vectors = settle(
         me, normed, grads, columns, table_rev, gain_one, shift_one, small, parts
     )
-    late_two, out_sent, square_grads = barrier((late_two, out_sent, square_grads))
-    summed = lax.all_to_all(square_grads, "seq", 0, 0, tiled=True)
+    late_two, out_sent, squares = barrier((late_two, out_sent, squares))
+    halves = squares.reshape(parts, 2, cols // 2, wide)
+    half = lambda at: lax.dynamic_index_in_dim(halves, at, 1, keepdims=False)
+    squares = add_up([half(core), swap(half(1 - core))])
+    squares, seg_part, vectors, late_two, packed = barrier(
+        (squares, seg_part, vectors, late_two, packed)
+    )
+    squares = exchange(squares.reshape(parts, layers, -1, wide), "z", 1)
+    squares = lax.all_to_all(add_up(squares), "seq", 0, 0, tiled=True)
+    squares = spread(squares, "z")
+    squares_far = swap(squares)
+    vectors = lax.all_to_all(vectors, "seq", 0, 0, tiled=True)
+    vectors = jnp.sum(vectors.astype(F32), axis=0).astype(BF16)
+    out_sent = jnp.sum(out_sent.astype(F32), axis=0).astype(BF16)
+    summed = jnp.concatenate([out_sent.reshape(-1, wide), vectors], axis=0)
+    summed = lax.psum(summed, ("z", "core")).astype(F32)
+    out_w = summed[: cols * width // wide].reshape(cols, width)
+    small = summed[cols * width // wide :]
     late_two = collect(add_up(late_two), "z")
-    out_sent = jnp.sum(out_sent.astype(F32), axis=0).astype(BF16)
-    late_two, out_sent, summed, seg_part = barrier((late_two, out_sent, summed, seg_part))
-    squares = parts * (cols + 16)
-    summed = jnp.concatenate([summed.reshape(squares, wide), out_sent.reshape(-1, wide)], axis=0)
-    summed, packed = barrier((summed, packed))
-    summed = lax.psum(summed, ("z", "core"))
     packed = jnp.stack(exchange(packed, "seq"))
     new_compressed = jnp.concatenate(
         [lax.dynamic_index_in_dim(packed, p ^ me, 0, keepdims=False) for p in range(parts)], axis=2
@@ -1140,13 +1160,10 @@
     halves = [late_one.reshape(2, unit_cols, width), late_two.reshape(2, unit_cols, width)]
     up_w, down_w = lay_out(core, halves, [swap(rows) for rows in halves], parts)
     down_w = down_w.reshape(4 * unit_cols, width)
-    summed, output, segment_grad, new_compressed, up_w, down_w = barrier(
-        (summed, output, segment_grad, new_compressed, up_w, down_w)
-    )
-    out_w = summed[squares:].reshape(cols, width).astype(F32)
-    summed = summed[:squares].reshape(parts, cols + 16, wide)
-    query_w, key_w, value_w, rel_w = lay_squares(summed, cols)
-    small = jnp.sum(summed[:, cols : cols + 3].astype(F32), axis=0)
+    squares, squares_far, out_w, small, output, segment_grad, new_compressed, up_w, down_w = barrier(
+        (squares, squares_far, out_w, small, output, segment_grad, new_compressed, up_w, down_w)
+    )
+    query_w, key_w, value_w, rel_w = lay_squares(jnp.stack([core, layer]), squares, squares_far)
     piece = lambda row, i: small[row, cols * i : cols * (i + 1)]
     return (
         output,

time: 559 us -> 611 us (1.093)
  waiting for transfers between devices: 158 us -> 177 us
  starting transfers between devices: 50.6 us -> 64.1 us
  blocking collectives: 0 us -> 10 us
    psum x1, waiting for transfers between devices: 8.11 us -> 34.2 us  [body(): summed = lax.psum(summed, ('z', 'core')).astype(F32)]
    all_to_all x0 -> x1, blocking collectives: none -> 10 us  [body(): squares = lax.all_to_all(add_up(squares), 'seq', 0, 0, tiled=True)]
    ppermute x9 -> x12, waiting for transfers between devices: 48.8 us -> 41 us  [exchange(): lax.ppermute(block(me ^ apart), name, [(i, i ^ apart) for i in range(coun...]
    ppermute x6 -> x9, starting transfers between devices: 9.38 us -> 14.3 us  [spread(): lax.ppermute(block, name, [(i, i ^ apart) for i in range(count)])]
    ppermute x9 -> x12, starting transfers between devices: 12.5 us -> 16.7 us  [exchange(): lax.ppermute(block(me ^ apart), name, [(i, i ^ apart) for i in range(coun...]
    another operation x5 -> x7, other arithmetic: 15.2 us -> 17.9 us
    ppermute x6 -> x9, waiting for transfers between devices: 20.3 us -> 18.4 us  [spread(): lax.ppermute(block, name, [(i, i ^ apart) for i in range(count)])]
    unnamed x106 -> x118, local copies, waits for them, and re-layouts: 24.3 us -> 23.7 us
  transfers between devices with their start and end apart: 34 -> 42, of which waited for: 13 -> 15; matrix products, arithmetic and copies ran while one was open for 20% -> 20% of each run, Pallas kernels for 36% -> 32%
where the time goes in v3:
time: 611 us; the launch traced here: 603 us
  Pallas kernels  203 us (33%)
  waiting for transfers between devices  177 us (29%)
  local copies, waits for them, and re-layouts  67.4 us (11%)
  starting transfers between devices  64.1 us (10%)
  other arithmetic  61.2 us (10%)
  between operations  15.2 us (2%)
  blocking collectives  10 us (2%)
    pallas_call x2, Pallas kernels, forward_back(): pl.pallas_call(functools.partial(forward_back_kernel, last, parts, pair),...  56.8 us
    all_to_all x1, waiting for transfers between devices, body(): got = lax.all_to_all(sent, 'seq', 0, 0, tiled=True)  48.1 us
    ppermute x12, waiting for transfers between devices, exchange(): lax.ppermute(block(me ^ apart), name, [(i, i ^ apart) for i in range(coun...  41 us
    pallas_call x2, Pallas kernels, pull(): pl.pallas_call(functools.partial(pull_kernel, cuts), grid_spec=grid_spec,...  38.1 us
    psum x1, waiting for transfers between devices, body(): summed = lax.psum(summed, ('z', 'core')).astype(F32)  34.2 us
    pallas_call x1, Pallas kernels, attend(): pl.pallas_call(functools.partial(attend_kernel, cuts), grid_spec=grid_spe...  29.7 us
    unnamed x118, local copies, waits for them, and re-layouts  23.7 us
    pallas_call x1, Pallas kernels, settle(): pl.pallas_call(functools.partial(settle_kernel, len(grads)), grid_spec=pl...  20.2 us
  transfers between devices with their start and end apart: 42, of which 15 were waited for; matrix products, arithmetic and copies ran while one was open for 20% of the time, Pallas kernels for 32%

profile of v3, /device:TPU:0, one launch (start us, length us, event | category | flops | bytes accessed | tf_op | source)
XLA Modules:
  0.0 603.0 jit_solution(1070804790155406316)
XLA Ops:
  26.3 3.9 pad_maximum_fusion
  30.1 7.5 %copy.112 = bf16[4,144,2816]{2,1,0:T(8,128)(2,1)} copy(bf16[4,144,2816]{1,2,0:T(8,128)(2,1)} %pad_maximum_fusion) | data formatting | bytes 6488064 | tf_op jit(solution)/shard_map/concatenate | solution.py:977
  37.6 5.3 all-to-all-start
  44.7 48.1 %all-to-all-done = bf16[4,144,2816]{2,1,0:T(8,128)(2,1)S(1)} async-done(((bf16[4,144,2816]{2,1,0:T(8,128)(2,1)}), bf16[4,144,2816]{2,1,0:T(8,128)(2,1)S(1)}, u32[]{:S(2)}, u32[]{:S(2)}) %all-to-all-start) | async-done | bytes 3244064 | tf_op jit(solution)/shard_map/all_to_all | solution.py:978
  98.2 4.5 reshape.353
  109.3 13.8 %fusion = (bf16[1792,512]{1,0:T(8,128)(2,1)S(1)}, bf16[1792,512]{1,0:T(8,128)(2,1)S(1)}) fusion(f32[512]{0:T(512)S(1)} %multiply_exponential_fusion, f32[1792]{0:T(1024)S(1)} %subtract_convert_fusion), kind=kLoop, calls=%fused_computation.6 | loop fusion | flops 2752512 | bytes 3679232 | tf_op jit(solution)/shard_map/convert.8
  137.5 16.5 %all-gather.7.cloned.1.call-done = bf16[12,448,1024]{2,1,0:T(8,128)(2,1)} async-done(((bf16[3,448,1024]{2,1,0:T(8,128)(2,1)}), bf16[12,448,1024]{2,1,0:T(8,128)(2,1)}) %all-gather.7.cloned.1.call-update) | async-done | bytes 11010064 | tf_op jit(solution)/shard_map/all_gather | solution.py:984
  156.2 18.2 %project.1 = (bf16[3,256,1024]{2,1,0:T(8,128)(2,1)}, bf16[3,768,1024]{2,1,0:T(8,128)(2,1)}, bf16[3,768,1024]{2,1,0:T(8,128)(2,1)}, f32[4,3,192,256]{3,2,1,0:T(8,...) custom-call(bf16[4,3,448,1024]{3,2,1,0:T(8,128)(2,1)} %bitcast.188, f32[1,1024]{1,0:T(1,128)} %bitcast.243, ...), custom_call_target="tpu_custom_call" | custom-call | flops 195500000 | tf_op jit(solution)/shard_map/project/pallas_call | solution.py:379
  175.6 29.7 %attend.1 = (bf16[3,2,768,1792]{3,2,1,0:T(8,128)(2,1)}, f32[3,2,768,128]{3,2,1,0:T(8,128)}, bf16[4,3,192,256]{3,2,1,0:T(8,128)(2,1)}, bf16[4,3,192,256]{3,2,1,0:T(8,128)(2,1)}, bf16[4,3,192,256]{3,2,1,0:T(8,128)(2,1)}) custom-call(f32[4,3,192,256]{3,2,1,0:T(8,128)} %get-tuple-element.129.q_ref, f32[1,256]{1,0:T(1,128)} %bitcast.269, f32[1,256]{1,0:T(1,128)} %bitcast.270, ...), custom_call_target="tpu_custom_call" | custom-call | flops 460000000 | tf_op jit(solution)/shard_map/attend/pallas_call | solution.py:189
  211.8 11.7 %compress.1 = bf16[4,3,64,256]{3,2,1,0:T(8,128)(2,1)} custom-call(bf16[4,3,448,1024]{3,2,1,0:T(8,128)(2,1)} %bitcast.189, bf16[1024,768]{1,0:T(8,128)(2,1)} %slice.155.w_ref, f32[1,256]{1,0:T(1,128)} %bitcast.260), custom_call_target="tpu_custom_call" | custom-call | flops 74750000 | tf_op jit(solution)/shard_map/compress/pallas_call | solution.py:672
  223.5 3.7 all-to-all-done.1.a_ref
  228.2 5.9 leave.1
  240.0 27.7 %forward_back.2 = (f32[1152,1024]{1,0:T(8,128)}, f32[1152,1024]{1,0:T(8,128)}, bf16[4,512,1024]{2,1,0:T(8,128)(2,1)}, f32[1,1024]{1,0:T(1,128)}) custom-call(bf16[1152,1024]{1,0:T(8,128)(2,1)} %pad_maximum_fusion.4.n_ref, bf16[1152,1024]{1,0:T(8,128)(2,1)} %pad_maximum_fusion.3.c_ref, bf16[4,512,1024]{2,1,0:T(8,128)(2,1)} %bitcast.182, ...), custom_call_target="tpu_custom_call" | custom-call | flops 333500000 | tf_op jit(solution)/shard_map/forward_back/pallas_call | solution.py:508
  268.3 29.2 %forward_back.3 = (f32[576,1024]{1,0:T(8,128)}, bf16[576,1024]{1,0:T(8,128)(2,1)}, f32[576,1024]{1,0:T(8,128)}, bf16[576,1024]{1,0:T(8,128)(2,1)}, bf16[4,512,1024]{2,1,0:T(8,128)(2,1)}, /*index=5*/f32[1,1024]{1,0:T(1,128)}) custom-call(bf16[1152,1024]{1,0:T(8,128)(2,1)} %pad_maximum_fusion.4.n_ref, bf16[1152,1024]{1,0:T(8,128)(2,1)} %pad_maximum_fusion.3.c_ref, ...), custom_call_target="tpu_custom_call" | custom-call | flops 333500000 | tf_op jit(solution)/shard_map/forward_back/pallas_call | solution.py:508
  301.9 9.3 %enter.1 = (f32[3,192,1024]{2,1,0:T(8,128)}, bf16[3,192,1024]{2,1,0:T(8,128)(2,1)}, bf16[4,3,192,256]{3,2,1,0:T(8,128)(2,1)}, f32[8,1024]{1,0:T(8,128)}) custom-call(f32[3,192,1024]{2,1,0:T(8,128)} %get-tuple-element.143.m_ref, f32[3,192,1024]{2,1,0:T(8,128)} %bitcast.205, bf16[3,192,1024]{2,1,0:T(8,128)(2,1)} %bitcast.218, bf16[3,192,1024]{2,1,0:T(8,128)(2,1)} %c_ref.1, ...), custom_call_target="tpu_custom_call" | custom-call | flops 80500000 | tf_op jit(solution)/shard_map/enter/pallas_call | solution.py:621
  318.7 3.8 fusion.11
  325.7 7.6 %all-to-all-done.2.g_ref = bf16[4,3,192,256]{3,2,1,0:T(8,128)(2,1)S(1)} async-done(((bf16[4,3,192,256]{3,2,1,0:T(8,128)(2,1)}), bf16[4,3,192,256]{3,2,1,0:T(8,128)(2,1)S(1)}, u32[]{:S(2)}, u32[]{:S(2)}) %all-to-all-start.2) | async-done | bytes 1179680 | tf_op jit(solution)/shard_map/all_to_all | solution.py:1076
  339.4 19.2 %pull.2 = (bf16[3,768,128]{2,1,0:T(8,128)(2,1)}, bf16[3,128,1792]{2,1,0:T(8,128)(2,1)}, bf16[3,128,1792]{2,1,0:T(8,128)(2,1)}, bf16[3,768,128]{2,1,0:T(8,128)(2,...) custom-call(bf16[3,2,768,1792]{3,2,1,0:T(8,128)(2,1)} %get-tuple-element.161.e_ref, ...), custom_call_target="tpu_custom_call" | custom-call | flops 448500000 | tf_op jit(solution)/shard_map/pull/pallas_call | solution.py:332
  364.4 18.9 %pull.3 = (bf16[3,768,128]{2,1,0:T(8,128)(2,1)}, bf16[3,128,1792]{2,1,0:T(8,128)(2,1)}, bf16[3,128,1792]{2,1,0:T(8,128)(2,1)}, bf16[3,768,128]{2,1,0:T(8,128)(2,...) custom-call(bf16[3,2,768,1792]{3,2,1,0:T(8,128)(2,1)} %get-tuple-element.161.e_ref, ...), custom_call_target="tpu_custom_call" | custom-call | flops 448500000 | tf_op jit(solution)/shard_map/pull/pallas_call | solution.py:332
  386.1 9.2 %all-to-all-start.3 = ((bf16[4,256,1024]{2,1,0:T(8,128)(2,1)}), bf16[4,256,1024]{2,1,0:T(8,128)(2,1)S(1)}, u32[]{:S(2)}, u32[]{:S(2)}) async-start(bf16[4,256,1024]{2,1,0:T(8,128)(2,1)} %bitcast.208), calls=%async_computation.5 | async-start | bytes 4194304 | tf_op jit(solution)/shard_map/all_to_all | solution.py:1127
  401.8 20.2 %settle.1 = (bf16[4,3,192,1024]{3,2,1,0:T(8,128)(2,1)}, bf16[4,256,1024]{2,1,0:T(8,128)(2,1)}, bf16[4,16,1024]{2,1,0:T(8,128)(2,1)}) custom-call(s32[1]{0:T(128)} %bitcast.47.me_ref, bf16[3,256,1024]{2,1,0:T(8,128)(2,1)} %get-tuple-element.176.old_ref, bf16[3,768,1024]{2,1,0:T(8,128)(2,1)} %get-tuple-element.177.mem_ref, ...), custom_call_target="tpu_custom_call" | custom-call | flops 161000000 | tf_op jit(solution)/shard_map/settle/pallas_call | solution.py:834
  433.6 4.2 all-to-all-start.5
  440.6 14.6 %collective-permute-done.16 = bf16[4,32,1024]{2,1,0:T(8,128)(2,1)} collective-permute-done((bf16[4,32,1024]{2,1,0:T(8,128)(2,1)}, bf16[4,32,1024]{2,1,0:T(8,128)(2,1)}, u32[]{:S(2)}, u32[]{:S(2)}) %collective-permute-start.16) | collective-permute-done | bytes 262176 | tf_op jit(solution)/shard_map/ppermute | solution.py:908
  457.4 10.0 %all_to_all.35 = bf16[4,32,1024]{2,1,0:T(8,128)(2,1)} all-to-all(bf16[4,32,1024]{2,1,0:T(8,128)(2,1)} %fusion.16), channel_id=1, replica_groups=mesh['z'=4,'core'=2,'seq'=4] {'seq'}, dimensions={0} | all-to-all | bytes 524288 | tf_op jit(solution)/shard_map/all_to_all | solution.py:1139
  467.4 5.1 all-to-all-start.6
  479.1 6.2 %collective-permute-done.27 = bf16[128,1024]{1,0:T(8,128)(2,1)S(1)} collective-permute-done((bf16[128,1024]{1,0:T(8,128)(2,1)S(1)}, bf16[128,1024]{1,0:T(8,128)(2,1)S(1)}, u32[]{:S(2)}, u32[]{:S(2)}) %collective-permute-start.27) | collective-permute-done | bytes 262176 | tf_op jit(solution)/shard_map/ppermute | solution.py:918
  485.3 10.3 %collective-permute-done.26 = bf16[128,1024]{1,0:T(8,128)(2,1)S(1)} collective-permute-done((bf16[128,1024]{1,0:T(8,128)(2,1)S(1)}, bf16[128,1024]{1,0:T(8,128)(2,1)S(1)}, u32[]{:S(2)}, u32[]{:S(2)}) %collective-permute-start.26) | collective-permute-done | bytes 262176 | tf_op jit(solution)/shard_map/ppermute | solution.py:918
  504.9 23.5 %collective-permute-done.24 = bf16[3,64,256]{2,1,0:T(8,128)(2,1)S(1)} collective-permute-done((bf16[3,64,256]{2,1,0:T(8,128)(2,1)}, bf16[3,64,256]{2,1,0:T(8,128)(2,1)S(1)}, u32[]{:S(2)}, u32[]{:S(2)}) %collective-permute-start.24) | collective-permute-done | bytes 98336 | tf_op jit(solution)/shard_map/ppermute | solution.py:908
  534.7 34.2 %all-reduce.7.cloned.1.call-done = bf16[272,1024]{1,0:T(8,128)(2,1)} async-done(((bf16[272,1024]{1,0:T(8,128)(2,1)}), bf16[272,1024]{1,0:T(8,128)(2,1)}) %all-reduce.7.cloned.1.call-update) | async-done | bytes 557072 | tf_op jit(solution)/shard_map/psum | solution.py:1146
  574.0 6.0 lay_out.1
  580.0 3.7 convert_reduce_fusion
  588.8 7.2 %lay_squares.1 = (f32[256,1024]{1,0:T(8,128)}, f32[256,1024]{1,0:T(8,128)}, f32[256,1024]{1,0:T(8,128)}, f32[256,1024]{1,0:T(8,128)}) custom-call(s32[2]{0:T(128)} %pad_add_fusion.where_ref, bf16[4,4,32,1024]{3,2,1,0:T(8,128)(2,1)} %pad_maximum_fusion.9.mine_ref, bf16[4,4,32,1024]{3,2,1,0:T(8,128)(2,1)} %collective-permute-done.21.far_ref), custom_call_target="tpu_custom_call" | custom-call | flops 28750000 | tf_op jit(solution)/shard_map/lay_squares/pallas_call | solution.py:749
  (291 shorter events, 149.0 us)
Async XLA Ops:
  7.2 146.7 %all-gather.7.cloned.1.call-start = ((), (), s32[]{:S(2)}) async-start(), calls=%async_computation.12 | async-start | bytes 13762560 | tf_op jit(solution)/shard_map/all_gather | solution.py:984
  37.6 55.2 %all-to-all-start = ((bf16[4,144,2816]{2,1,0:T(8,128)(2,1)}), bf16[4,144,2816]{2,1,0:T(8,128)(2,1)S(1)}, u32[]{:S(2)}, u32[]{:S(2)}) async-start(bf16[4,144,2816]{2,1,0:T(8,128)(2,1)} %copy.112), calls=%async_computation | async-start | bytes 6488064 | tf_op jit(solution)/shard_map/all_to_all | solution.py:978
  42.9 197.1 %all-gather.9.cloned.1.call-start = ((), (), s32[]{:S(2)}) async-start(), calls=%async_computation.13 | async-start | bytes 5242880 | tf_op jit(solution)/shard_map/all_gather | solution.py:1029
  43.2 82.2 %collective-permute-start.1 = (bf16[576,1024]{1,0:T(8,128)(2,1)}, bf16[576,1024]{1,0:T(8,128)(2,1)}, u32[]{:S(2)}, u32[]{:S(2)}) collective-permute-start(bf16[576,1024]{1,0:T(8,128)(2,1)} %bitcast.196), channel_id=1, source_target_pairs={{0,4},{4,0},{1,5},{5,1},{2,6},{6,2},{3,7},{7,3},{8,12},{12,8},{9,1... | collective-permute-start | bytes 3538952 | tf_op jit(solution)/shard_map/ppermute | solution.py:900
  94.9 33.5 %collective-permute-start = (bf16[4,128,2816]{2,1,0:T(8,128)(2,1)}, bf16[4,128,2816]{2,1,0:T(8,128)(2,1)}, u32[]{:S(2)}, u32[]{:S(2)}) collective-permute-start(bf16[4,128,2816]{2,1,0:T(8,128)(2,1)} %slice.151), channel_id=1, source_target_pairs={{0,4},{4,0},{1,5},{5,1},{2,6},{6,2},{3,7},{7,3},{8,12},{12,8},{9,1... | collective-permute-start | bytes 8650760 | tf_op jit(solution)/shard_map/ppermute | solution.py:900
  154.0 114.4 %all-gather.11.cloned.1.call-start = ((), (), s32[]{:S(2)}) async-start(), calls=%async_computation.14 | async-start | bytes 5242880 | tf_op jit(solution)/shard_map/all_gather | solution.py:1032
  205.2 21.9 %all-to-all-start.1 = ((bf16[4,3,192,256]{3,2,1,0:T(8,128)(2,1)}), bf16[4,3,192,256]{3,2,1,0:T(8,128)(2,1)S(1)}, u32[]{:S(2)}, u32[]{:S(2)}) async-start(bf16[4,3,192,256]{3,2,1,0:T(8,128)(2,1)} %get-tuple-element.134.o_ref), calls=%async_computation.1 | async-start | bytes 2359296 | tf_op jit(solution)/shard_map/all_to_all | solution.py:1044
  208.8 124.4 %reduce-scatter.3.cloned.1.call-start = ((), (), s32[]{:S(2)}) async-start(), calls=%async_computation.9 | async-start | bytes 5242880 | tf_op jit(solution)/shard_map/reduce_scatter | solution.py:1060
  297.7 21.0 %collective-permute-start.4 = (bf16[576,1024]{1,0:T(8,128)(2,1)}, bf16[576,1024]{1,0:T(8,128)(2,1)}, u32[]{:S(2)}, u32[]{:S(2)}) collective-permute-start(bf16[576,1024]{1,0:T(8,128)(2,1)} %get-tuple-element.156), channel_id=1, source_target_pairs={{0,4},{4,0},{1,5},{5,1},{2,6},{6,2},{3,7},{7,3},{8,12},{12,8},{9,1... | collective-permute-start | bytes 3538952 | tf_op jit(solution)/shard_map/ppermute | solution.py:900
  317.1 69.0 %reduce-scatter.5.cloned.1.call-start = ((), (), s32[]{:S(2)}) async-start(), calls=%async_computation.10 | async-start | bytes 5242880 | tf_op jit(solution)/shard_map/reduce_scatter | solution.py:1106
  335.0 23.7 %collective-permute-start.5 = (bf16[128,1024]{1,0:T(8,128)(2,1)S(1)}, bf16[128,1024]{1,0:T(8,128)(2,1)S(1)}, u32[]{:S(2)}, u32[]{:S(2)}) collective-permute-start(bf16[128,1024]{1,0:T(8,128)(2,1)S(1)} %get-tuple-element.260), channel_id=1, source_target_pairs={{0,8},{8,0},{16,24},{24,16},{1,9},{9,1},{17,25},{25,17},{2,10},{10... | collective-permute-start | bytes 786440 | tf_op jit(solution)/shard_map/ppermute | solution.py:908
  336.5 22.2 %collective-permute-start.6 = (bf16[128,1024]{1,0:T(8,128)(2,1)S(1)}, bf16[128,1024]{1,0:T(8,128)(2,1)S(1)}, u32[]{:S(2)}, u32[]{:S(2)}) collective-permute-start(bf16[128,1024]{1,0:T(8,128)(2,1)S(1)} %get-tuple-element.259), channel_id=1, source_target_pairs={{0,16},{8,24},{16,0},{24,8},{1,17},{9,25},{17,1},{25,9},{2,18},{10... | collective-permute-start | bytes 786440 | tf_op jit(solution)/shard_map/ppermute | solution.py:908
  358.9 24.4 %collective-permute-start.10 = (bf16[128,1024]{1,0:T(8,128)(2,1)S(1)}, bf16[128,1024]{1,0:T(8,128)(2,1)S(1)}, u32[]{:S(2)}, u32[]{:S(2)}) collective-permute-start(bf16[128,1024]{1,0:T(8,128)(2,1)S(1)} %add_convert_fusion.1), channel_id=1, source_target_pairs={{0,24},{8,16},{16,8},{24,0},{1,25},{9,17},{17,9},{25,1},{2,26},{10... | collective-permute-start | bytes 786440 | tf_op jit(solution)/shard_map/ppermute | solution.py:918
  362.6 22.6 %collective-permute-start.9 = (bf16[128,1024]{1,0:T(8,128)(2,1)S(1)}, bf16[128,1024]{1,0:T(8,128)(2,1)S(1)}, u32[]{:S(2)}, u32[]{:S(2)}) collective-permute-start(bf16[128,1024]{1,0:T(8,128)(2,1)S(1)} %add_convert_fusion.1), channel_id=1, source_target_pairs={{0,16},{8,24},{16,0},{24,8},{1,17},{9,25},{17,1},{25,9},{2,18},{10... | collective-permute-start | bytes 786440 | tf_op jit(solution)/shard_map/ppermute | solution.py:918
  364.3 20.9 %collective-permute-start.8 = (bf16[128,1024]{1,0:T(8,128)(2,1)S(1)}, bf16[128,1024]{1,0:T(8,128)(2,1)S(1)}, u32[]{:S(2)}, u32[]{:S(2)}) collective-permute-start(bf16[128,1024]{1,0:T(8,128)(2,1)S(1)} %add_convert_fusion.1), channel_id=1, source_target_pairs={{0,8},{8,0},{16,24},{24,16},{1,9},{9,1},{17,25},{25,17},{2,10},{10... | collective-permute-start | bytes 786440 | tf_op jit(solution)/shard_map/ppermute | solution.py:918
  386.1 35.9 %all-to-all-start.3 = ((bf16[4,256,1024]{2,1,0:T(8,128)(2,1)}), bf16[4,256,1024]{2,1,0:T(8,128)(2,1)S(1)}, u32[]{:S(2)}, u32[]{:S(2)}) async-start(bf16[4,256,1024]{2,1,0:T(8,128)(2,1)} %bitcast.208), calls=%async_computation.5 | async-start | bytes 4194304 | tf_op jit(solution)/shard_map/all_to_all | solution.py:1127
  397.4 24.6 %collective-permute-start.11 = (bf16[128,1024]{1,0:T(8,128)(2,1)}, bf16[128,1024]{1,0:T(8,128)(2,1)}, u32[]{:S(2)}, u32[]{:S(2)}) collective-permute-start(bf16[128,1024]{1,0:T(8,128)(2,1)} %get-tuple-element.252), channel_id=1, source_target_pairs={{0,8},{8,0},{16,24},{24,16},{1,9},{9,1},{17,25},{25,17},{2,10},{10... | collective-permute-start | bytes 786440 | tf_op jit(solution)/shard_map/ppermute | solution.py:908
  399.4 22.7 %collective-permute-start.12 = (bf16[128,1024]{1,0:T(8,128)(2,1)}, bf16[128,1024]{1,0:T(8,128)(2,1)}, u32[]{:S(2)}, u32[]{:S(2)}) collective-permute-start(bf16[128,1024]{1,0:T(8,128)(2,1)} %get-tuple-element.251), channel_id=1, source_target_pairs={{0,16},{8,24},{16,0},{24,8},{1,17},{9,25},{17,1},{25,9},{2,18},{10... | collective-permute-start | bytes 786440 | tf_op jit(solution)/shard_map/ppermute | solution.py:908
  400.1 22.0 %collective-permute-start.13 = (bf16[128,1024]{1,0:T(8,128)(2,1)}, bf16[128,1024]{1,0:T(8,128)(2,1)}, u32[]{:S(2)}, u32[]{:S(2)}) collective-permute-start(bf16[128,1024]{1,0:T(8,128)(2,1)} %get-tuple-element.250), channel_id=1, source_target_pairs={{0,24},{8,16},{16,8},{24,0},{1,25},{9,17},{17,9},{25,1},{2,26},{10... | collective-permute-start | bytes 786440 | tf_op jit(solution)/shard_map/ppermute | solution.py:908
  431.4 23.9 %collective-permute-start.16 = (bf16[4,32,1024]{2,1,0:T(8,128)(2,1)}, bf16[4,32,1024]{2,1,0:T(8,128)(2,1)}, u32[]{:S(2)}, u32[]{:S(2)}) collective-permute-start(bf16[4,32,1024]{2,1,0:T(8,128)(2,1)} %get-tuple-element.249), channel_id=1, source_target_pairs={{0,16},{8,24},{16,0},{24,8},{1,17},{9,25},{17,1},{25,9},{2,18},{10... | collective-permute-start | bytes 786440 | tf_op jit(solution)/shard_map/ppermute | solution.py:908
  431.8 23.5 %collective-permute-start.15 = (bf16[4,32,1024]{2,1,0:T(8,128)(2,1)}, bf16[4,32,1024]{2,1,0:T(8,128)(2,1)}, u32[]{:S(2)}, u32[]{:S(2)}) collective-permute-start(bf16[4,32,1024]{2,1,0:T(8,128)(2,1)} %get-tuple-element.247), channel_id=1, source_target_pairs={{0,8},{8,0},{16,24},{24,16},{1,9},{9,1},{17,25},{25,17},{2,10},{10... | collective-permute-start | bytes 786440 | tf_op jit(solution)/shard_map/ppermute | solution.py:908
  433.6 23.7 %all-to-all-start.5 = ((bf16[4,16,1024]{2,1,0:T(8,128)(2,1)}), bf16[4,16,1024]{2,1,0:T(8,128)(2,1)S(1)}, u32[]{:S(2)}, u32[]{:S(2)}) async-start(bf16[4,16,1024]{2,1,0:T(8,128)(2,1)} %get-tuple-element.206), calls=%async_computation.7 | async-start | bytes 262144 | tf_op jit(solution)/shard_map/all_to_all | solution.py:1142
  467.4 112.6 %all-to-all-start.6 = ((bf16[4,3,192,1024]{3,2,1,0:T(8,128)(2,1)}), bf16[4,3,192,1024]{3,2,1,0:T(8,128)(2,1)}, u32[]{:S(2)}, u32[]{:S(2)}) async-start(bf16[4,3,192,1024]{3,2,1,0:T(8,128)(2,1)} %get-tuple-element.209), calls=%async_computation.8 | async-start | bytes 9437184 | tf_op jit(solution)/shard_map/all_to_all | solution.py:1154
  472.5 96.5 %all-reduce.7.cloned.1.call-start = ((), (), s32[]{:S(2)}) async-start(), calls=%async_computation.11 | async-start | bytes 1114112 | tf_op jit(solution)/shard_map/psum | solution.py:1146
  479.0 95.0 %collective-permute-start.28 = (bf16[2,256,1024]{2,1,0:T(8,128)(2,1)S(1)}, bf16[2,256,1024]{2,1,0:T(8,128)(2,1)}, u32[]{:S(2)}, u32[]{:S(2)}) collective-permute-start(bf16[2,256,1024]{2,1,0:T(8,128)(2,1)S(1)} %bitcast.198), channel_id=1, source_target_pairs={{0,4},{4,0},{1,5},{5,1},{2,6},{6,2},{3,7},{7,3},{8,12},{12,8},{9,1... | collective-permute-start | bytes 3145736 | tf_op jit(solution)/shard_map/ppermute | solution.py:900
  497.0 77.0 %collective-permute-start.29 = (bf16[2,256,1024]{2,1,0:T(8,128)(2,1)}, bf16[2,256,1024]{2,1,0:T(8,128)(2,1)}, u32[]{:S(2)}, u32[]{:S(2)}) collective-permute-start(bf16[2,256,1024]{2,1,0:T(8,128)(2,1)} %bitcast.76.b_ref), channel_id=1, source_target_pairs={{0,4},{4,0},{1,5},{5,1},{2,6},{6,2},{3,7},{7,3},{8,12},{12,8},{9,1... | collective-permute-start | bytes 3145736 | tf_op jit(solution)/shard_map/ppermute | solution.py:900
  500.5 27.9 %collective-permute-start.24 = (bf16[3,64,256]{2,1,0:T(8,128)(2,1)}, bf16[3,64,256]{2,1,0:T(8,128)(2,1)S(1)}, u32[]{:S(2)}, u32[]{:S(2)}) collective-permute-start(bf16[3,64,256]{2,1,0:T(8,128)(2,1)} %get-tuple-element.269), channel_id=1, source_target_pairs={{0,3},{1,2},{2,1},{3,0},{4,7},{5,6},{6,5},{7,4},{8,11},{9,10},{10,... | collective-permute-start | bytes 294920 | tf_op jit(solution)/shard_map/ppermute | solution.py:908
  503.1 26.7 %collective-permute-start.23 = (bf16[3,64,256]{2,1,0:T(8,128)(2,1)}, bf16[3,64,256]{2,1,0:T(8,128)(2,1)S(1)}, u32[]{:S(2)}, u32[]{:S(2)}) collective-permute-start(bf16[3,64,256]{2,1,0:T(8,128)(2,1)} %get-tuple-element.270), channel_id=1, source_target_pairs={{0,2},{1,3},{2,0},{3,1},{4,6},{5,7},{6,4},{7,5},{8,10},{9,11},{10,... | collective-permute-start | bytes 294920 | tf_op jit(solution)/shard_map/ppermute | solution.py:908
  503.7 26.1 %collective-permute-start.22 = (bf16[3,64,256]{2,1,0:T(8,128)(2,1)}, bf16[3,64,256]{2,1,0:T(8,128)(2,1)S(1)}, u32[]{:S(2)}, u32[]{:S(2)}) collective-permute-start(bf16[3,64,256]{2,1,0:T(8,128)(2,1)} %get-tuple-element.271), channel_id=1, source_target_pairs={{0,1},{1,0},{2,3},{3,2},{4,5},{5,4},{6,7},{7,6},{8,9},{9,8},{10,11... | collective-permute-start | bytes 294920 | tf_op jit(solution)/shard_map/ppermute | solution.py:908
  528.4 43.5 %collective-permute-start.20 = (bf16[4,32,1024]{2,1,0:T(8,128)(2,1)S(1)}, bf16[4,32,1024]{2,1,0:T(8,128)(2,1)S(1)}, u32[]{:S(2)}, u32[]{:S(2)}) collective-permute-start(bf16[4,32,1024]{2,1,0:T(8,128)(2,1)S(1)} %copy-done.17), channel_id=1, source_target_pairs={{0,24},{8,16},{16,8},{24,0},{1,25},{9,17},{17,9},{25,1},{2,26},{10... | collective-permute-start | bytes 786440 | tf_op jit(solution)/shard_map/ppermute | solution.py:918
  529.8 42.0 %collective-permute-start.19 = (bf16[4,32,1024]{2,1,0:T(8,128)(2,1)S(1)}, bf16[4,32,1024]{2,1,0:T(8,128)(2,1)S(1)}, u32[]{:S(2)}, u32[]{:S(2)}) collective-permute-start(bf16[4,32,1024]{2,1,0:T(8,128)(2,1)S(1)} %copy-done.17), channel_id=1, source_target_pairs={{0,16},{8,24},{16,0},{24,8},{1,17},{9,25},{17,1},{25,9},{2,18},{10... | collective-permute-start | bytes 786440 | tf_op jit(solution)/shard_map/ppermute | solution.py:918
  529.8 42.0 %collective-permute-start.18 = (bf16[4,32,1024]{2,1,0:T(8,128)(2,1)S(1)}, bf16[4,32,1024]{2,1,0:T(8,128)(2,1)}, u32[]{:S(2)}, u32[]{:S(2)}) collective-permute-start(bf16[4,32,1024]{2,1,0:T(8,128)(2,1)S(1)} %copy-done.17), channel_id=1, source_target_pairs={{0,8},{8,0},{16,24},{24,16},{1,9},{9,1},{17,25},{25,17},{2,10},{10... | collective-permute-start | bytes 786440 | tf_op jit(solution)/shard_map/ppermute | solution.py:918
  (52 other events, 474.1 us)
Sparse Core Ops, SparseCore 0:
  12.8 141.0 all-gather.6
  156.4 52.6 all-gather.8
  211.5 54.4 all-gather.10
  269.4 53.3 reduce-scatter.2
  333.4 52.6 reduce-scatter.4
  505.0 63.9 all-reduce.6
